TPU v7x, 256 devices: a whole 4x4x8 slice. The times are simulated.
256 devices in a mesh: section: 4 (over y), band: 16 (over z, core), rep: 4 (over x).
Axes of the slice: x: 4, y: 4, z: 8, core: 2. Of those that a mesh axis runs over, the one named last changes fastest.
Arguments:
- images: bfloat16 [8, 64, 64, 128], P('rep', None, 'band'), may hold values from -6 to 6
- weights: bfloat16 [4, 3, 3, 3, 64, 64], P('section'), may hold values from -0.25 to 0.25
- cotangent: bfloat16 [8, 64, 64, 128], P('rep', None, 'band'), may hold values from -6 to 6
Outputs:
- section_acts: bfloat16 [4, 8, 64, 64, 128], P('section', 'rep', None, 'band')
- input_grads: bfloat16 [4, 8, 64, 64, 128], P('section', 'rep', None, 'band')
- weight_grads: float32 [4, 3, 3, 3, 64, 64], P('section')
All inputs are finite; a program needn't handle non-finite values.
Results may differ from a plain program's by a relative error of at most 0.029.
Values may be sent and summed in bfloat16 or wider, within the bound.
No kernel may reach another device: no remote copies, remote signals or barrier semaphores. Data moves between devices by JAX's collectives and lax.ppermute only.
A program may use at most 128 MiB of HBM per device.

v0:
```python
import jax
import jax.numpy as jnp
from jax import lax
from jax.experimental import pallas as pl
from jax.experimental.pallas import tpu as pltpu
from jax.sharding import PartitionSpec as P

BF = jnp.bfloat16
F32 = jnp.float32
gelu_scale = 0.7978845608028654
cubic_coef = 0.044715

C = 64
WID = 128
ROWS = 64
OWN = 8
OFF = 24
WINDOW = 56
DEPTH = 4


def weight_blocks_kernel(where_ref, w0, w1, w2, w3, fwd_ref, bwd_ref):
    zero = jnp.zeros((C, C), F32)
    for hop, piece in enumerate((w0, w1, w2, w3)):
        section = lax.rem(where_ref[0] - hop + DEPTH, DEPTH)

        def one_layer(layer, carry, piece=piece, section=section):
            slot = section * 3 + layer
            for kw in range(3):
                taps = []
                for kh in range(3):
                    at = pl.multiple_of(layer * 288 + (kh * 3 + kw) * 32, 32)
                    block = piece[pl.ds(at, 32), :].astype(F32)
                    taps.append(jnp.concatenate([block[:, :C], block[:, C:]], axis=0))
                low = jnp.concatenate([taps[0], taps[1]], axis=0).T
                high = jnp.concatenate([taps[2], zero], axis=0).T
                low_up = jnp.concatenate([zero, taps[0]], axis=0).T
                high_up = jnp.concatenate([taps[1], taps[2]], axis=0).T
                first = jnp.concatenate([low, high], axis=1)
                second = jnp.concatenate([low_up, high_up], axis=1)
                fwd_ref[slot, pl.ds(kw * 128, 128), :] = jnp.concatenate(
                    [first, second], axis=0
                ).astype(BF)
                first = jnp.concatenate([taps[2], taps[1], taps[0], zero], axis=1)
                second = jnp.concatenate([zero, taps[2], taps[1], taps[0]], axis=1)
                bwd_ref[slot, pl.ds((2 - kw) * 128, 128), :] = jnp.concatenate(
                    [first, second], axis=0
                ).astype(BF)
            return carry

        lax.fori_loop(0, 3, one_layer, 0)


def sections_kernel(
    where_ref,
    im_c, im_l1, im_r1, im_l2, im_r2, im_l3, im_r3,
    wf_ref, wb_ref,
    keep_ref, send_ref, wg_ref,
    h_ref, a1_ref, a2_ref, p1_ref, p2_ref, g_ref, gp1_ref, gp2_ref,
):
    mine = where_ref[0]
    first_row = where_ref[1]
    core = where_ref[2]
    h_ref[0, 24:32] = im_c[0:8]
    h_ref[0, 16:24] = im_l1[0:8]
    h_ref[0, 32:40] = im_r1[0:8]
    h_ref[0, 8:16] = im_l2[0:8]
    h_ref[0, 40:48] = im_r2[0:8]
    h_ref[0, 2:8] = im_l3[...]
    h_ref[0, 48:54] = im_r3[...]
    g_ref[24:32] = im_c[8:16]
    g_ref[16:24] = im_l1[8:16]
    g_ref[32:40] = im_r1[8:16]
    g_ref[12:16] = im_l2[8:12]
    g_ref[40:44] = im_r2[8:12]

    lane = lax.broadcasted_iota(jnp.int32, (128, WID), 1)
    not_first = lane > 0
    not_last = lane < WID - 1

    def inside(row):
        at = row - OFF + first_row
        return jnp.logical_and(at >= 0, at < ROWS)

    def conv_loop(reach, source, slab, finish):
        start = OFF - reach
        steps = 2 + (reach + 1) // 2

        def step(t, carry):
            row = start + 4 * t
            low = source[pl.ds(row - 1, 4)].reshape(4 * C, WID)
            high = source[pl.ds(row + 1, 4)].reshape(4 * C, WID)
            product = lax.dot_general(
                slab[...],
                jnp.concatenate([low, high], axis=1),
                (((1,), (0,)), ((), ())),
                preferred_element_type=F32,
            )
            for half in range(2):
                part = product[:, half * WID:(half + 1) * WID]
                total = (
                    part[128:256]
                    + jnp.where(not_first, pltpu.roll(part[0:128], 1, 1), 0.0)
                    + jnp.where(not_last, pltpu.roll(part[256:384], WID - 1, 1), 0.0)
                )
                for one in range(2):
                    finish(row + 2 * half + one, total[one * C:(one + 1) * C])
            return carry

        lax.fori_loop(0, steps, step, 0)

    def tangent_of(values):
        return jnp.tanh(values * (gelu_scale + (gelu_scale * cubic_coef) * (values * values)))

    def slope_of(values):
        square = values * values
        tangent = jnp.tanh(values * (gelu_scale + (gelu_scale * cubic_coef) * square))
        return 0.5 * (1.0 + tangent) + (0.5 * values) * (1.0 - tangent * tangent) * (
            gelu_scale + (3.0 * gelu_scale * cubic_coef) * square
        )

    def forward(section, carry):
        def activate(pre_ref, act_ref):
            def finish(row, values):
                pre_ref[section, row] = values
                half = 0.5 * values
                act = half + half * tangent_of(values)
                act_ref[section, row] = jnp.where(inside(row), act, 0.0).astype(BF)

            return finish

        def residual(row, values):
            result = h_ref[section, row].astype(F32) + values
            h_ref[section + 1, row] = jnp.where(inside(row), result, 0.0).astype(BF)

        slot = section * 3
        conv_loop(21 - 3 * section, h_ref.at[section], wf_ref.at[slot],
                  activate(p1_ref, a1_ref))
        conv_loop(20 - 3 * section, a1_ref.at[section], wf_ref.at[slot + 1],
                  activate(p2_ref, a2_ref))
        conv_loop(jnp.where(section == DEPTH - 1, 0, 19 - 3 * section), a2_ref.at[section],
                  wf_ref.at[slot + 2], residual)
        return carry

    lax.fori_loop(0, DEPTH, forward, 0)

    def kernel_grad(layer, source, grads):
        wide_in, wide_out = [], []
        for row in range(OFF, OFF + OWN):
            wide_in.append(source[pl.ds(row - 1, 3)].reshape(3 * C, WID))
            out = grads[row].astype(F32)
            after = jnp.where(not_last[:C], pltpu.roll(out, WID - 1, 1), 0.0)
            before = jnp.where(not_first[:C], pltpu.roll(out, 1, 1), 0.0)
            wide_out.append(jnp.concatenate([after, out, before], axis=0).astype(BF))
        result = lax.dot_general(
            jnp.concatenate(wide_in, axis=1),
            jnp.concatenate(wide_out, axis=1),
            (((1,), (1,)), ((), ())),
            preferred_element_type=F32,
        )
        for kw in range(3):
            part = result[:, kw * C:(kw + 1) * C]
            packed = jnp.concatenate([part[:96], part[96:]], axis=1)
            wg_ref[pl.ds((layer * 3 + kw) * 96, 96), :] = packed.astype(BF)

    wg_ref[864:1024, :] = jnp.zeros((160, 128), BF)

    def backward(turn, carry):
        section = DEPTH - 1 - turn
        slot = section * 3

        @pl.when(section == mine)
        def _():
            kernel_grad(2, a2_ref.at[section], g_ref)

        def through(pre_ref, target):
            def finish(row, values):
                result = values * slope_of(pre_ref[section, row])
                target[row] = jnp.where(inside(row), result, 0.0).astype(BF)

            return finish

        def residual(row, values):
            result = g_ref[row].astype(F32) + values
            g_ref[row] = jnp.where(inside(row), result, 0.0).astype(BF)

        conv_loop(2 + 3 * section, g_ref, wb_ref.at[slot + 2], through(p2_ref, gp2_ref))
        conv_loop(1 + 3 * section, gp2_ref, wb_ref.at[slot + 1], through(p1_ref, gp1_ref))

        @pl.when(section == mine)
        def _():
            kernel_grad(1, a1_ref.at[section], gp2_ref)
            kernel_grad(0, h_ref.at[section], gp1_ref)

        conv_loop(3 * section, gp1_ref, wb_ref.at[slot], residual)
        return carry

    lax.fori_loop(0, DEPTH - mine, backward, 0)

    kept = OFF + 4 * core
    sent = OFF + 4 * (1 - core)
    keep_ref[0] = h_ref[mine + 1, pl.ds(kept, 4)]
    keep_ref[1] = g_ref[pl.ds(kept, 4)]
    send_ref[0] = h_ref[mine + 1, pl.ds(sent, 4)]
    send_ref[1] = g_ref[pl.ds(sent, 4)]


def unpack_kernel(sum_ref, out_ref):
    for layer in range(3):
        for kw in range(3):
            base = (layer * 3 + kw) * 96
            block = sum_ref[base:base + 96, :].astype(F32)
            tall = jnp.concatenate([block[:, :C], block[:, C:]], axis=0)
            for kh in range(3):
                out_ref[0, layer, kh, kw] = tall[kh * C:(kh + 1) * C]


def vmem(count):
    return [pl.BlockSpec(memory_space=pltpu.VMEM)] * count


def on_device(images, weights, cotangent):
    section = lax.axis_index("section")
    band = lax.axis_index("band")
    core = band % 2
    where = jnp.stack([section, (band // 2) * OWN, core]).astype(jnp.int32)

    field = jnp.stack([images, cotangent]).transpose(1, 0, 3, 2, 4)
    mine = jnp.where(core == 0, field[0], field[1])
    other = jnp.where(core == 0, field[1], field[0])
    bands = lax.axis_size("band")
    swapped = [(i, i ^ 1) for i in range(bands)]
    got = lax.ppermute(other, "band", swapped)
    center = jnp.where(
        core == 0,
        jnp.concatenate([mine, got], axis=1),
        jnp.concatenate([got, mine], axis=1),
    ).reshape(16, C, WID)

    def chips_away(value, chips):
        pairs = [(i, i + 2 * chips) for i in range(bands) if 0 <= i + 2 * chips < bands]
        return lax.ppermute(value, "band", pairs)

    left1 = chips_away(center, 1)
    right1 = chips_away(center, -1)
    left2 = chips_away(jnp.concatenate([center[0:8], center[12:16]]), 2)
    right2 = chips_away(center[0:12], -2)
    left3 = chips_away(center[2:8], 3)
    right3 = chips_away(center[0:6], -3)

    raw = weights.reshape(27, 2, 32, C)
    raw = jnp.concatenate([raw[:, 0], raw[:, 1]], axis=-1).reshape(864, 128)
    around = [
        lax.ppermute(raw, "section", [(i, (i + hop) % DEPTH) for i in range(DEPTH)])
        for hop in range(1, DEPTH)
    ]
    fwd, bwd = pl.pallas_call(
        weight_blocks_kernel,
        out_shape=[jax.ShapeDtypeStruct((12, 384, 256), BF)] * 2,
        in_specs=[pl.BlockSpec(memory_space=pltpu.SMEM)] + vmem(4),
        out_specs=vmem(2),
        name="weight_blocks",
    )(where, raw, *around)

    window = (WINDOW, C, WID)
    keep, send, grads = pl.pallas_call(
        sections_kernel,
        out_shape=[
            jax.ShapeDtypeStruct((2, 4, C, WID), BF),
            jax.ShapeDtypeStruct((2, 4, C, WID), BF),
            jax.ShapeDtypeStruct((1024, 128), BF),
        ],
        in_specs=[pl.BlockSpec(memory_space=pltpu.SMEM)] + vmem(9),
        out_specs=vmem(3),
        scratch_shapes=[
            pltpu.VMEM((DEPTH + 1,) + window, BF),
            pltpu.VMEM((DEPTH,) + window, BF),
            pltpu.VMEM((DEPTH,) + window, BF),
            pltpu.VMEM((DEPTH,) + window, F32),
            pltpu.VMEM((DEPTH,) + window, F32),
            pltpu.VMEM(window, BF),
            pltpu.VMEM(window, BF),
            pltpu.VMEM(window, BF),
        ],
        compiler_params=pltpu.CompilerParams(vmem_limit_bytes=48 * 1024 * 1024),
        name="sections",
    )(where, center, left1, right1, left2, right2, left3, right3, fwd, bwd)

    received = lax.ppermute(send, "band", swapped)
    zero = jnp.where(core == 0, keep, received)
    one = jnp.where(core == 0, received, keep)
    both = jnp.stack([zero, one]).transpose(1, 0, 3, 2, 4)

    parts = lax.all_to_all(grads.reshape(64, 16, 128), ("rep", "band"), 0, 0, tiled=True)
    total = jnp.sum(parts.astype(F32), axis=0).astype(BF)
    summed = lax.all_to_all(
        jnp.broadcast_to(total[None], (64, 16, 128)), ("rep", "band"), 0, 0, tiled=True
    ).reshape(1024, 128)
    weight_grads = pl.pallas_call(
        unpack_kernel,
        out_shape=jax.ShapeDtypeStruct((1, 3, 3, 3, C, C), F32),
        in_specs=vmem(1),
        out_specs=pl.BlockSpec(memory_space=pltpu.VMEM),
        name="unpack",
    )(summed)
    return both[0][None], both[1][None], weight_grads


def solution(mesh):
    in_specs = (
        P("rep", None, "band", None),
        P("section", None, None, None, None, None),
        P("rep", None, "band", None),
    )
    out_specs = (
        P("section", "rep", None, "band", None),
        P("section", "rep", None, "band", None),
        P("section", None, None, None, None, None),
    )
    return jax.shard_map(
        on_device, mesh=mesh, in_specs=in_specs, out_specs=out_specs, check_vma=False
    )
```

profile of v0, /device:TPU:1, one launch (start us, length us, event | category | flops | bytes accessed | tf_op | source)
XLA Modules:
  0.0 148.4 jit_solution(11235858157296347196)
XLA Ops:
  0.6 1.0 copy_bitcast_fusion
  1.7 3.3 %collective-permute-start = (bf16[2,4,64,128]{3,2,1,0:T(8,128)(2,1)S(1)}, bf16[2,4,64,128]{3,2,1,0:T(8,128)(2,1)S(1)}, u32[]{:S(2)}, u32[]{:S(2)}) collective-permute-start(bf16[2,4,64,128]{3,2,1,0:T(8,128)(2,1)S(1)} %get-tuple-element.25), channel_id=1, source_target_pairs={{0,4},{4,0},{8,12},{12,8},{16,20},{20,16},{24,28},{28,24},{32,36},... | collective-permute-start | bytes 393224 | tf_op jit(solution)/shard_map/ppermute | solution.py:233
  5.1 1.1 fusion
  6.1 0.1 pad_maximum_fusion.w0
  6.3 0.0 copy-start.3
  6.3 0.1 collective-permute-start.7
  6.4 2.2 %collective-permute-start.8 = (bf16[864,128]{1,0:T(8,128)(2,1)S(1)}, bf16[864,128]{1,0:T(8,128)(2,1)S(1)}, u32[]{:S(2)}, u32[]{:S(2)}) collective-permute-start(bf16[864,128]{1,0:T(8,128)(2,1)S(1)} %pad_maximum_fusion.w0), channel_id=1, source_target_pairs={{0,128},{64,192},{128,0},{192,64},{1,129},{65,193},{129,1},{193,65... | collective-permute-start | bytes 663560 | tf_op jit(solution)/shard_map/ppermute | solution.py:254
  8.6 1.1 collective-permute-start.9
  9.7 3.6 %collective-permute-start.1 = (bf16[16,64,128]{2,1,0:T(8,128)(2,1)S(1)}, bf16[16,64,128]{2,1,0:T(8,128)(2,1)S(1)}, u32[]{:S(2)}, u32[]{:S(2)}) collective-permute-start(bf16[16,64,128]{2,1,0:T(8,128)(2,1)S(1)} %bitcast.33), channel_id=1, source_target_pairs={{0,8},{4,12},{8,16},{12,20},{16,24},{20,28},{24,32},{28,36},{32,40... | collective-permute-start | bytes 786440 | tf_op jit(solution)/shard_map/ppermute | solution.py:242
  13.3 1.3 collective-permute-start.2
  14.6 0.5 collective-permute-done.7.w1
  15.0 7.6 %collective-permute-start.5 = (bf16[6,64,128]{2,1,0:T(8,128)(2,1)S(1)}, bf16[6,64,128]{2,1,0:T(8,128)(2,1)S(1)}, u32[]{:S(2)}, u32[]{:S(2)}) collective-permute-start(bf16[6,64,128]{2,1,0:T(8,128)(2,1)S(1)} %get-tuple-element.23), channel_id=1, source_target_pairs={{0,24},{4,28},{8,32},{12,36},{16,40},{20,44},{24,48},{28,52},{32,5... | collective-permute-start | bytes 294920 | tf_op jit(solution)/shard_map/ppermute | solution.py:242
  22.8 3.8 %collective-permute-start.3 = (bf16[12,64,128]{2,1,0:T(8,128)(2,1)S(1)}, bf16[12,64,128]{2,1,0:T(8,128)(2,1)S(1)}, u32[]{:S(2)}, u32[]{:S(2)}) collective-permute-start(bf16[12,64,128]{2,1,0:T(8,128)(2,1)S(1)} %pad_maximum_fusion.1), channel_id=1, source_target_pairs={{0,16},{4,20},{8,24},{12,28},{16,32},{20,36},{24,40},{28,44},{32,4... | collective-permute-start | bytes 589832 | tf_op jit(solution)/shard_map/ppermute | solution.py:242
  26.6 1.3 collective-permute-start.4
  27.9 1.3 collective-permute-start.6
  29.2 0.7 pad_add_fusion.where_ref
  29.9 7.5 %weight_blocks.1 = (bf16[12,384,256]{2,1,0:T(8,128)(2,1)}, bf16[12,384,256]{2,1,0:T(8,128)(2,1)}) custom-call(s32[3]{0:T(128)} %pad_add_fusion.where_ref, bf16[864,128]{1,0:T(8,128)(2,1)} %copy-done.3, bf16[864,128]{1,0:T(8,128)(2,1)} %copy-done.4, bf16[864,128]{1,0:T(8,128)(2,1)} %copy-done.5, bf16[864,128]{1,0:T(8,128)(2,1)} %copy-done.6), custom_call_target="tpu_custom_call" | custom-call | tf_op jit(solution)/shard_map/weight_blocks/pallas_call | solution.py:257
  37.5 3.8 %collective-permute-done.4.im_r2 = bf16[12,64,128]{2,1,0:T(8,128)(2,1)S(1)} collective-permute-done((bf16[12,64,128]{2,1,0:T(8,128)(2,1)S(1)}, bf16[12,64,128]{2,1,0:T(8,128)(2,1)S(1)}, u32[]{:S(2)}, u32[]{:S(2)}) %collective-permute-start.4) | collective-permute-done | bytes 196640 | tf_op jit(solution)/shard_map/ppermute | solution.py:242
  41.3 1.7 %copy-done = bf16[12,384,256]{2,1,0:T(8,128)(2,1)S(1)} copy-done((bf16[12,384,256]{2,1,0:T(8,128)(2,1)S(1)}, bf16[12,384,256]{2,1,0:T(8,128)(2,1)}, u32[]{:S(2)}) %copy-start) | copy-done | bytes 2359320
  43.0 0.7 copy-done.1
  43.7 57.7 %sections.1 = (bf16[2,4,64,128]{3,2,1,0:T(8,128)(2,1)S(1)}, bf16[2,4,64,128]{3,2,1,0:T(8,128)(2,1)S(1)}, bf16[1024,128]{1,0:T(8,128)(2,1)}) custom-call(s32[3]{0:T(128)S(1)} %copy-done.1, bf16[16,64,128]{2,1,0:T(8,128)(2,1)S(1)} %bitcast.36, bf16[16,64,128]{2,1,0:T(8,128)(2,1)S(1)} %collective-permute-done.1.im_l1, ...), custom_call_target="tpu_custom_call" | custom-call | tf_op jit(solution)/shard_map/sections/pallas_call | solution.py:266
  101.4 13.5 %all-to-all-start = ((bf16[64,16,128]{2,1,0:T(8,128)(2,1)}), bf16[64,16,128]{2,1,0:T(8,128)(2,1)S(1)}, u32[]{:S(2)}, u32[]{:S(2)}) async-start(bf16[64,16,128]{2,1,0:T(8,128)(2,1)} %bitcast.16), calls=%async_computation | async-start | bytes 524288 | tf_op jit(solution)/shard_map/all_to_all | solution.py:294
  114.9 0.5 collective-permute-start.10
  115.5 11.5 %all-to-all-done = bf16[64,16,128]{2,1,0:T(8,128)(2,1)S(1)} async-done(((bf16[64,16,128]{2,1,0:T(8,128)(2,1)}), bf16[64,16,128]{2,1,0:T(8,128)(2,1)S(1)}, u32[]{:S(2)}, u32[]{:S(2)}) %all-to-all-start) | async-done | bytes 262176 | tf_op jit(solution)/shard_map/all_to_all | solution.py:294
  126.9 0.1 reduce_sum.12
  127.0 0.7 broadcast_in_dim.2
  127.7 6.0 %all-to-all-start.1 = ((bf16[64,16,128]{2,1,0:T(8,128)(2,1)}), bf16[64,16,128]{2,1,0:T(8,128)(2,1)S(1)}, u32[]{:S(2)}, u32[]{:S(2)}) async-start(bf16[64,16,128]{2,1,0:T(8,128)(2,1)} %broadcast_in_dim.2), calls=%async_computation.1 | async-start | bytes 524288 | tf_op jit(solution)/shard_map/all_to_all | solution.py:296
  133.9 0.8 copy.10
  134.6 0.8 copy.11
  135.4 10.4 %all-to-all-done.1 = bf16[64,16,128]{2,1,0:T(8,128)(2,1)S(1)} async-done(((bf16[64,16,128]{2,1,0:T(8,128)(2,1)}), bf16[64,16,128]{2,1,0:T(8,128)(2,1)S(1)}, u32[]{:S(2)}, u32[]{:S(2)}) %all-to-all-start.1) | async-done | bytes 262176 | tf_op jit(solution)/shard_map/all_to_all | solution.py:296
  145.8 0.7 copy-done.2
  146.5 2.0 %unpack.1 = f32[1,3,3,3,64,64]{5,4,3,2,1,0:T(8,128)} custom-call(bf16[1024,128]{1,0:T(8,128)(2,1)} %bitcast.37), custom_call_target="tpu_custom_call" | custom-call | tf_op jit(solution)/shard_map/unpack/pallas_call | solution.py:299
  (30 shorter events, 0.3 us)
Async XLA Ops:
  1.7 7.9 %collective-permute-start = (bf16[2,4,64,128]{3,2,1,0:T(8,128)(2,1)S(1)}, bf16[2,4,64,128]{3,2,1,0:T(8,128)(2,1)S(1)}, u32[]{:S(2)}, u32[]{:S(2)}) collective-permute-start(bf16[2,4,64,128]{3,2,1,0:T(8,128)(2,1)S(1)} %get-tuple-element.25), channel_id=1, source_target_pairs={{0,4},{4,0},{8,12},{12,8},{16,20},{20,16},{24,28},{28,24},{32,36},... | collective-permute-start | bytes 393224 | tf_op jit(solution)/shard_map/ppermute | solution.py:233
  6.3 23.6 %copy-start.3 = (bf16[864,128]{1,0:T(8,128)(2,1)}, bf16[864,128]{1,0:T(8,128)(2,1)S(1)}, u32[]{:S(2)}) copy-start(bf16[864,128]{1,0:T(8,128)(2,1)S(1)} %pad_maximum_fusion.w0) | copy-start | bytes 663556
  6.3 8.7 %collective-permute-start.7 = (bf16[864,128]{1,0:T(8,128)(2,1)S(1)}, bf16[864,128]{1,0:T(8,128)(2,1)S(1)}, u32[]{:S(2)}, u32[]{:S(2)}) collective-permute-start(bf16[864,128]{1,0:T(8,128)(2,1)S(1)} %pad_maximum_fusion.w0), channel_id=1, source_target_pairs={{0,64},{64,128},{128,192},{192,0},{1,65},{65,129},{129,193},{193,1... | collective-permute-start | bytes 663560 | tf_op jit(solution)/shard_map/ppermute | solution.py:254
  6.4 16.4 %collective-permute-start.8 = (bf16[864,128]{1,0:T(8,128)(2,1)S(1)}, bf16[864,128]{1,0:T(8,128)(2,1)S(1)}, u32[]{:S(2)}, u32[]{:S(2)}) collective-permute-start(bf16[864,128]{1,0:T(8,128)(2,1)S(1)} %pad_maximum_fusion.w0), channel_id=1, source_target_pairs={{0,128},{64,192},{128,0},{192,64},{1,129},{65,193},{129,1},{193,65... | collective-permute-start | bytes 663560 | tf_op jit(solution)/shard_map/ppermute | solution.py:254
  8.6 18.0 %collective-permute-start.9 = (bf16[864,128]{1,0:T(8,128)(2,1)S(1)}, bf16[864,128]{1,0:T(8,128)(2,1)S(1)}, u32[]{:S(2)}, u32[]{:S(2)}) collective-permute-start(bf16[864,128]{1,0:T(8,128)(2,1)S(1)} %pad_maximum_fusion.w0), channel_id=1, source_target_pairs={{0,192},{64,0},{128,64},{192,128},{1,193},{65,1},{129,65},{193,129... | collective-permute-start | bytes 663560 | tf_op jit(solution)/shard_map/ppermute | solution.py:254
  9.7 31.6 %collective-permute-start.1 = (bf16[16,64,128]{2,1,0:T(8,128)(2,1)S(1)}, bf16[16,64,128]{2,1,0:T(8,128)(2,1)S(1)}, u32[]{:S(2)}, u32[]{:S(2)}) collective-permute-start(bf16[16,64,128]{2,1,0:T(8,128)(2,1)S(1)} %bitcast.33), channel_id=1, source_target_pairs={{0,8},{4,12},{8,16},{12,20},{16,24},{20,28},{24,32},{28,36},{32,40... | collective-permute-start | bytes 786440 | tf_op jit(solution)/shard_map/ppermute | solution.py:242
  13.3 28.0 %collective-permute-start.2 = (bf16[16,64,128]{2,1,0:T(8,128)(2,1)S(1)}, bf16[16,64,128]{2,1,0:T(8,128)(2,1)S(1)}, u32[]{:S(2)}, u32[]{:S(2)}) collective-permute-start(bf16[16,64,128]{2,1,0:T(8,128)(2,1)S(1)} %bitcast.34), channel_id=1, source_target_pairs={{8,0},{12,4},{16,8},{20,12},{24,16},{28,20},{32,24},{36,28},{40,32... | collective-permute-start | bytes 786440 | tf_op jit(solution)/shard_map/ppermute | solution.py:242
  15.0 14.9 %copy-start.4 = (bf16[864,128]{1,0:T(8,128)(2,1)}, bf16[864,128]{1,0:T(8,128)(2,1)S(1)}, u32[]{:S(2)}) copy-start(bf16[864,128]{1,0:T(8,128)(2,1)S(1)} %collective-permute-done.7.w1) | copy-start | bytes 663556
  15.0 12.9 %collective-permute-start.5 = (bf16[6,64,128]{2,1,0:T(8,128)(2,1)S(1)}, bf16[6,64,128]{2,1,0:T(8,128)(2,1)S(1)}, u32[]{:S(2)}, u32[]{:S(2)}) collective-permute-start(bf16[6,64,128]{2,1,0:T(8,128)(2,1)S(1)} %get-tuple-element.23), channel_id=1, source_target_pairs={{0,24},{4,28},{8,32},{12,36},{16,40},{20,44},{24,48},{28,52},{32,5... | collective-permute-start | bytes 294920 | tf_op jit(solution)/shard_map/ppermute | solution.py:242
  22.8 7.2 %copy-start.5 = (bf16[864,128]{1,0:T(8,128)(2,1)}, bf16[864,128]{1,0:T(8,128)(2,1)S(1)}, u32[]{:S(2)}) copy-start(bf16[864,128]{1,0:T(8,128)(2,1)S(1)} %collective-permute-done.8.w2) | copy-start | bytes 663556
  22.8 14.7 %collective-permute-start.3 = (bf16[12,64,128]{2,1,0:T(8,128)(2,1)S(1)}, bf16[12,64,128]{2,1,0:T(8,128)(2,1)S(1)}, u32[]{:S(2)}, u32[]{:S(2)}) collective-permute-start(bf16[12,64,128]{2,1,0:T(8,128)(2,1)S(1)} %pad_maximum_fusion.1), channel_id=1, source_target_pairs={{0,16},{4,20},{8,24},{12,28},{16,32},{20,36},{24,40},{28,44},{32,4... | collective-permute-start | bytes 589832 | tf_op jit(solution)/shard_map/ppermute | solution.py:242
  26.6 3.3 %copy-start.6 = (bf16[864,128]{1,0:T(8,128)(2,1)}, bf16[864,128]{1,0:T(8,128)(2,1)S(1)}, u32[]{:S(2)}) copy-start(bf16[864,128]{1,0:T(8,128)(2,1)S(1)} %collective-permute-done.9.w3) | copy-start | bytes 663556
  26.6 14.7 %collective-permute-start.4 = (bf16[12,64,128]{2,1,0:T(8,128)(2,1)S(1)}, bf16[12,64,128]{2,1,0:T(8,128)(2,1)S(1)}, u32[]{:S(2)}, u32[]{:S(2)}) collective-permute-start(bf16[12,64,128]{2,1,0:T(8,128)(2,1)S(1)} %slice.54), channel_id=1, source_target_pairs={{16,0},{20,4},{24,8},{28,12},{32,16},{36,20},{40,24},{44,28},{48,3... | collective-permute-start | bytes 589832 | tf_op jit(solution)/shard_map/ppermute | solution.py:242
  27.9 9.5 %collective-permute-start.6 = (bf16[6,64,128]{2,1,0:T(8,128)(2,1)S(1)}, bf16[6,64,128]{2,1,0:T(8,128)(2,1)S(1)}, u32[]{:S(2)}, u32[]{:S(2)}) collective-permute-start(bf16[6,64,128]{2,1,0:T(8,128)(2,1)S(1)} %get-tuple-element.22), channel_id=1, source_target_pairs={{24,0},{28,4},{32,8},{36,12},{40,16},{44,20},{48,24},{52,28},{56,3... | collective-permute-start | bytes 294920 | tf_op jit(solution)/shard_map/ppermute | solution.py:242
  41.3 1.7 %copy-start = (bf16[12,384,256]{2,1,0:T(8,128)(2,1)S(1)}, bf16[12,384,256]{2,1,0:T(8,128)(2,1)}, u32[]{:S(2)}) copy-start(bf16[12,384,256]{2,1,0:T(8,128)(2,1)} %get-tuple-element.8.wf_ref) | copy-start | bytes 7077892
  43.0 0.7 copy-start.1
  101.4 25.5 %all-to-all-start = ((bf16[64,16,128]{2,1,0:T(8,128)(2,1)}), bf16[64,16,128]{2,1,0:T(8,128)(2,1)S(1)}, u32[]{:S(2)}, u32[]{:S(2)}) async-start(bf16[64,16,128]{2,1,0:T(8,128)(2,1)} %bitcast.16), calls=%async_computation | async-start | bytes 524288 | tf_op jit(solution)/shard_map/all_to_all | solution.py:294
  114.9 18.9 %collective-permute-start.10 = (bf16[2,4,64,128]{3,2,1,0:T(8,128)(2,1)S(1)}, bf16[2,4,64,128]{3,2,1,0:T(8,128)(2,1)S(1)}, u32[]{:S(2)}, u32[]{:S(2)}) collective-permute-start(bf16[2,4,64,128]{3,2,1,0:T(8,128)(2,1)S(1)} %get-tuple-element.11), channel_id=1, source_target_pairs={{0,4},{4,0},{8,12},{12,8},{16,20},{20,16},{24,28},{28,24},{32,36},... | collective-permute-start | bytes 393224 | tf_op jit(solution)/shard_map/ppermute | solution.py:289
  127.7 18.0 %all-to-all-start.1 = ((bf16[64,16,128]{2,1,0:T(8,128)(2,1)}), bf16[64,16,128]{2,1,0:T(8,128)(2,1)S(1)}, u32[]{:S(2)}, u32[]{:S(2)}) async-start(bf16[64,16,128]{2,1,0:T(8,128)(2,1)} %broadcast_in_dim.2), calls=%async_computation.1 | async-start | bytes 524288 | tf_op jit(solution)/shard_map/all_to_all | solution.py:296
  145.8 0.7 copy-start.2
where the time goes:
time: 149 us; the launch traced here: 148 us
  Pallas kernels  67.3 us (45%)
  starting transfers between devices  45.6 us (31%)
  waiting for transfers between devices  26.2 us (18%)
  local copies, waits for them, and re-layouts  7.48 us (5%)
    pallas_call x1, Pallas kernels, on_device(): pl.pallas_call(sections_kernel, out_shape=[jax.ShapeDtypeStruct((2, 4, C,...  57.7 us
    ppermute x6, starting transfers between devices, chips_away(): return lax.ppermute(value, 'band', pairs)  18.9 us
    all_to_all x1, starting transfers between devices, on_device(): lax.all_to_all(grads.reshape(64, 16, 128), ('rep', 'band'), 0, 0, tiled=T...  13.5 us
    all_to_all x1, waiting for transfers between devices, on_device(): lax.all_to_all(grads.reshape(64, 16, 128), ('rep', 'band'), 0, 0, tiled=T...  11.5 us
    all_to_all x1, waiting for transfers between devices, on_device(): lax.all_to_all(jnp.broadcast_to(total[None], (64, 16, 128)), ('rep', 'ban...  10.4 us
    pallas_call x1, Pallas kernels, on_device(): pl.pallas_call(weight_blocks_kernel, out_shape=[jax.ShapeDtypeStruct((12,...  7.53 us
    all_to_all x1, starting transfers between devices, on_device(): lax.all_to_all(jnp.broadcast_to(total[None], (64, 16, 128)), ('rep', 'ban...  6.03 us
    unnamed x16, local copies, waits for them, and re-layouts  4.57 us
  transfers between devices with their start and end apart: 13, of which 4 were waited for; matrix products, arithmetic and copies ran while one was open for 3% of the time, Pallas kernels for 5%

commit v1 on v0

v1 whole, which is shorter than its diff:
```python
import jax
import jax.numpy as jnp
from jax import lax
from jax.experimental import pallas as pl
from jax.experimental.pallas import tpu as pltpu
from jax.sharding import PartitionSpec as P

BF = jnp.bfloat16
F32 = jnp.float32
gelu_scale = 0.7978845608028654
cubic_coef = 0.044715

C = 64
WID = 128
ROWS = 64
OWN = 8
OFF = 24
WINDOW = 56
DEPTH = 4


def weight_blocks_kernel(where_ref, own, near, half, other, fwd_ref, bwd_ref, far):
    zero = jnp.zeros((C, C), BF)
    same = (
        lax.broadcasted_iota(jnp.int32, (C, C), 0) == lax.broadcasted_iota(jnp.int32, (C, C), 1)
    ).astype(F32).astype(BF)
    core = where_ref[2]
    far[pl.ds(pl.multiple_of(416 * core, 32), 448), :] = half[...]
    far[pl.ds(pl.multiple_of(416 * (1 - core), 32), 448), :] = other[864:1312, :]
    for piece, hop in ((own, 0), (near, 1 + 2 * core), (other, 3 - 2 * core), (far, 2)):
        section = lax.rem(where_ref[0] - hop + DEPTH, DEPTH)
        for layer in range(3):
            slot = section * 3 + layer
            for kw in range(3):
                taps = []
                for kh in range(3):
                    at = layer * 288 + (kh * 3 + kw) * 32
                    block = piece[at:at + 32, :]
                    taps.append(jnp.concatenate([block[:, :C], block[:, C:]], axis=0))
                tall = jnp.concatenate(taps + [zero] + [zero] + taps, axis=0)
                flat = lax.dot_general(
                    same, tall, (((1,), (1,)), ((), ())), preferred_element_type=F32
                ).astype(BF)
                here = slice(kw * 256, kw * 256 + 256)
                fwd_ref[slot, 0:C, here] = flat[:, 0:256]
                fwd_ref[slot, C:2 * C, here] = flat[:, 256:512]
                there = (2 - kw) * 256
                left = jnp.concatenate([taps[2], taps[1]], axis=1)
                middle = jnp.concatenate([taps[1], taps[0]], axis=1)
                bwd_ref[slot, 0:C, there:there + 128] = left
                bwd_ref[slot, 0:C, there + 128:there + 256] = jnp.concatenate([taps[0], zero], axis=1)
                bwd_ref[slot, C:2 * C, there:there + 128] = jnp.concatenate([zero, taps[2]], axis=1)
                bwd_ref[slot, C:2 * C, there + 128:there + 256] = middle


def sections_kernel(
    where_ref,
    im_c, im_l1, im_r1, im_l2, im_r2, im_l3, im_r3,
    wf_ref, wb_ref,
    keep_ref, send_ref, wg_ref,
    h_ref, a1_ref, a2_ref, p1_ref, p2_ref, g_ref, gp1_ref, gp2_ref,
):
    mine = where_ref[0]
    first_row = where_ref[1]
    core = where_ref[2]
    h_ref[0, 24:32] = im_c[0:8]
    h_ref[0, 16:24] = im_l1[0:8]
    h_ref[0, 32:40] = im_r1[0:8]
    h_ref[0, 8:16] = im_l2[0:8]
    h_ref[0, 40:48] = im_r2[0:8]
    h_ref[0, 2:8] = im_l3[...]
    h_ref[0, 48:54] = im_r3[...]
    g_ref[DEPTH, 24:32] = im_c[8:16]
    g_ref[DEPTH, 16:24] = im_l1[8:16]
    g_ref[DEPTH, 32:40] = im_r1[8:16]
    g_ref[DEPTH, 12:16] = im_l2[8:12]
    g_ref[DEPTH, 40:44] = im_r2[8:12]

    lane = lax.broadcasted_iota(jnp.int32, (128, WID), 1)
    not_first = lane > 0
    not_last = lane < WID - 1
    lane1 = lax.broadcasted_iota(jnp.int32, (1, WID), 1)
    keep_first = (lane1 > 0).astype(F32).astype(BF)
    keep_last = (lane1 < WID - 1).astype(F32).astype(BF)

    def inside(row):
        at = row - OFF + first_row
        return jnp.logical_and(at >= 0, at < ROWS)

    def conv_rows(row, count, source, slab, finish):
        rows = source[pl.ds(row - 1, count + 2)].reshape((count + 2) * C, WID)
        before = pltpu.roll(rows, 1, 1) * keep_first
        after = pltpu.roll(rows, WID - 1, 1) * keep_last
        products = []
        for at in range(0, count, 4):
            halves = []
            for part in (at, at + 2):
                cut = slice(part * C, (part + 4) * C)
                halves.append(jnp.concatenate([before[cut], rows[cut], after[cut]], axis=0))
            products.append(lax.dot_general(
                slab[...],
                jnp.concatenate(halves, axis=1),
                (((1,), (0,)), ((), ())),
                preferred_element_type=F32,
            ))
        for at, product in zip(range(0, count, 4), products):
            for half in range(2):
                for one in range(2):
                    finish(row + at + 2 * half + one, product[one * C:(one + 1) * C, half * WID:(half + 1) * WID])

    def conv_loop(reach, source, slab, finish):
        start = OFF - reach
        count = -(-(8 + 2 * reach) // 4) * 4
        parts = -(-count // 28)
        size = -(-count // (4 * parts)) * 4
        for part in range(parts):
            @pl.when(mine >= 0)
            def _(part=part):
                conv_rows(start + size * part, min(size, count - size * part), source, slab, finish)

    def tangent_of(values):
        return jnp.tanh(values * (gelu_scale + (gelu_scale * cubic_coef) * (values * values)))

    def slope_of(values):
        square = values * values
        tangent = jnp.tanh(values * (gelu_scale + (gelu_scale * cubic_coef) * square))
        return 0.5 * (1.0 + tangent) + (0.5 * values) * (1.0 - tangent * tangent) * (
            gelu_scale + (3.0 * gelu_scale * cubic_coef) * square
        )

    def forward(section, carry):
        def activate(pre_ref, act_ref):
            def finish(row, values):
                pre_ref[section, row] = values
                half = 0.5 * values
                act = half + half * tangent_of(values)
                act_ref[section, row] = jnp.where(inside(row), act, 0.0).astype(BF)

            return finish

        def residual(row, values):
            result = h_ref[section, row].astype(F32) + values
            h_ref[section + 1, row] = jnp.where(inside(row), result, 0.0).astype(BF)

        slot = section * 3
        conv_loop(21 - 3 * section, h_ref.at[section], wf_ref.at[slot],
                  activate(p1_ref, a1_ref))
        conv_loop(20 - 3 * section, a1_ref.at[section], wf_ref.at[slot + 1],
                  activate(p2_ref, a2_ref))
        conv_loop(0 if section == DEPTH - 1 else 19 - 3 * section, a2_ref.at[section],
                  wf_ref.at[slot + 2], residual)
        return carry

    for section in range(DEPTH):
        forward(section, 0)

    def kernel_grad(layer, source, grads):
        wide_in, wide_out = [], []
        for row in range(OFF, OFF + OWN):
            wide_in.append(source[pl.ds(row - 1, 3)].reshape(3 * C, WID))
            out = grads[row].astype(F32)
            after = jnp.where(not_last[:C], pltpu.roll(out, WID - 1, 1), 0.0)
            before = jnp.where(not_first[:C], pltpu.roll(out, 1, 1), 0.0)
            wide_out.append(jnp.concatenate([after, out, before], axis=0).astype(BF))
        result = lax.dot_general(
            jnp.concatenate(wide_in, axis=1),
            jnp.concatenate(wide_out, axis=1),
            (((1,), (1,)), ((), ())),
            preferred_element_type=F32,
        )
        for kw in range(3):
            part = result[:, kw * C:(kw + 1) * C]
            packed = jnp.concatenate([part[:96], part[96:]], axis=1)
            wg_ref[pl.ds((layer * 3 + kw) * 96, 96), :] = packed.astype(BF)

    wg_ref[864:1024, :] = jnp.zeros((160, 128), BF)

    def backward(turn, carry):
        section = DEPTH - 1 - turn
        slot = section * 3

        def through(pre_ref, target):
            def finish(row, values):
                result = values * slope_of(pre_ref[section, row])
                target[section, row] = jnp.where(inside(row), result, 0.0).astype(BF)

            return finish

        def residual(row, values):
            result = g_ref[section + 1, row].astype(F32) + values
            g_ref[section, row] = jnp.where(inside(row), result, 0.0).astype(BF)

        conv_loop(2 + 3 * section, g_ref.at[section + 1], wb_ref.at[slot + 2], through(p2_ref, gp2_ref))
        conv_loop(1 + 3 * section, gp2_ref.at[section], wb_ref.at[slot + 1], through(p1_ref, gp1_ref))

        conv_loop(3 * section, gp1_ref.at[section], wb_ref.at[slot], residual)
        return carry

    for turn in range(DEPTH):
        backward(turn, 0)

    kernel_grad(2, a2_ref.at[mine], g_ref.at[mine + 1])
    kernel_grad(1, a1_ref.at[mine], gp2_ref.at[mine])
    kernel_grad(0, h_ref.at[mine], gp1_ref.at[mine])

    kept = OFF + 4 * core
    sent = OFF + 4 * (1 - core)
    keep_ref[0] = h_ref[mine + 1, pl.ds(kept, 4)]
    keep_ref[1] = g_ref[mine, pl.ds(kept, 4)]
    send_ref[0] = h_ref[mine + 1, pl.ds(sent, 4)]
    send_ref[1] = g_ref[mine, pl.ds(sent, 4)]


def unpack_kernel(sum_ref, out_ref):
    for layer in range(3):
        for kw in range(3):
            base = (layer * 3 + kw) * 96
            block = sum_ref[base:base + 96, :].astype(F32)
            tall = jnp.concatenate([block[:, :C], block[:, C:]], axis=0)
            for kh in range(3):
                out_ref[0, layer, kh, kw] = tall[kh * C:(kh + 1) * C]


def vmem(count):
    return [pl.BlockSpec(memory_space=pltpu.VMEM)] * count


def sections_call(where, pieces, fwd, bwd):
    window = (WINDOW, C, WID)
    return pl.pallas_call(
        sections_kernel,
        out_shape=[
            jax.ShapeDtypeStruct((2, 4, C, WID), BF),
            jax.ShapeDtypeStruct((2, 4, C, WID), BF),
            jax.ShapeDtypeStruct((1024, 128), BF),
        ],
        in_specs=[pl.BlockSpec(memory_space=pltpu.SMEM)] + vmem(9),
        out_specs=vmem(3),
        scratch_shapes=[
            pltpu.VMEM((DEPTH + 1,) + window, BF),
            pltpu.VMEM((DEPTH,) + window, BF),
            pltpu.VMEM((DEPTH,) + window, BF),
            pltpu.VMEM((DEPTH,) + window, F32),
            pltpu.VMEM((DEPTH,) + window, F32),
            pltpu.VMEM((DEPTH + 1,) + window, BF),
            pltpu.VMEM((DEPTH,) + window, BF),
            pltpu.VMEM((DEPTH,) + window, BF),
        ],
        compiler_params=pltpu.CompilerParams(vmem_limit_bytes=62 * 1024 * 1024),
        name="sections",
    )(where, *pieces, fwd, bwd)


def on_device(images, weights, cotangent):
    section = lax.axis_index("section")
    band = lax.axis_index("band")
    core = band % 2
    where = jnp.stack([section, (band // 2) * OWN, core]).astype(jnp.int32)

    field = jnp.stack([images, cotangent]).transpose(1, 0, 3, 2, 4)
    mine = jnp.where(core == 0, field[0], field[1])
    other = jnp.where(core == 0, field[1], field[0])
    bands = lax.axis_size("band")
    swapped = [(i, i ^ 1) for i in range(bands)]
    got = lax.ppermute(other, "band", swapped)
    center = jnp.where(
        core == 0,
        jnp.concatenate([mine, got], axis=1),
        jnp.concatenate([got, mine], axis=1),
    ).reshape(16, C, WID)

    def chips_away(value, chips):
        pairs = [(i, i + 2 * chips) for i in range(bands) if 0 <= i + 2 * chips < bands]
        return lax.ppermute(value, "band", pairs)

    left1 = chips_away(center, 1)
    right1 = chips_away(center, -1)
    left2 = chips_away(jnp.concatenate([center[0:8], center[12:16]]), 2)
    right2 = chips_away(center[0:12], -2)
    left3 = chips_away(center[2:8], 3)
    right3 = chips_away(center[0:6], -3)

    raw = weights.reshape(27, 2, 32, C)
    raw = jnp.concatenate([raw[:, 0], raw[:, 1]], axis=-1).reshape(864, 128)
    near = lax.ppermute(
        raw,
        ("section", "band"),
        [
            (s * bands + b, (s + 1 - 2 * (b % 2)) % DEPTH * bands + b)
            for s in range(DEPTH)
            for b in range(bands)
        ],
    )
    half = lax.ppermute(
        jnp.where(core == 0, raw[:448], raw[416:]),
        "section",
        [(s, (s + 2) % DEPTH) for s in range(DEPTH)],
    )
    other_weights = lax.ppermute(jnp.concatenate([near, half]), "band", swapped)
    fwd, bwd = pl.pallas_call(
        weight_blocks_kernel,
        out_shape=[jax.ShapeDtypeStruct((12, 128, 768), BF)] * 2,
        in_specs=[pl.BlockSpec(memory_space=pltpu.SMEM)] + vmem(4),
        out_specs=vmem(2),
        scratch_shapes=[pltpu.VMEM((864, 128), BF)],
        name="weight_blocks",
    )(where, raw, near, half, other_weights)

    keep, send, grads = sections_call(
        where, (center, left1, right1, left2, right2, left3, right3), fwd, bwd
    )

    received = lax.ppermute(send, "band", swapped)
    zero = jnp.where(core == 0, keep, received)
    one = jnp.where(core == 0, received, keep)
    both = jnp.stack([zero, one]).transpose(1, 0, 3, 2, 4)

    parts = lax.all_to_all(grads.reshape(64, 16, 128), ("rep", "band"), 0, 0, tiled=True)
    total = jnp.sum(parts.astype(F32), axis=0).astype(BF)
    summed = lax.all_to_all(
        jnp.broadcast_to(total[None], (64, 16, 128)), ("rep", "band"), 0, 0, tiled=True
    ).reshape(1024, 128)
    weight_grads = pl.pallas_call(
        unpack_kernel,
        out_shape=jax.ShapeDtypeStruct((1, 3, 3, 3, C, C), F32),
        in_specs=vmem(1),
        out_specs=pl.BlockSpec(memory_space=pltpu.VMEM),
        name="unpack",
    )(summed)
    return both[0][None], both[1][None], weight_grads


def solution(mesh):
    in_specs = (
        P("rep", None, "band", None),
        P("section", None, None, None, None, None),
        P("rep", None, "band", None),
    )
    out_specs = (
        P("section", "rep", None, "band", None),
        P("section", "rep", None, "band", None),
        P("section", None, None, None, None, None),
    )
    return jax.shard_map(
        on_device, mesh=mesh, in_specs=in_specs, out_specs=out_specs, check_vma=False
    )
```

time: 149 us -> 110 us (0.74)
  Pallas kernels: 67.3 us -> 25 us
  waiting for transfers between devices: 26.2 us -> 29.1 us
    pallas_call x1, Pallas kernels: 57.7 us -> 17.8 us  [sections_call(): pl.pallas_call(sections_kernel, out_shape=[jax.ShapeDtypeStruct((2, 4, C,...]
    ppermute x6, waiting for transfers between devices: 3.86 us -> 8.14 us  [chips_away(): return lax.ppermute(value, 'band', pairs)]
    pallas_call x1, Pallas kernels: 7.53 us -> 5.23 us  [on_device(): pl.pallas_call(weight_blocks_kernel, out_shape=[jax.ShapeDtypeStruct((12,...]
    unnamed x16 -> x26, local copies, waits for them, and re-layouts: 4.57 us -> 3.06 us
  transfers between devices with their start and end apart: 13 -> 13, of which waited for: 4 -> 4; matrix products, arithmetic and copies ran while one was open for 3% -> 5% of each run, Pallas kernels for 5% -> 5%
where the time goes in v1:
time: 110 us
  starting transfers between devices  46.4 us (42%)
  waiting for transfers between devices  29.1 us (26%)
  Pallas kernels  25 us (23%)
  local copies, waits for them, and re-layouts  6.05 us (6%)
  other arithmetic  2.04 us (2%)
    ppermute x6, starting transfers between devices, chips_away(): return lax.ppermute(value, 'band', pairs)  19.6 us
    pallas_call x1, Pallas kernels, sections_call(): pl.pallas_call(sections_kernel, out_shape=[jax.ShapeDtypeStruct((2, 4, C,...  17.8 us
    all_to_all x1, starting transfers between devices, on_device(): lax.all_to_all(grads.reshape(64, 16, 128), ('rep', 'band'), 0, 0, tiled=T...  13.9 us
    all_to_all x1, waiting for transfers between devices, on_device(): lax.all_to_all(grads.reshape(64, 16, 128), ('rep', 'band'), 0, 0, tiled=T...  11.5 us
    all_to_all x1, waiting for transfers between devices, on_device(): lax.all_to_all(jnp.broadcast_to(total[None], (64, 16, 128)), ('rep', 'ban...  9.48 us
    ppermute x6, waiting for transfers between devices, chips_away(): return lax.ppermute(value, 'band', pairs)  8.14 us
    all_to_all x1, starting transfers between devices, on_device(): lax.all_to_all(jnp.broadcast_to(total[None], (64, 16, 128)), ('rep', 'ban...  6.03 us
    pallas_call x1, Pallas kernels, on_device(): pl.pallas_call(weight_blocks_kernel, out_shape=[jax.ShapeDtypeStruct((12,...  5.23 us
  transfers between devices with their start and end apart: 13, of which 4 were waited for; matrix products, arithmetic and copies ran while one was open for 5% of the time, Pallas kernels for 5%

profile of v1, /device:TPU:1, one launch (start us, length us, event | category | flops | bytes accessed | tf_op | source)
XLA Modules:
  0.0 109.5 jit_solution(30372955205115270)
XLA Ops:
  0.6 1.0 copy_bitcast_fusion
  1.7 3.3 %collective-permute-start = (bf16[2,4,64,128]{3,2,1,0:T(8,128)(2,1)S(1)}, bf16[2,4,64,128]{3,2,1,0:T(8,128)(2,1)S(1)}, u32[]{:S(2)}, u32[]{:S(2)}) collective-permute-start(bf16[2,4,64,128]{3,2,1,0:T(8,128)(2,1)S(1)} %get-tuple-element.27), channel_id=1, source_target_pairs={{0,4},{4,0},{8,12},{12,8},{16,20},{20,16},{24,28},{28,24},{32,36},... | collective-permute-start | bytes 393224 | tf_op jit(solution)/shard_map/ppermute | solution.py:265
  5.1 1.2 %slice_bitcast_fusion.1 = (bf16[27,32,64]{2,1,0:T(8,128)(2,1)S(1)}, bf16[27,32,64]{2,1,0:T(8,128)(2,1)S(1)}, bf16[27,1,32,64]{3,2,1,0:T(8,128)(2,1)S(1)}, bf16[27,1,32,64]{3,2,1,0:T(8,128)(2,1)S(1)}) fusion(bf16[27,2,32,64]{3,2,1,0:T(8,128)(2,1)} %bitcast.47), kind=kLoop, calls=%fused_computation.19 | loop fusion | bytes 663552 | tf_op jit(solution)/shard_map/squeeze | solution.py:284
  6.2 0.1 fusion.1
  6.4 1.3 %collective-permute-start.8 = (bf16[448,128]{1,0:T(8,128)(2,1)S(1)}, bf16[448,128]{1,0:T(8,128)(2,1)S(1)}, u32[]{:S(2)}, u32[]{:S(2)}) collective-permute-start(bf16[448,128]{1,0:T(8,128)(2,1)S(1)} %bitcast.49), channel_id=1, source_target_pairs={{0,128},{64,192},{128,0},{192,64},{1,129},{65,193},{129,1},{193,65... | collective-permute-start | bytes 344072 | tf_op jit(solution)/shard_map/ppermute | solution.py:294
  7.6 0.1 pad_maximum_fusion.1.own
  7.8 0.9 collective-permute-start.7
  8.7 3.6 %collective-permute-start.1 = (bf16[16,64,128]{2,1,0:T(8,128)(2,1)S(1)}, bf16[16,64,128]{2,1,0:T(8,128)(2,1)S(1)}, u32[]{:S(2)}, u32[]{:S(2)}) collective-permute-start(bf16[16,64,128]{2,1,0:T(8,128)(2,1)S(1)} %bitcast.41), channel_id=1, source_target_pairs={{0,8},{4,12},{8,16},{12,20},{16,24},{20,28},{24,32},{28,36},{32,40... | collective-permute-start | bytes 786440 | tf_op jit(solution)/shard_map/ppermute | solution.py:274
  12.3 1.3 %collective-permute-start.2 = (bf16[16,64,128]{2,1,0:T(8,128)(2,1)S(1)}, bf16[16,64,128]{2,1,0:T(8,128)(2,1)S(1)}, u32[]{:S(2)}, u32[]{:S(2)}) collective-permute-start(bf16[16,64,128]{2,1,0:T(8,128)(2,1)S(1)} %bitcast.42), channel_id=1, source_target_pairs={{8,0},{12,4},{16,8},{20,12},{24,16},{28,20},{32,24},{36,28},{40,32... | collective-permute-start | bytes 786440 | tf_op jit(solution)/shard_map/ppermute | solution.py:274
  13.6 8.1 %collective-permute-start.5 = (bf16[6,64,128]{2,1,0:T(8,128)(2,1)S(1)}, bf16[6,64,128]{2,1,0:T(8,128)(2,1)S(1)}, u32[]{:S(2)}, u32[]{:S(2)}) collective-permute-start(bf16[6,64,128]{2,1,0:T(8,128)(2,1)S(1)} %get-tuple-element.25), channel_id=1, source_target_pairs={{0,24},{4,28},{8,32},{12,36},{16,40},{20,44},{24,48},{28,52},{32,5... | collective-permute-start | bytes 294920 | tf_op jit(solution)/shard_map/ppermute | solution.py:274
  21.8 0.9 collective-permute-start.9
  22.7 4.1 %collective-permute-start.3 = (bf16[12,64,128]{2,1,0:T(8,128)(2,1)S(1)}, bf16[12,64,128]{2,1,0:T(8,128)(2,1)S(1)}, u32[]{:S(2)}, u32[]{:S(2)}) collective-permute-start(bf16[12,64,128]{2,1,0:T(8,128)(2,1)S(1)} %pad_maximum_fusion.2), channel_id=1, source_target_pairs={{0,16},{4,20},{8,24},{12,28},{16,32},{20,36},{24,40},{28,44},{32,4... | collective-permute-start | bytes 589832 | tf_op jit(solution)/shard_map/ppermute | solution.py:274
  26.8 1.3 %collective-permute-start.4 = (bf16[12,64,128]{2,1,0:T(8,128)(2,1)S(1)}, bf16[12,64,128]{2,1,0:T(8,128)(2,1)S(1)}, u32[]{:S(2)}, u32[]{:S(2)}) collective-permute-start(bf16[12,64,128]{2,1,0:T(8,128)(2,1)S(1)} %slice.64), channel_id=1, source_target_pairs={{16,0},{20,4},{24,8},{28,12},{32,16},{36,20},{40,24},{44,28},{48,3... | collective-permute-start | bytes 589832 | tf_op jit(solution)/shard_map/ppermute | solution.py:274
  28.1 1.3 %collective-permute-start.6 = (bf16[6,64,128]{2,1,0:T(8,128)(2,1)S(1)}, bf16[6,64,128]{2,1,0:T(8,128)(2,1)S(1)}, u32[]{:S(2)}, u32[]{:S(2)}) collective-permute-start(bf16[6,64,128]{2,1,0:T(8,128)(2,1)S(1)} %get-tuple-element.24), channel_id=1, source_target_pairs={{24,0},{28,4},{32,8},{36,12},{40,16},{44,20},{48,24},{52,28},{56,3... | collective-permute-start | bytes 294920 | tf_op jit(solution)/shard_map/ppermute | solution.py:274
  29.4 0.6 pad_add_fusion.where_ref
  30.1 5.2 %weight_blocks.1 = (bf16[12,128,768]{2,1,0:T(8,128)(2,1)}, bf16[12,128,768]{2,1,0:T(8,128)(2,1)}) custom-call(s32[3]{0:T(128)} %pad_add_fusion.where_ref, bf16[864,128]{1,0:T(8,128)(2,1)} %copy-done.2, bf16[864,128]{1,0:T(8,128)(2,1)} %copy-done.3, bf16[448,128]{1,0:T(8,128)(2,1)} %copy-done.4, bf16[1312,128]{1,0:T(8,128)(2,1)} %copy-done.5), custom_call_target="tpu_custom_call" | custom-call | tf_op jit(solution)/shard_map/weight_blocks/pallas_call | solution.py:300
  35.3 6.2 %collective-permute-done.6.im_r3 = bf16[6,64,128]{2,1,0:T(8,128)(2,1)S(1)} collective-permute-done((bf16[6,64,128]{2,1,0:T(8,128)(2,1)S(1)}, bf16[6,64,128]{2,1,0:T(8,128)(2,1)S(1)}, u32[]{:S(2)}, u32[]{:S(2)}) %collective-permute-start.6) | collective-permute-done | bytes 98336 | tf_op jit(solution)/shard_map/ppermute | solution.py:274
  41.5 2.0 %collective-permute-done.4.im_r2 = bf16[12,64,128]{2,1,0:T(8,128)(2,1)S(1)} collective-permute-done((bf16[12,64,128]{2,1,0:T(8,128)(2,1)S(1)}, bf16[12,64,128]{2,1,0:T(8,128)(2,1)S(1)}, u32[]{:S(2)}, u32[]{:S(2)}) %collective-permute-start.4) | collective-permute-done | bytes 196640 | tf_op jit(solution)/shard_map/ppermute | solution.py:274
  43.5 0.6 copy-done.9
  44.2 0.1 copy-done.7
  44.3 17.8 %sections.1 = (bf16[2,4,64,128]{3,2,1,0:T(8,128)(2,1)}, bf16[2,4,64,128]{3,2,1,0:T(8,128)(2,1)}, bf16[1024,128]{1,0:T(8,128)(2,1)}) custom-call(s32[3]{0:T(128)} %pad_add_fusion.where_ref, bf16[16,64,128]{2,1,0:T(8,128)(2,1)} %bitcast.43, bf16[16,64,128]{2,1,0:T(8,128)(2,1)} %copy-done.6, bf16[16,64,128]{2,1,0:T(8,128)(2,1)} %copy-done.7, ...), custom_call_target="tpu_custom_call" | custom-call | tf_op jit(solution)/shard_map/sections/pallas_call | solution.py:230
  62.1 13.9 %all-to-all-start = ((bf16[64,16,128]{2,1,0:T(8,128)(2,1)}), bf16[64,16,128]{2,1,0:T(8,128)(2,1)S(1)}, u32[]{:S(2)}, u32[]{:S(2)}) async-start(bf16[64,16,128]{2,1,0:T(8,128)(2,1)} %bitcast.48), calls=%async_computation | async-start | bytes 524288 | tf_op jit(solution)/shard_map/all_to_all | solution.py:318
  76.0 0.5 collective-permute-start.10
  76.6 11.5 %all-to-all-done = bf16[64,16,128]{2,1,0:T(8,128)(2,1)S(1)} async-done(((bf16[64,16,128]{2,1,0:T(8,128)(2,1)}), bf16[64,16,128]{2,1,0:T(8,128)(2,1)S(1)}, u32[]{:S(2)}, u32[]{:S(2)}) %all-to-all-start) | async-done | bytes 262176 | tf_op jit(solution)/shard_map/all_to_all | solution.py:318
  88.1 0.7 broadcast_in_dim.2
  88.8 6.0 %all-to-all-start.1 = ((bf16[64,16,128]{2,1,0:T(8,128)(2,1)}), bf16[64,16,128]{2,1,0:T(8,128)(2,1)S(1)}, u32[]{:S(2)}, u32[]{:S(2)}) async-start(bf16[64,16,128]{2,1,0:T(8,128)(2,1)} %broadcast_in_dim.2), calls=%async_computation.1 | async-start | bytes 524288 | tf_op jit(solution)/shard_map/all_to_all | solution.py:320
  94.9 0.9 select_bitcast_fusion.1
  95.9 0.8 copy.10
  96.6 0.8 copy.11
  97.4 9.5 %all-to-all-done.1 = bf16[64,16,128]{2,1,0:T(8,128)(2,1)S(1)} async-done(((bf16[64,16,128]{2,1,0:T(8,128)(2,1)}), bf16[64,16,128]{2,1,0:T(8,128)(2,1)S(1)}, u32[]{:S(2)}, u32[]{:S(2)}) %all-to-all-start.1) | async-done | bytes 262176 | tf_op jit(solution)/shard_map/all_to_all | solution.py:320
  106.9 0.7 copy-done.1
  107.6 2.0 %unpack.1 = f32[1,3,3,3,64,64]{5,4,3,2,1,0:T(8,128)} custom-call(bf16[1024,128]{1,0:T(8,128)(2,1)} %bitcast.44), custom_call_target="tpu_custom_call" | custom-call | tf_op jit(solution)/shard_map/unpack/pallas_call | solution.py:323
  (42 shorter events, 0.5 us)
Async XLA Ops:
  1.7 6.9 %collective-permute-start = (bf16[2,4,64,128]{3,2,1,0:T(8,128)(2,1)S(1)}, bf16[2,4,64,128]{3,2,1,0:T(8,128)(2,1)S(1)}, u32[]{:S(2)}, u32[]{:S(2)}) collective-permute-start(bf16[2,4,64,128]{3,2,1,0:T(8,128)(2,1)S(1)} %get-tuple-element.27), channel_id=1, source_target_pairs={{0,4},{4,0},{8,12},{12,8},{16,20},{20,16},{24,28},{28,24},{32,36},... | collective-permute-start | bytes 393224 | tf_op jit(solution)/shard_map/ppermute | solution.py:265
  6.4 15.3 %collective-permute-start.8 = (bf16[448,128]{1,0:T(8,128)(2,1)S(1)}, bf16[448,128]{1,0:T(8,128)(2,1)S(1)}, u32[]{:S(2)}, u32[]{:S(2)}) collective-permute-start(bf16[448,128]{1,0:T(8,128)(2,1)S(1)} %bitcast.49), channel_id=1, source_target_pairs={{0,128},{64,192},{128,0},{192,64},{1,129},{65,193},{129,1},{193,65... | collective-permute-start | bytes 344072 | tf_op jit(solution)/shard_map/ppermute | solution.py:294
  7.8 22.3 %copy-start.2 = (bf16[864,128]{1,0:T(8,128)(2,1)}, bf16[864,128]{1,0:T(8,128)(2,1)S(1)}, u32[]{:S(2)}) copy-start(bf16[864,128]{1,0:T(8,128)(2,1)S(1)} %pad_maximum_fusion.1.own) | copy-start | bytes 663556
  7.8 13.9 %collective-permute-start.7 = (bf16[864,128]{1,0:T(8,128)(2,1)S(1)}, bf16[864,128]{1,0:T(8,128)(2,1)S(1)}, u32[]{:S(2)}, u32[]{:S(2)}) collective-permute-start(bf16[864,128]{1,0:T(8,128)(2,1)S(1)} %pad_maximum_fusion.1.own), channel_id=1, source_target_pairs={{0,64},{4,196},{8,72},{12,204},{16,80},{20,212},{24,88},{28,220},{... | collective-permute-start | bytes 663560 | tf_op jit(solution)/shard_map/ppermute | solution.py:285
  8.7 34.8 %copy-start = (bf16[2,8,64,128]{3,2,1,0:T(8,128)(2,1)}, bf16[2,8,64,128]{3,2,1,0:T(8,128)(2,1)S(1)}, u32[]{:S(2)}) copy-start(bf16[2,8,64,128]{3,2,1,0:T(8,128)(2,1)S(1)} %maximum_select_fusion) | copy-start | bytes 786436
  8.7 34.7 %collective-permute-start.1 = (bf16[16,64,128]{2,1,0:T(8,128)(2,1)S(1)}, bf16[16,64,128]{2,1,0:T(8,128)(2,1)S(1)}, u32[]{:S(2)}, u32[]{:S(2)}) collective-permute-start(bf16[16,64,128]{2,1,0:T(8,128)(2,1)S(1)} %bitcast.41), channel_id=1, source_target_pairs={{0,8},{4,12},{8,16},{12,20},{16,24},{20,28},{24,32},{28,36},{32,40... | collective-permute-start | bytes 786440 | tf_op jit(solution)/shard_map/ppermute | solution.py:274
  12.3 31.1 %collective-permute-start.2 = (bf16[16,64,128]{2,1,0:T(8,128)(2,1)S(1)}, bf16[16,64,128]{2,1,0:T(8,128)(2,1)S(1)}, u32[]{:S(2)}, u32[]{:S(2)}) collective-permute-start(bf16[16,64,128]{2,1,0:T(8,128)(2,1)S(1)} %bitcast.42), channel_id=1, source_target_pairs={{8,0},{12,4},{16,8},{20,12},{24,16},{28,20},{32,24},{36,28},{40,32... | collective-permute-start | bytes 786440 | tf_op jit(solution)/shard_map/ppermute | solution.py:274
  13.6 13.2 %collective-permute-start.5 = (bf16[6,64,128]{2,1,0:T(8,128)(2,1)S(1)}, bf16[6,64,128]{2,1,0:T(8,128)(2,1)S(1)}, u32[]{:S(2)}, u32[]{:S(2)}) collective-permute-start(bf16[6,64,128]{2,1,0:T(8,128)(2,1)S(1)} %get-tuple-element.25), channel_id=1, source_target_pairs={{0,24},{4,28},{8,32},{12,36},{16,40},{20,44},{24,48},{28,52},{32,5... | collective-permute-start | bytes 294920 | tf_op jit(solution)/shard_map/ppermute | solution.py:274
  21.7 8.4 %copy-start.4 = (bf16[448,128]{1,0:T(8,128)(2,1)}, bf16[448,128]{1,0:T(8,128)(2,1)S(1)}, u32[]{:S(2)}) copy-start(bf16[448,128]{1,0:T(8,128)(2,1)S(1)} %collective-permute-done.8.half) | copy-start | bytes 344068
  21.7 8.3 %copy-start.3 = (bf16[864,128]{1,0:T(8,128)(2,1)}, bf16[864,128]{1,0:T(8,128)(2,1)S(1)}, u32[]{:S(2)}) copy-start(bf16[864,128]{1,0:T(8,128)(2,1)S(1)} %collective-permute-done.7.near) | copy-start | bytes 663556
  21.8 6.3 %collective-permute-start.9 = (bf16[1312,128]{1,0:T(8,128)(2,1)S(1)}, bf16[1312,128]{1,0:T(8,128)(2,1)S(1)}, u32[]{:S(2)}, u32[]{:S(2)}) collective-permute-start(bf16[1312,128]{1,0:T(8,128)(2,1)S(1)} %pad_maximum_fusion), channel_id=1, source_target_pairs={{0,4},{4,0},{8,12},{12,8},{16,20},{20,16},{24,28},{28,24},{32,36},... | collective-permute-start | bytes 1007624 | tf_op jit(solution)/shard_map/ppermute | solution.py:299
  22.7 18.8 %collective-permute-start.3 = (bf16[12,64,128]{2,1,0:T(8,128)(2,1)S(1)}, bf16[12,64,128]{2,1,0:T(8,128)(2,1)S(1)}, u32[]{:S(2)}, u32[]{:S(2)}) collective-permute-start(bf16[12,64,128]{2,1,0:T(8,128)(2,1)S(1)} %pad_maximum_fusion.2), channel_id=1, source_target_pairs={{0,16},{4,20},{8,24},{12,28},{16,32},{20,36},{24,40},{28,44},{32,4... | collective-permute-start | bytes 589832 | tf_op jit(solution)/shard_map/ppermute | solution.py:274
  26.8 16.7 %copy-start.10 = (bf16[6,64,128]{2,1,0:T(8,128)(2,1)}, bf16[6,64,128]{2,1,0:T(8,128)(2,1)S(1)}, u32[]{:S(2)}) copy-start(bf16[6,64,128]{2,1,0:T(8,128)(2,1)S(1)} %collective-permute-done.5.im_l3) | copy-start | bytes 294916
  26.8 16.6 %collective-permute-start.4 = (bf16[12,64,128]{2,1,0:T(8,128)(2,1)S(1)}, bf16[12,64,128]{2,1,0:T(8,128)(2,1)S(1)}, u32[]{:S(2)}, u32[]{:S(2)}) collective-permute-start(bf16[12,64,128]{2,1,0:T(8,128)(2,1)S(1)} %slice.64), channel_id=1, source_target_pairs={{16,0},{20,4},{24,8},{28,12},{32,16},{36,20},{40,24},{44,28},{48,3... | collective-permute-start | bytes 589832 | tf_op jit(solution)/shard_map/ppermute | solution.py:274
  28.1 1.9 %copy-start.5 = (bf16[1312,128]{1,0:T(8,128)(2,1)}, bf16[1312,128]{1,0:T(8,128)(2,1)S(1)}, u32[]{:S(2)}) copy-start(bf16[1312,128]{1,0:T(8,128)(2,1)S(1)} %collective-permute-done.9.other) | copy-start | bytes 1007620
  28.1 13.3 %collective-permute-start.6 = (bf16[6,64,128]{2,1,0:T(8,128)(2,1)S(1)}, bf16[6,64,128]{2,1,0:T(8,128)(2,1)S(1)}, u32[]{:S(2)}, u32[]{:S(2)}) collective-permute-start(bf16[6,64,128]{2,1,0:T(8,128)(2,1)S(1)} %get-tuple-element.24), channel_id=1, source_target_pairs={{24,0},{28,4},{32,8},{36,12},{40,16},{44,20},{48,24},{52,28},{56,3... | collective-permute-start | bytes 294920 | tf_op jit(solution)/shard_map/ppermute | solution.py:274
  41.5 2.0 %copy-start.11 = (bf16[6,64,128]{2,1,0:T(8,128)(2,1)}, bf16[6,64,128]{2,1,0:T(8,128)(2,1)S(1)}, u32[]{:S(2)}) copy-start(bf16[6,64,128]{2,1,0:T(8,128)(2,1)S(1)} %collective-permute-done.6.im_r3) | copy-start | bytes 294916
  41.5 2.0 %copy-start.8 = (bf16[12,64,128]{2,1,0:T(8,128)(2,1)}, bf16[12,64,128]{2,1,0:T(8,128)(2,1)S(1)}, u32[]{:S(2)}) copy-start(bf16[12,64,128]{2,1,0:T(8,128)(2,1)S(1)} %collective-permute-done.3.im_l2) | copy-start | bytes 589828
  43.4 0.7 copy-start.9
  43.5 0.8 copy-start.6
  43.5 0.9 copy-start.7
  62.1 25.9 %all-to-all-start = ((bf16[64,16,128]{2,1,0:T(8,128)(2,1)}), bf16[64,16,128]{2,1,0:T(8,128)(2,1)S(1)}, u32[]{:S(2)}, u32[]{:S(2)}) async-start(bf16[64,16,128]{2,1,0:T(8,128)(2,1)} %bitcast.48), calls=%async_computation | async-start | bytes 524288 | tf_op jit(solution)/shard_map/all_to_all | solution.py:318
  76.0 18.9 %collective-permute-start.10 = (bf16[2,4,64,128]{3,2,1,0:T(8,128)(2,1)}, bf16[2,4,64,128]{3,2,1,0:T(8,128)(2,1)S(1)}, u32[]{:S(2)}, u32[]{:S(2)}) collective-permute-start(bf16[2,4,64,128]{3,2,1,0:T(8,128)(2,1)} %get-tuple-element.11), channel_id=1, source_target_pairs={{0,4},{4,0},{8,12},{12,8},{16,20},{20,16},{24,28},{28,24},{32,36},... | collective-permute-start | bytes 393224 | tf_op jit(solution)/shard_map/ppermute | solution.py:313
  88.8 18.0 %all-to-all-start.1 = ((bf16[64,16,128]{2,1,0:T(8,128)(2,1)}), bf16[64,16,128]{2,1,0:T(8,128)(2,1)S(1)}, u32[]{:S(2)}, u32[]{:S(2)}) async-start(bf16[64,16,128]{2,1,0:T(8,128)(2,1)} %broadcast_in_dim.2), calls=%async_computation.1 | async-start | bytes 524288 | tf_op jit(solution)/shard_map/all_to_all | solution.py:320
  106.9 0.7 copy-start.1

commit v2 on v1

v2 whole, which is shorter than its diff:
```python
import jax
import jax.numpy as jnp
from jax import lax
from jax.experimental import pallas as pl
from jax.experimental.pallas import tpu as pltpu
from jax.sharding import PartitionSpec as P

BF = jnp.bfloat16
F32 = jnp.float32
gelu_scale = 0.7978845608028654
cubic_coef = 0.044715

C = 64
WID = 128
ROWS = 64
OWN = 8
OFF = 24
WINDOW = 56
DEPTH = 4
LOW = 19
KEPT = 20


def weight_blocks_kernel(where_ref, own, near, half, other, fwd_ref, bwd_ref, far):
    zero = jnp.zeros((C, C), BF)
    same = (
        lax.broadcasted_iota(jnp.int32, (C, C), 0) == lax.broadcasted_iota(jnp.int32, (C, C), 1)
    ).astype(F32).astype(BF)
    core = where_ref[2]
    far[pl.ds(pl.multiple_of(416 * core, 32), 448), :] = half[...]
    far[pl.ds(pl.multiple_of(416 * (1 - core), 32), 448), :] = other[864:1312, :]
    for piece, hop in ((own, 0), (near, 1 + 2 * core), (other, 3 - 2 * core), (far, 2)):
        section = lax.rem(where_ref[0] - hop + DEPTH, DEPTH)
        for layer in range(3):
            slot = section * 3 + layer
            for kw in range(3):
                taps = []
                for kh in range(3):
                    at = layer * 288 + (kh * 3 + kw) * 32
                    block = piece[at:at + 32, :]
                    taps.append(jnp.concatenate([block[:, :C], block[:, C:]], axis=0))
                tall = jnp.concatenate(taps + [zero] + [zero] + taps, axis=0)
                flat = lax.dot_general(
                    same, tall, (((1,), (1,)), ((), ())), preferred_element_type=F32
                ).astype(BF)
                here = slice(kw * 256, kw * 256 + 256)
                fwd_ref[slot, 0:C, here] = flat[:, 0:256]
                fwd_ref[slot, C:2 * C, here] = flat[:, 256:512]
                there = (2 - kw) * 256
                left = jnp.concatenate([taps[2], taps[1]], axis=1)
                middle = jnp.concatenate([taps[1], taps[0]], axis=1)
                bwd_ref[slot, 0:C, there:there + 128] = left
                bwd_ref[slot, 0:C, there + 128:there + 256] = jnp.concatenate([taps[0], zero], axis=1)
                bwd_ref[slot, C:2 * C, there:there + 128] = jnp.concatenate([zero, taps[2]], axis=1)
                bwd_ref[slot, C:2 * C, there + 128:there + 256] = middle


def conv_tools(where_ref):
    first_row = where_ref[1]
    lane = lax.broadcasted_iota(jnp.int32, (1, WID), 1)
    keep_first = (lane > 0).astype(F32).astype(BF)
    keep_last = (lane < WID - 1).astype(F32).astype(BF)

    def inside(row):
        at = row - OFF + first_row
        return jnp.logical_and(at >= 0, at < ROWS)

    def conv_rows(row, count, source, slab, finish):
        rows = source[pl.ds(row - 1, count + 2)].reshape((count + 2) * C, WID)
        before = pltpu.roll(rows, 1, 1) * keep_first
        after = pltpu.roll(rows, WID - 1, 1) * keep_last
        products = []
        for at in range(0, count, 4):
            halves = []
            for part in (at, at + 2):
                cut = slice(part * C, (part + 4) * C)
                halves.append(jnp.concatenate([before[cut], rows[cut], after[cut]], axis=0))
            products.append(
                lax.dot_general(
                    slab[...],
                    jnp.concatenate(halves, axis=1),
                    (((1,), (0,)), ((), ())),
                    preferred_element_type=F32,
                )
            )
        for at, product in zip(range(0, count, 4), products):
            for half in range(2):
                for one in range(2):
                    finish(
                        row + at + 2 * half + one,
                        product[one * C:(one + 1) * C, half * WID:(half + 1) * WID],
                    )

    def conv(reach, source, slab, finish):
        start = OFF - reach
        count = -(-(OWN + 2 * reach) // 4) * 4
        parts = -(-count // 28)
        size = -(-count // (4 * parts)) * 4
        for part in range(parts):

            @pl.when(where_ref[0] >= 0)
            def _(part=part):
                conv_rows(start + size * part, min(size, count - size * part), source, slab, finish)

    return inside, conv


def tangent_of(values):
    return jnp.tanh(values * (gelu_scale + (gelu_scale * cubic_coef) * (values * values)))


def slope_of(values):
    square = values * values
    tangent = jnp.tanh(values * (gelu_scale + (gelu_scale * cubic_coef) * square))
    return 0.5 * (1.0 + tangent) + (0.5 * values) * (1.0 - tangent * tangent) * (
        gelu_scale + (3.0 * gelu_scale * cubic_coef) * square
    )


def kernel_grad(layer, source, grads, wg_ref):
    lane = lax.broadcasted_iota(jnp.int32, (C, WID), 1)
    wide_in, wide_out = [], []
    for row in range(OWN):
        wide_in.append(source[pl.ds(row, 3)].reshape(3 * C, WID))
        out = grads[OFF + row].astype(F32)
        after = jnp.where(lane < WID - 1, pltpu.roll(out, WID - 1, 1), 0.0)
        before = jnp.where(lane > 0, pltpu.roll(out, 1, 1), 0.0)
        wide_out.append(jnp.concatenate([after, out, before], axis=0).astype(BF))
    result = lax.dot_general(
        jnp.concatenate(wide_in, axis=1),
        jnp.concatenate(wide_out, axis=1),
        (((1,), (1,)), ((), ())),
        preferred_element_type=F32,
    )
    for kw in range(3):
        part = result[:, kw * C:(kw + 1) * C]
        packed = jnp.concatenate([part[:96], part[96:]], axis=1)
        wg_ref[pl.ds((layer * 3 + kw) * 96, 96), :] = packed.astype(BF)


def back_section(where_ref, section, level, slot, reach, pre, grads, gp1_ref, gp2_ref, wb_ref):
    inside, conv = conv_tools(where_ref)

    def through(layer, target):
        def finish(row, values):
            result = values * slope_of(pre(section, layer, row))
            target[level, row] = jnp.where(inside(row), result, 0.0).astype(BF)

        return finish

    def residual(row, values):
        result = grads[level + 1, row].astype(F32) + values
        grads[level, row] = jnp.where(inside(row), result, 0.0).astype(BF)

    conv(reach + 2, grads.at[level + 1], wb_ref.at[slot + 2], through(1, gp2_ref))
    conv(reach + 1, gp2_ref.at[level], wb_ref.at[slot + 1], through(0, gp1_ref))
    conv(reach, gp1_ref.at[level], wb_ref.at[slot], residual)


def first_kernel(
    where_ref,
    im_c, im_l1, im_r1, im_l2, im_r2,
    wf_ref, wb_ref,
    act_keep_ref, act_send_ref, top_ref, edge_ref, pre_ref, in_ref, wg_ref,
    h_ref, a1_ref, a2_ref, p1_ref, p2_ref, g_ref, gp1_ref, gp2_ref,
):
    mine = where_ref[0]
    core = where_ref[2]
    inside, conv = conv_tools(where_ref)
    h_ref[0, 24:32] = im_c[0:8]
    h_ref[0, 16:24] = im_l1[0:8]
    h_ref[0, 32:40] = im_r1[0:8]
    h_ref[0, 8:16] = im_l2[...]
    h_ref[0, 40:48] = im_r2[...]
    g_ref[2, 24:32] = im_c[8:16]
    g_ref[2, 18:24] = im_l1[8:14]
    g_ref[2, 32:38] = im_r1[8:14]

    def activate(section, keep_ref, act_ref):
        def finish(row, values):
            keep_ref[section, row] = values
            half = 0.5 * values
            act = half + half * tangent_of(values)
            act_ref[section, row] = jnp.where(inside(row), act, 0.0).astype(BF)

        return finish

    for section in range(DEPTH):
        slot = section * 3

        def residual(row, values, section=section):
            result = h_ref[section, row].astype(F32) + values
            h_ref[section + 1, row] = jnp.where(inside(row), result, 0.0).astype(BF)

        conv(15 - 3 * section, h_ref.at[section], wf_ref.at[slot], activate(section, p1_ref, a1_ref))
        conv(14 - 3 * section, a1_ref.at[section], wf_ref.at[slot + 1], activate(section, p2_ref, a2_ref))
        conv(
            0 if section == DEPTH - 1 else 13 - 3 * section,
            a2_ref.at[section], wf_ref.at[slot + 2], residual,
        )

    def pre(section, layer, row):
        return (p2_ref if layer else p1_ref)[section, row]

    back_section(where_ref, 3, 1, 9, 3, pre, g_ref, gp1_ref, gp2_ref, wb_ref)
    back_section(where_ref, 2, 0, 6, 0, pre, g_ref, gp1_ref, gp2_ref, wb_ref)

    act_keep_ref[...] = h_ref[mine + 1, pl.ds(OFF + 4 * core, 4)]
    act_send_ref[...] = h_ref[mine + 1, pl.ds(OFF + 4 * (1 - core), 4)]
    edge_ref[...] = g_ref[0, OFF:OFF + OWN]
    for section in range(2):
        pre_ref[section, 0] = p1_ref[section, LOW:LOW + KEPT]
        pre_ref[section, 1] = p2_ref[section, LOW:LOW + KEPT]

    @pl.when(mine >= 2)
    def _():
        top_ref[...] = g_ref[mine - 2, OFF:OFF + OWN]
        kernel_grad(2, a2_ref.at[mine, OFF - 1:OFF + 9], g_ref.at[mine - 1], wg_ref)
        kernel_grad(1, a1_ref.at[mine, OFF - 1:OFF + 9], gp2_ref.at[mine - 2], wg_ref)
        kernel_grad(0, h_ref.at[mine, OFF - 1:OFF + 9], gp1_ref.at[mine - 2], wg_ref)
        wg_ref[864:1024, :] = jnp.zeros((160, 128), BF)
        in_ref[...] = jnp.zeros(in_ref.shape, BF)

    @pl.when(mine < 2)
    def _():
        top_ref[...] = jnp.zeros(top_ref.shape, BF)
        wg_ref[...] = jnp.zeros(wg_ref.shape, BF)
        in_ref[0] = h_ref[mine, OFF - 1:OFF + 9]
        in_ref[1] = a1_ref[mine, OFF - 1:OFF + 9]
        in_ref[2] = a2_ref[mine, OFF - 1:OFF + 9]


def second_kernel(
    where_ref,
    edge_ref, left_ref, right_ref, pre_ref, in_ref, top_ref, top_wg_ref, wb_ref,
    keep_ref, send_ref, wg_ref,
    g_ref, gp1_ref, gp2_ref,
):
    mine = where_ref[0]
    core = where_ref[2]
    g_ref[2, OFF:OFF + OWN] = edge_ref[...]
    g_ref[2, OFF - 6:OFF] = left_ref[...]
    g_ref[2, OFF + OWN:OFF + OWN + 6] = right_ref[...]

    @pl.when(mine < 2)
    def _():
        def pre(section, layer, row):
            return pre_ref[section, layer, row - LOW]

        back_section(where_ref, 1, 1, 3, 3, pre, g_ref, gp1_ref, gp2_ref, wb_ref)
        back_section(where_ref, 0, 0, 0, 0, pre, g_ref, gp1_ref, gp2_ref, wb_ref)
        kernel_grad(2, in_ref.at[2], g_ref.at[mine + 1], wg_ref)
        kernel_grad(1, in_ref.at[1], gp2_ref.at[mine], wg_ref)
        kernel_grad(0, in_ref.at[0], gp1_ref.at[mine], wg_ref)
        wg_ref[864:1024, :] = jnp.zeros((160, 128), BF)
        keep_ref[...] = g_ref[mine, pl.ds(OFF + 4 * core, 4)]
        send_ref[...] = g_ref[mine, pl.ds(OFF + 4 * (1 - core), 4)]

    @pl.when(mine >= 2)
    def _():
        wg_ref[...] = top_wg_ref[...]
        keep_ref[...] = top_ref[pl.ds(4 * core, 4)]
        send_ref[...] = top_ref[pl.ds(4 * (1 - core), 4)]


def unpack_kernel(sum_ref, out_ref):
    for layer in range(3):
        for kw in range(3):
            base = (layer * 3 + kw) * 96
            block = sum_ref[base:base + 96, :].astype(F32)
            tall = jnp.concatenate([block[:, :C], block[:, C:]], axis=0)
            for kh in range(3):
                out_ref[0, layer, kh, kw] = tall[kh * C:(kh + 1) * C]


def vmem(count):
    return [pl.BlockSpec(memory_space=pltpu.VMEM)] * count


WINDOW_SHAPE = (WINDOW, C, WID)


def first_call(where, pieces, fwd, bwd):
    return pl.pallas_call(
        first_kernel,
        out_shape=[
            jax.ShapeDtypeStruct((4, C, WID), BF),
            jax.ShapeDtypeStruct((4, C, WID), BF),
            jax.ShapeDtypeStruct((OWN, C, WID), BF),
            jax.ShapeDtypeStruct((OWN, C, WID), BF),
            jax.ShapeDtypeStruct((2, 2, KEPT, C, WID), F32),
            jax.ShapeDtypeStruct((3, 10, C, WID), BF),
            jax.ShapeDtypeStruct((1024, 128), BF),
        ],
        in_specs=[pl.BlockSpec(memory_space=pltpu.SMEM)] + vmem(7),
        out_specs=vmem(7),
        scratch_shapes=[
            pltpu.VMEM((DEPTH + 1,) + WINDOW_SHAPE, BF),
            pltpu.VMEM((DEPTH,) + WINDOW_SHAPE, BF),
            pltpu.VMEM((DEPTH,) + WINDOW_SHAPE, BF),
            pltpu.VMEM((DEPTH,) + WINDOW_SHAPE, F32),
            pltpu.VMEM((DEPTH,) + WINDOW_SHAPE, F32),
            pltpu.VMEM((3,) + WINDOW_SHAPE, BF),
            pltpu.VMEM((2,) + WINDOW_SHAPE, BF),
            pltpu.VMEM((2,) + WINDOW_SHAPE, BF),
        ],
        compiler_params=pltpu.CompilerParams(vmem_limit_bytes=58 * 1024 * 1024),
        name="first_part",
    )(where, *pieces, fwd, bwd)


def second_call(where, *arrays):
    return pl.pallas_call(
        second_kernel,
        out_shape=[
            jax.ShapeDtypeStruct((4, C, WID), BF),
            jax.ShapeDtypeStruct((4, C, WID), BF),
            jax.ShapeDtypeStruct((1024, 128), BF),
        ],
        in_specs=[pl.BlockSpec(memory_space=pltpu.SMEM)] + vmem(8),
        out_specs=vmem(3),
        scratch_shapes=[
            pltpu.VMEM((3,) + WINDOW_SHAPE, BF),
            pltpu.VMEM((2,) + WINDOW_SHAPE, BF),
            pltpu.VMEM((2,) + WINDOW_SHAPE, BF),
        ],
        compiler_params=pltpu.CompilerParams(vmem_limit_bytes=32 * 1024 * 1024),
        name="second_part",
    )(where, *arrays)


def on_device(images, weights, cotangent):
    section = lax.axis_index("section")
    band = lax.axis_index("band")
    core = band % 2
    where = jnp.stack([section, (band // 2) * OWN, core]).astype(jnp.int32)

    field = jnp.stack([images, cotangent]).transpose(1, 0, 3, 2, 4)
    mine = jnp.where(core == 0, field[0], field[1])
    other = jnp.where(core == 0, field[1], field[0])
    bands = lax.axis_size("band")
    swapped = [(i, i ^ 1) for i in range(bands)]
    got = lax.ppermute(other, "band", swapped)
    center = jnp.where(
        core == 0,
        jnp.concatenate([mine, got], axis=1),
        jnp.concatenate([got, mine], axis=1),
    ).reshape(16, C, WID)

    def chips_away(value, chips):
        pairs = [(i, i + 2 * chips) for i in range(bands) if 0 <= i + 2 * chips < bands]
        return lax.ppermute(value, "band", pairs)

    left1 = chips_away(jnp.concatenate([center[0:8], center[10:16]]), 1)
    right1 = chips_away(center[0:14], -1)
    left2 = chips_away(center[0:8], 2)
    right2 = chips_away(center[0:8], -2)

    raw = weights.reshape(27, 2, 32, C)
    raw = jnp.concatenate([raw[:, 0], raw[:, 1]], axis=-1).reshape(864, 128)
    near = lax.ppermute(
        raw,
        ("section", "band"),
        [
            (s * bands + b, (s + 1 - 2 * (b % 2)) % DEPTH * bands + b)
            for s in range(DEPTH)
            for b in range(bands)
        ],
    )
    half = lax.ppermute(
        jnp.where(core == 0, raw[:448], raw[416:]),
        "section",
        [(s, (s + 2) % DEPTH) for s in range(DEPTH)],
    )
    other_weights = lax.ppermute(jnp.concatenate([near, half]), "band", swapped)
    fwd, bwd = pl.pallas_call(
        weight_blocks_kernel,
        out_shape=[jax.ShapeDtypeStruct((12, 128, 768), BF)] * 2,
        in_specs=[pl.BlockSpec(memory_space=pltpu.SMEM)] + vmem(4),
        out_specs=vmem(2),
        scratch_shapes=[pltpu.VMEM((864, 128), BF)],
        name="weight_blocks",
    )(where, raw, near, half, other_weights)

    act_keep, act_send, top, edge, pre, inputs, top_wg = first_call(
        where, (center, left1, right1, left2, right2), fwd, bwd
    )
    edge_left = chips_away(edge[2:8], 1)
    edge_right = chips_away(edge[0:6], -1)
    act_got = lax.ppermute(act_send, "band", swapped)
    keep, send, grads = second_call(
        where, edge, edge_left, edge_right, pre, inputs, top, top_wg, bwd
    )
    got_back = lax.ppermute(send, "band", swapped)

    def placed(kept, received):
        zero = jnp.where(core == 0, kept, received)
        one = jnp.where(core == 0, received, kept)
        return jnp.stack([zero, one]).transpose(0, 2, 1, 3)[None]

    parts = lax.all_to_all(grads.reshape(64, 16, 128), ("rep", "band"), 0, 0, tiled=True)
    total = jnp.sum(parts.astype(F32), axis=0).astype(BF)
    summed = lax.all_to_all(
        jnp.broadcast_to(total[None], (64, 16, 128)), ("rep", "band"), 0, 0, tiled=True
    ).reshape(1024, 128)
    weight_grads = pl.pallas_call(
        unpack_kernel,
        out_shape=jax.ShapeDtypeStruct((1, 3, 3, 3, C, C), F32),
        in_specs=vmem(1),
        out_specs=pl.BlockSpec(memory_space=pltpu.VMEM),
        name="unpack",
    )(summed)
    return placed(act_keep, act_got), placed(keep, got_back), weight_grads


def solution(mesh):
    in_specs = (
        P("rep", None, "band", None),
        P("section", None, None, None, None, None),
        P("rep", None, "band", None),
    )
    out_specs = (
        P("section", "rep", None, "band", None),
        P("section", "rep", None, "band", None),
        P("section", None, None, None, None, None),
    )
    return jax.shard_map(
        on_device, mesh=mesh, in_specs=in_specs, out_specs=out_specs, check_vma=False
    )
```

time: 110 us -> 120 us (1.091)
  local copies, waits for them, and re-layouts: 6.05 us -> 13.2 us
  Pallas kernels: 25 us -> 29.2 us
  waiting for transfers between devices: 29.1 us -> 27 us
  starting transfers between devices: 46.4 us -> 47.7 us
    ppermute x6, waiting for transfers between devices: 8.14 us -> 1.63 us  [chips_away(): return lax.ppermute(value, 'band', pairs)]
    unnamed x26 -> x40, local copies, waits for them, and re-layouts: 3.06 us -> 9.31 us
    pallas_call x1 -> x2, Pallas kernels: 17.8 us -> 22.1 us  [the longest x1 17.3 us: first_call(): pl.pallas_call(first_kernel, out_shape=[jax.ShapeDtypeStruct((4, C, WID),...]
    ppermute x1, waiting for transfers between devices: 0.01 us -> 2.68 us  [on_device(): lax.ppermute(jnp.where(core == 0, raw[:448], raw[416:]), 'section', [(s,...]
    ppermute x6, starting transfers between devices: 19.6 us -> 17.8 us  [chips_away(): return lax.ppermute(value, 'band', pairs)]
    all_to_all x1, starting transfers between devices: 13.9 us -> 15.5 us  [on_device(): lax.all_to_all(grads.reshape(64, 16, 128), ('rep', 'band'), 0, 0, tiled=T...]
    ppermute x1, waiting for transfers between devices: 0.01 us -> 1.38 us  [on_device(): lax.ppermute(raw, ('section', 'band'), [(s * bands + b, (s + 1 - 2 * (b %...]
  transfers between devices with their start and end apart: 13 -> 14, of which waited for: 4 -> 7; matrix products, arithmetic and copies ran while one was open for 5% -> 4% of each run, Pallas kernels for 5% -> 4%
where the time goes in v2:
time: 120 us; the launch traced here: 119 us
  starting transfers between devices  47.7 us (40%)
  Pallas kernels  29.2 us (24%)
  waiting for transfers between devices  27 us (22%)
  local copies, waits for them, and re-layouts  13.2 us (11%)
    ppermute x6, starting transfers between devices, chips_away(): return lax.ppermute(value, 'band', pairs)  17.8 us
    pallas_call x1, Pallas kernels, first_call(): pl.pallas_call(first_kernel, out_shape=[jax.ShapeDtypeStruct((4, C, WID),...  17.3 us
    all_to_all x1, starting transfers between devices, on_device(): lax.all_to_all(grads.reshape(64, 16, 128), ('rep', 'band'), 0, 0, tiled=T...  15.5 us
    all_to_all x1, waiting for transfers between devices, on_device(): lax.all_to_all(grads.reshape(64, 16, 128), ('rep', 'band'), 0, 0, tiled=T...  11.4 us
    all_to_all x1, waiting for transfers between devices, on_device(): lax.all_to_all(jnp.broadcast_to(total[None], (64, 16, 128)), ('rep', 'ban...  9.71 us
    unnamed x40, local copies, waits for them, and re-layouts  9.31 us
    all_to_all x1, starting transfers between devices, on_device(): lax.all_to_all(jnp.broadcast_to(total[None], (64, 16, 128)), ('rep', 'ban...  6.03 us
    pallas_call x1, Pallas kernels, on_device(): pl.pallas_call(weight_blocks_kernel, out_shape=[jax.ShapeDtypeStruct((12,...  5.18 us
  transfers between devices with their start and end apart: 14, of which 7 were waited for; matrix products, arithmetic and copies ran while one was open for 4% of the time, Pallas kernels for 4%

profile of v2, /device:TPU:1, one launch (start us, length us, event | category | flops | bytes accessed | tf_op | source)
XLA Modules:
  0.0 119.3 jit_solution(5665472503496547662)
XLA Ops:
  0.6 1.0 copy_bitcast_fusion
  1.7 3.3 %collective-permute-start = (bf16[2,4,64,128]{3,2,1,0:T(8,128)(2,1)S(1)}, bf16[2,4,64,128]{3,2,1,0:T(8,128)(2,1)S(1)}, u32[]{:S(2)}, u32[]{:S(2)}) collective-permute-start(bf16[2,4,64,128]{3,2,1,0:T(8,128)(2,1)S(1)} %get-tuple-element.35), channel_id=1, source_target_pairs={{0,4},{4,0},{8,12},{12,8},{16,20},{20,16},{24,28},{28,24},{32,36},... | collective-permute-start | bytes 393224 | tf_op jit(solution)/shard_map/ppermute | solution.py:343
  5.1 1.2 slice_bitcast_fusion.1
  6.4 1.3 %collective-permute-start.6 = (bf16[448,128]{1,0:T(8,128)(2,1)S(1)}, bf16[448,128]{1,0:T(8,128)(2,1)S(1)}, u32[]{:S(2)}, u32[]{:S(2)}) collective-permute-start(bf16[448,128]{1,0:T(8,128)(2,1)S(1)} %bitcast.55), channel_id=1, source_target_pairs={{0,128},{64,192},{128,0},{192,64},{1,129},{65,193},{129,1},{193,65... | collective-permute-start | bytes 344072 | tf_op jit(solution)/shard_map/ppermute | solution.py:370
  7.8 0.9 collective-permute-start.5
  8.7 1.3 %collective-permute-start.2 = (bf16[14,64,128]{2,1,0:T(8,128)(2,1)S(1)}, bf16[14,64,128]{2,1,0:T(8,128)(2,1)S(1)}, u32[]{:S(2)}, u32[]{:S(2)}) collective-permute-start(bf16[14,64,128]{2,1,0:T(8,128)(2,1)S(1)} %slice.58), channel_id=1, source_target_pairs={{8,0},{12,4},{16,8},{20,12},{24,16},{28,20},{32,24},{36,28},{40,32... | collective-permute-start | bytes 688136 | tf_op jit(solution)/shard_map/ppermute | solution.py:352
  10.0 2.7 %collective-permute-done.6.half = bf16[448,128]{1,0:T(8,128)(2,1)S(1)} collective-permute-done((bf16[448,128]{1,0:T(8,128)(2,1)S(1)}, bf16[448,128]{1,0:T(8,128)(2,1)S(1)}, u32[]{:S(2)}, u32[]{:S(2)}) %collective-permute-start.6) | collective-permute-done | bytes 114720 | tf_op jit(solution)/shard_map/ppermute | solution.py:370
  12.7 1.4 %collective-permute-done.5.near = bf16[864,128]{1,0:T(8,128)(2,1)S(1)} collective-permute-done((bf16[864,128]{1,0:T(8,128)(2,1)S(1)}, bf16[864,128]{1,0:T(8,128)(2,1)S(1)}, u32[]{:S(2)}, u32[]{:S(2)}) %collective-permute-start.5) | collective-permute-done | bytes 221216 | tf_op jit(solution)/shard_map/ppermute | solution.py:361
  14.1 1.9 %collective-permute-start.7 = (bf16[1312,128]{1,0:T(8,128)(2,1)S(1)}, bf16[1312,128]{1,0:T(8,128)(2,1)S(1)}, u32[]{:S(2)}, u32[]{:S(2)}) collective-permute-start(bf16[1312,128]{1,0:T(8,128)(2,1)S(1)} %pad_maximum_fusion), channel_id=1, source_target_pairs={{0,4},{4,0},{8,12},{12,8},{16,20},{20,16},{24,28},{28,24},{32,36},... | collective-permute-start | bytes 1007624 | tf_op jit(solution)/shard_map/ppermute | solution.py:375
  16.0 3.0 %collective-permute-start.1 = (bf16[14,64,128]{2,1,0:T(8,128)(2,1)S(1)}, bf16[14,64,128]{2,1,0:T(8,128)(2,1)S(1)}, u32[]{:S(2)}, u32[]{:S(2)}) collective-permute-start(bf16[14,64,128]{2,1,0:T(8,128)(2,1)S(1)} %pad_maximum_fusion.1), channel_id=1, source_target_pairs={{0,8},{4,12},{8,16},{12,20},{16,24},{20,28},{24,32},{28,36},{32,40... | collective-permute-start | bytes 688136 | tf_op jit(solution)/shard_map/ppermute | solution.py:352
  19.0 1.3 %collective-permute-start.4 = (bf16[8,64,128]{2,1,0:T(8,128)(2,1)S(1)}, bf16[8,64,128]{2,1,0:T(8,128)(2,1)S(1)}, u32[]{:S(2)}, u32[]{:S(2)}) collective-permute-start(bf16[8,64,128]{2,1,0:T(8,128)(2,1)S(1)} %slice_bitcast_fusion), channel_id=1, source_target_pairs={{16,0},{20,4},{24,8},{28,12},{32,16},{36,20},{40,24},{44,28},{48,3... | collective-permute-start | bytes 393224 | tf_op jit(solution)/shard_map/ppermute | solution.py:352
  20.3 5.5 %collective-permute-start.3 = (bf16[8,64,128]{2,1,0:T(8,128)(2,1)S(1)}, bf16[8,64,128]{2,1,0:T(8,128)(2,1)S(1)}, u32[]{:S(2)}, u32[]{:S(2)}) collective-permute-start(bf16[8,64,128]{2,1,0:T(8,128)(2,1)S(1)} %slice_bitcast_fusion), channel_id=1, source_target_pairs={{0,16},{4,20},{8,24},{12,28},{16,32},{20,36},{24,40},{28,44},{32,4... | collective-permute-start | bytes 393224 | tf_op jit(solution)/shard_map/ppermute | solution.py:352
  27.3 5.2 %weight_blocks.1 = (bf16[12,128,768]{2,1,0:T(8,128)(2,1)}, bf16[12,128,768]{2,1,0:T(8,128)(2,1)}) custom-call(s32[3]{0:T(128)} %pad_add_fusion.where_ref, bf16[864,128]{1,0:T(8,128)(2,1)} %copy-done.9, bf16[864,128]{1,0:T(8,128)(2,1)} %copy-done.10, bf16[448,128]{1,0:T(8,128)(2,1)} %copy-done.11, bf16[1312,128]{1,0:T(8,128)(2,1)} %copy-done.12), custom_call_target="tpu_custom_call" | custom-call | tf_op jit(solution)/shard_map/weight_blocks/pallas_call | solution.py:376
  33.3 17.3 %first_part.1 = (bf16[4,64,128]{2,1,0:T(8,128)(2,1)}, bf16[4,64,128]{2,1,0:T(8,128)(2,1)}, bf16[8,64,128]{2,1,0:T(8,128)(2,1)}, bf16[8,64,128]{2,1,0:T(8,128)(2,...) custom-call(s32[3]{0:T(128)} %pad_add_fusion.where_ref, ...), custom_call_target="tpu_custom_call" | custom-call | tf_op jit(solution)/shard_map/first_part/pallas_call | solution.py:284
  50.6 1.0 fusion.2
  51.6 1.3 %collective-permute-start.10 = (bf16[6,64,128]{2,1,0:T(8,128)(2,1)S(1)}, bf16[6,64,128]{2,1,0:T(8,128)(2,1)S(1)}, u32[]{:S(2)}, u32[]{:S(2)}) collective-permute-start(bf16[6,64,128]{2,1,0:T(8,128)(2,1)S(1)} %get-tuple-element.38), channel_id=1, source_target_pairs={{8,0},{12,4},{16,8},{20,12},{24,16},{28,20},{32,24},{36,28},{40,32... | collective-permute-start | bytes 294920 | tf_op jit(solution)/shard_map/ppermute | solution.py:352
  52.9 5.4 %collective-permute-start.9 = (bf16[6,64,128]{2,1,0:T(8,128)(2,1)S(1)}, bf16[6,64,128]{2,1,0:T(8,128)(2,1)S(1)}, u32[]{:S(2)}, u32[]{:S(2)}) collective-permute-start(bf16[6,64,128]{2,1,0:T(8,128)(2,1)S(1)} %get-tuple-element.39), channel_id=1, source_target_pairs={{0,8},{4,12},{8,16},{12,20},{16,24},{20,28},{24,32},{28,36},{32,40... | collective-permute-start | bytes 294920 | tf_op jit(solution)/shard_map/ppermute | solution.py:352
  59.0 0.9 collective-permute-done.9.left_ref
  59.9 1.7 %copy-done.1 = f32[2,2,20,64,128]{4,3,2,1,0:T(8,128)S(1)} copy-done((f32[2,2,20,64,128]{4,3,2,1,0:T(8,128)S(1)}, f32[2,2,20,64,128]{4,3,2,1,0:T(8,128)}, u32[]{:S(2)}) %copy-start.1) | copy-done | bytes 2621464
  61.6 0.9 copy-done.2
  62.5 1.0 copy-done.3
  63.6 0.9 copy-done.4
  64.5 0.9 copy-done.5
  65.4 4.8 %second_part.1 = (bf16[4,64,128]{2,1,0:T(8,128)(2,1)S(1)}, bf16[4,64,128]{2,1,0:T(8,128)(2,1)S(1)}, bf16[1024,128]{1,0:T(8,128)(2,1)}) custom-call(s32[3]{0:T(128)S(1)} %copy-done.6, bf16[8,64,128]{2,1,0:T(8,128)(2,1)S(1)} %copy-done.2, bf16[6,64,128]{2,1,0:T(8,128)(2,1)S(1)} %collective-permute-done.9.left_ref, ...), custom_call_target="tpu_custom_call" | custom-call | tf_op jit(solution)/shard_map/second_part/pallas_call | solution.py:313
  70.2 15.5 %all-to-all-start = ((bf16[64,16,128]{2,1,0:T(8,128)(2,1)}), bf16[64,16,128]{2,1,0:T(8,128)(2,1)S(1)}, u32[]{:S(2)}, u32[]{:S(2)}) async-start(bf16[64,16,128]{2,1,0:T(8,128)(2,1)} %bitcast.24), calls=%async_computation | async-start | bytes 524288 | tf_op jit(solution)/shard_map/all_to_all | solution.py:401
  86.3 11.4 %all-to-all-done = bf16[64,16,128]{2,1,0:T(8,128)(2,1)S(1)} async-done(((bf16[64,16,128]{2,1,0:T(8,128)(2,1)}), bf16[64,16,128]{2,1,0:T(8,128)(2,1)S(1)}, u32[]{:S(2)}, u32[]{:S(2)}) %all-to-all-start) | async-done | bytes 262176 | tf_op jit(solution)/shard_map/all_to_all | solution.py:401
  97.9 0.7 broadcast_in_dim.14
  98.6 6.0 %all-to-all-start.1 = ((bf16[64,16,128]{2,1,0:T(8,128)(2,1)}), bf16[64,16,128]{2,1,0:T(8,128)(2,1)S(1)}, u32[]{:S(2)}, u32[]{:S(2)}) async-start(bf16[64,16,128]{2,1,0:T(8,128)(2,1)} %broadcast_in_dim.14), calls=%async_computation.1 | async-start | bytes 524288 | tf_op jit(solution)/shard_map/all_to_all | solution.py:403
  105.2 0.8 copy.10
  106.2 0.8 copy.11
  106.9 9.7 %all-to-all-done.1 = bf16[64,16,128]{2,1,0:T(8,128)(2,1)S(1)} async-done(((bf16[64,16,128]{2,1,0:T(8,128)(2,1)}), bf16[64,16,128]{2,1,0:T(8,128)(2,1)S(1)}, u32[]{:S(2)}, u32[]{:S(2)}) %all-to-all-start.1) | async-done | bytes 262176 | tf_op jit(solution)/shard_map/all_to_all | solution.py:403
  117.3 2.0 %unpack.1 = f32[1,3,3,3,64,64]{5,4,3,2,1,0:T(8,128)} custom-call(bf16[1024,128]{1,0:T(8,128)(2,1)} %bitcast.51), custom_call_target="tpu_custom_call" | custom-call | tf_op jit(solution)/shard_map/unpack/pallas_call | solution.py:406
  (60 shorter events, 5.4 us)
Async XLA Ops:
  1.7 6.9 %collective-permute-start = (bf16[2,4,64,128]{3,2,1,0:T(8,128)(2,1)S(1)}, bf16[2,4,64,128]{3,2,1,0:T(8,128)(2,1)S(1)}, u32[]{:S(2)}, u32[]{:S(2)}) collective-permute-start(bf16[2,4,64,128]{3,2,1,0:T(8,128)(2,1)S(1)} %get-tuple-element.35), channel_id=1, source_target_pairs={{0,4},{4,0},{8,12},{12,8},{16,20},{20,16},{24,28},{28,24},{32,36},... | collective-permute-start | bytes 393224 | tf_op jit(solution)/shard_map/ppermute | solution.py:343
  6.4 6.4 %collective-permute-start.6 = (bf16[448,128]{1,0:T(8,128)(2,1)S(1)}, bf16[448,128]{1,0:T(8,128)(2,1)S(1)}, u32[]{:S(2)}, u32[]{:S(2)}) collective-permute-start(bf16[448,128]{1,0:T(8,128)(2,1)S(1)} %bitcast.55), channel_id=1, source_target_pairs={{0,128},{64,192},{128,0},{192,64},{1,129},{65,193},{129,1},{193,65... | collective-permute-start | bytes 344072 | tf_op jit(solution)/shard_map/ppermute | solution.py:370
  7.8 18.7 %copy-start.9 = (bf16[864,128]{1,0:T(8,128)(2,1)}, bf16[864,128]{1,0:T(8,128)(2,1)S(1)}, u32[]{:S(2)}) copy-start(bf16[864,128]{1,0:T(8,128)(2,1)S(1)} %pad_maximum_fusion.2.own) | copy-start | bytes 663556
  7.8 6.3 %collective-permute-start.5 = (bf16[864,128]{1,0:T(8,128)(2,1)S(1)}, bf16[864,128]{1,0:T(8,128)(2,1)S(1)}, u32[]{:S(2)}, u32[]{:S(2)}) collective-permute-start(bf16[864,128]{1,0:T(8,128)(2,1)S(1)} %pad_maximum_fusion.2.own), channel_id=1, source_target_pairs={{0,64},{4,196},{8,72},{12,204},{16,80},{20,212},{24,88},{28,220},{... | collective-permute-start | bytes 663560 | tf_op jit(solution)/shard_map/ppermute | solution.py:361
  8.7 23.9 %copy-start.7 = (bf16[2,8,64,128]{3,2,1,0:T(8,128)(2,1)}, bf16[2,8,64,128]{3,2,1,0:T(8,128)(2,1)S(1)}, u32[]{:S(2)}) copy-start(bf16[2,8,64,128]{3,2,1,0:T(8,128)(2,1)S(1)} %maximum_select_fusion) | copy-start | bytes 786436
  8.7 23.7 %collective-permute-start.2 = (bf16[14,64,128]{2,1,0:T(8,128)(2,1)S(1)}, bf16[14,64,128]{2,1,0:T(8,128)(2,1)S(1)}, u32[]{:S(2)}, u32[]{:S(2)}) collective-permute-start(bf16[14,64,128]{2,1,0:T(8,128)(2,1)S(1)} %slice.58), channel_id=1, source_target_pairs={{8,0},{12,4},{16,8},{20,12},{24,16},{28,20},{32,24},{36,28},{40,32... | collective-permute-start | bytes 688136 | tf_op jit(solution)/shard_map/ppermute | solution.py:352
  12.7 13.8 %copy-start.11 = (bf16[448,128]{1,0:T(8,128)(2,1)}, bf16[448,128]{1,0:T(8,128)(2,1)S(1)}, u32[]{:S(2)}) copy-start(bf16[448,128]{1,0:T(8,128)(2,1)S(1)} %collective-permute-done.6.half) | copy-start | bytes 344068
  14.1 12.4 %copy-start.10 = (bf16[864,128]{1,0:T(8,128)(2,1)}, bf16[864,128]{1,0:T(8,128)(2,1)S(1)}, u32[]{:S(2)}) copy-start(bf16[864,128]{1,0:T(8,128)(2,1)S(1)} %collective-permute-done.5.near) | copy-start | bytes 663556
  14.1 12.4 %collective-permute-start.7 = (bf16[1312,128]{1,0:T(8,128)(2,1)S(1)}, bf16[1312,128]{1,0:T(8,128)(2,1)S(1)}, u32[]{:S(2)}, u32[]{:S(2)}) collective-permute-start(bf16[1312,128]{1,0:T(8,128)(2,1)S(1)} %pad_maximum_fusion), channel_id=1, source_target_pairs={{0,4},{4,0},{8,12},{12,8},{16,20},{20,16},{24,28},{28,24},{32,36},... | collective-permute-start | bytes 1007624 | tf_op jit(solution)/shard_map/ppermute | solution.py:375
  16.0 16.5 %collective-permute-start.1 = (bf16[14,64,128]{2,1,0:T(8,128)(2,1)S(1)}, bf16[14,64,128]{2,1,0:T(8,128)(2,1)S(1)}, u32[]{:S(2)}, u32[]{:S(2)}) collective-permute-start(bf16[14,64,128]{2,1,0:T(8,128)(2,1)S(1)} %pad_maximum_fusion.1), channel_id=1, source_target_pairs={{0,8},{4,12},{8,16},{12,20},{16,24},{20,28},{24,32},{28,36},{32,40... | collective-permute-start | bytes 688136 | tf_op jit(solution)/shard_map/ppermute | solution.py:352
  19.0 13.4 %collective-permute-start.4 = (bf16[8,64,128]{2,1,0:T(8,128)(2,1)S(1)}, bf16[8,64,128]{2,1,0:T(8,128)(2,1)S(1)}, u32[]{:S(2)}, u32[]{:S(2)}) collective-permute-start(bf16[8,64,128]{2,1,0:T(8,128)(2,1)S(1)} %slice_bitcast_fusion), channel_id=1, source_target_pairs={{16,0},{20,4},{24,8},{28,12},{32,16},{36,20},{40,24},{44,28},{48,3... | collective-permute-start | bytes 393224 | tf_op jit(solution)/shard_map/ppermute | solution.py:352
  20.3 12.2 %collective-permute-start.3 = (bf16[8,64,128]{2,1,0:T(8,128)(2,1)S(1)}, bf16[8,64,128]{2,1,0:T(8,128)(2,1)S(1)}, u32[]{:S(2)}, u32[]{:S(2)}) collective-permute-start(bf16[8,64,128]{2,1,0:T(8,128)(2,1)S(1)} %slice_bitcast_fusion), channel_id=1, source_target_pairs={{0,16},{4,20},{8,24},{12,28},{16,32},{20,36},{24,40},{28,44},{32,4... | collective-permute-start | bytes 393224 | tf_op jit(solution)/shard_map/ppermute | solution.py:352
  26.5 0.7 copy-start.12
  32.5 0.7 copy-start.16
  32.5 0.7 copy-start.13
  32.5 0.8 copy-start.14
  33.3 26.6 %copy-start = (bf16[12,128,768]{2,1,0:T(8,128)(2,1)S(1)}, bf16[12,128,768]{2,1,0:T(8,128)(2,1)}, u32[]{:S(2)}) copy-start(bf16[12,128,768]{2,1,0:T(8,128)(2,1)} %get-tuple-element.16.wb_ref) | copy-start | bytes 7077892
  33.3 26.6 %copy-start.6 = (s32[3]{0:T(128)S(1)}, s32[3]{0:T(128)}, u32[]{:S(2)}) copy-start(s32[3]{0:T(128)} %pad_add_fusion.where_ref) | copy-start | bytes 40
  51.6 7.4 %collective-permute-start.10 = (bf16[6,64,128]{2,1,0:T(8,128)(2,1)S(1)}, bf16[6,64,128]{2,1,0:T(8,128)(2,1)S(1)}, u32[]{:S(2)}, u32[]{:S(2)}) collective-permute-start(bf16[6,64,128]{2,1,0:T(8,128)(2,1)S(1)} %get-tuple-element.38), channel_id=1, source_target_pairs={{8,0},{12,4},{16,8},{20,12},{24,16},{28,20},{32,24},{36,28},{40,32... | collective-permute-start | bytes 294920 | tf_op jit(solution)/shard_map/ppermute | solution.py:352
  52.9 7.0 %collective-permute-start.9 = (bf16[6,64,128]{2,1,0:T(8,128)(2,1)S(1)}, bf16[6,64,128]{2,1,0:T(8,128)(2,1)S(1)}, u32[]{:S(2)}, u32[]{:S(2)}) collective-permute-start(bf16[6,64,128]{2,1,0:T(8,128)(2,1)S(1)} %get-tuple-element.39), channel_id=1, source_target_pairs={{0,8},{4,12},{8,16},{12,20},{16,24},{20,28},{24,32},{28,36},{32,40... | collective-permute-start | bytes 294920 | tf_op jit(solution)/shard_map/ppermute | solution.py:352
  59.9 1.7 %copy-start.1 = (f32[2,2,20,64,128]{4,3,2,1,0:T(8,128)S(1)}, f32[2,2,20,64,128]{4,3,2,1,0:T(8,128)}, u32[]{:S(2)}) copy-start(f32[2,2,20,64,128]{4,3,2,1,0:T(8,128)} %get-tuple-element.20.pre_ref) | copy-start | bytes 7864324
  61.6 0.9 copy-start.2
  62.5 1.0 copy-start.3
  63.6 0.9 copy-start.4
  64.5 0.9 copy-start.5
  65.4 20.4 %copy-start.18 = (bf16[4,64,128]{2,1,0:T(8,128)(2,1)S(1)}, bf16[4,64,128]{2,1,0:T(8,128)(2,1)}, u32[]{:S(2)}) copy-start(bf16[4,64,128]{2,1,0:T(8,128)(2,1)} %get-tuple-element.18) | copy-start | bytes 196612
  65.4 39.2 %copy-start.17 = (bf16[4,64,128]{2,1,0:T(8,128)(2,1)S(1)}, bf16[4,64,128]{2,1,0:T(8,128)(2,1)}, u32[]{:S(2)}) copy-start(bf16[4,64,128]{2,1,0:T(8,128)(2,1)} %get-tuple-element.17) | copy-start | bytes 196612
  70.2 27.6 %all-to-all-start = ((bf16[64,16,128]{2,1,0:T(8,128)(2,1)}), bf16[64,16,128]{2,1,0:T(8,128)(2,1)S(1)}, u32[]{:S(2)}, u32[]{:S(2)}) async-start(bf16[64,16,128]{2,1,0:T(8,128)(2,1)} %bitcast.24), calls=%async_computation | async-start | bytes 524288 | tf_op jit(solution)/shard_map/all_to_all | solution.py:401
  85.8 18.8 %collective-permute-start.8 = (bf16[4,64,128]{2,1,0:T(8,128)(2,1)S(1)}, bf16[4,64,128]{2,1,0:T(8,128)(2,1)S(1)}, u32[]{:S(2)}, u32[]{:S(2)}) collective-permute-start(bf16[4,64,128]{2,1,0:T(8,128)(2,1)S(1)} %copy-done.18), channel_id=1, source_target_pairs={{0,4},{4,0},{8,12},{12,8},{16,20},{20,16},{24,28},{28,24},{32,36},... | collective-permute-start | bytes 196616 | tf_op jit(solution)/shard_map/ppermute | solution.py:390
  98.6 18.0 %all-to-all-start.1 = ((bf16[64,16,128]{2,1,0:T(8,128)(2,1)}), bf16[64,16,128]{2,1,0:T(8,128)(2,1)S(1)}, u32[]{:S(2)}, u32[]{:S(2)}) async-start(bf16[64,16,128]{2,1,0:T(8,128)(2,1)} %broadcast_in_dim.14), calls=%async_computation.1 | async-start | bytes 524288 | tf_op jit(solution)/shard_map/all_to_all | solution.py:403
  104.7 1.4 %collective-permute-start.11 = (bf16[4,64,128]{2,1,0:T(8,128)(2,1)S(1)}, bf16[4,64,128]{2,1,0:T(8,128)(2,1)S(1)}, u32[]{:S(2)}, u32[]{:S(2)}) collective-permute-start(bf16[4,64,128]{2,1,0:T(8,128)(2,1)S(1)} %get-tuple-element.25), channel_id=1, source_target_pairs={{0,4},{4,0},{8,12},{12,8},{16,20},{20,16},{24,28},{28,24},{32,36},... | collective-permute-start | bytes 196616 | tf_op jit(solution)/shard_map/ppermute | solution.py:394
  116.6 0.7 copy-start.8
  (1 other events, 0.7 us)

commit v3 on v1

--- a/solution.py
+++ b/solution.py
@@ -3,6 +3,7 @@
 from jax import lax
 from jax.experimental import pallas as pl
 from jax.experimental.pallas import tpu as pltpu
+from jax.sharding import Mesh
 from jax.sharding import PartitionSpec as P
 
 BF = jnp.bfloat16
@@ -28,7 +29,7 @@
     far[pl.ds(pl.multiple_of(416 * core, 32), 448), :] = half[...]
     far[pl.ds(pl.multiple_of(416 * (1 - core), 32), 448), :] = other[864:1312, :]
     for piece, hop in ((own, 0), (near, 1 + 2 * core), (other, 3 - 2 * core), (far, 2)):
-        section = lax.rem(where_ref[0] - hop + DEPTH, DEPTH)
+        section = lax.rem(where_ref[4] - hop + DEPTH, DEPTH)
         for layer in range(3):
             slot = section * 3 + layer
             for kw in range(3):
@@ -55,26 +56,27 @@
 
 def sections_kernel(
     where_ref,
-    im_c, im_l1, im_r1, im_l2, im_r2, im_l3, im_r3,
+    mine_c, mine_l1, mine_r1, mine_l2, mine_r2, mine_l3, mine_r3, other_c, other_1, other_23,
     wf_ref, wb_ref,
-    keep_ref, send_ref, wg_ref,
+    even_ref, odd_ref, wg_ref,
     h_ref, a1_ref, a2_ref, p1_ref, p2_ref, g_ref, gp1_ref, gp2_ref,
 ):
     mine = where_ref[0]
     first_row = where_ref[1]
     core = where_ref[2]
-    h_ref[0, 24:32] = im_c[0:8]
-    h_ref[0, 16:24] = im_l1[0:8]
-    h_ref[0, 32:40] = im_r1[0:8]
-    h_ref[0, 8:16] = im_l2[0:8]
-    h_ref[0, 40:48] = im_r2[0:8]
-    h_ref[0, 2:8] = im_l3[...]
-    h_ref[0, 48:54] = im_r3[...]
-    g_ref[DEPTH, 24:32] = im_c[8:16]
-    g_ref[DEPTH, 16:24] = im_l1[8:16]
-    g_ref[DEPTH, 32:40] = im_r1[8:16]
-    g_ref[DEPTH, 12:16] = im_l2[8:12]
-    g_ref[DEPTH, 40:44] = im_r2[8:12]
+    here, there = 4 * core, 4 * (1 - core)
+    mine_pieces = (mine_c, mine_l1, mine_r1, mine_l2, mine_r2, mine_l3, mine_r3)
+    for piece, base in zip(mine_pieces, (24, 16, 32, 8, 40, 0, 48)):
+        h_ref[0, pl.ds(base + here, 4)] = piece[0:4]
+        if 8 <= base <= 40:
+            g_ref[DEPTH, pl.ds(base + here, 4)] = piece[4:8]
+    for piece, at, base in (
+        (other_c, 0, 24), (other_1, 0, 16), (other_1, 8, 32),
+        (other_23, 0, 8), (other_23, 8, 40), (other_23, 16, 0), (other_23, 20, 48),
+    ):
+        h_ref[0, pl.ds(base + there, 4)] = piece[at:at + 4]
+        if 8 <= base <= 40:
+            g_ref[DEPTH, pl.ds(base + there, 4)] = piece[at + 4:at + 8]
 
     lane = lax.broadcasted_iota(jnp.int32, (128, WID), 1)
     not_first = lane > 0
@@ -203,12 +205,13 @@
     kernel_grad(1, a1_ref.at[mine], gp2_ref.at[mine])
     kernel_grad(0, h_ref.at[mine], gp1_ref.at[mine])
 
-    kept = OFF + 4 * core
-    sent = OFF + 4 * (1 - core)
-    keep_ref[0] = h_ref[mine + 1, pl.ds(kept, 4)]
-    keep_ref[1] = g_ref[mine, pl.ds(kept, 4)]
-    send_ref[0] = h_ref[mine + 1, pl.ds(sent, 4)]
-    send_ref[1] = g_ref[mine, pl.ds(sent, 4)]
+    side = where_ref[3]
+    kept = OFF + 4 * side
+    sent = OFF + 4 * (1 - side)
+    even_ref[0] = h_ref[mine + 1, pl.ds(kept, 4)]
+    even_ref[1] = g_ref[mine, pl.ds(kept, 4)]
+    odd_ref[0] = h_ref[mine + 1, pl.ds(sent, 4)]
+    odd_ref[1] = g_ref[mine, pl.ds(sent, 4)]
 
 
 def unpack_kernel(sum_ref, out_ref):
@@ -234,7 +237,7 @@
             jax.ShapeDtypeStruct((2, 4, C, WID), BF),
             jax.ShapeDtypeStruct((1024, 128), BF),
         ],
-        in_specs=[pl.BlockSpec(memory_space=pltpu.SMEM)] + vmem(9),
+        in_specs=[pl.BlockSpec(memory_space=pltpu.SMEM)] + vmem(12),
         out_specs=vmem(3),
         scratch_shapes=[
             pltpu.VMEM((DEPTH + 1,) + window, BF),
@@ -251,52 +254,50 @@
     )(where, *pieces, fwd, bwd)
 
 
+SECTION = ("pair", "side")
+BAND = ("z", "core")
+CHIPS = 8
+
+
 def on_device(images, weights, cotangent):
-    section = lax.axis_index("section")
-    band = lax.axis_index("band")
-    core = band % 2
-    where = jnp.stack([section, (band // 2) * OWN, core]).astype(jnp.int32)
-
-    field = jnp.stack([images, cotangent]).transpose(1, 0, 3, 2, 4)
-    mine = jnp.where(core == 0, field[0], field[1])
-    other = jnp.where(core == 0, field[1], field[0])
-    bands = lax.axis_size("band")
-    swapped = [(i, i ^ 1) for i in range(bands)]
-    got = lax.ppermute(other, "band", swapped)
-    center = jnp.where(
-        core == 0,
-        jnp.concatenate([mine, got], axis=1),
-        jnp.concatenate([got, mine], axis=1),
-    ).reshape(16, C, WID)
-
-    def chips_away(value, chips):
-        pairs = [(i, i + 2 * chips) for i in range(bands) if 0 <= i + 2 * chips < bands]
-        return lax.ppermute(value, "band", pairs)
-
-    left1 = chips_away(center, 1)
-    right1 = chips_away(center, -1)
-    left2 = chips_away(jnp.concatenate([center[0:8], center[12:16]]), 2)
-    right2 = chips_away(center[0:12], -2)
-    left3 = chips_away(center[2:8], 3)
-    right3 = chips_away(center[0:6], -3)
+    pair, side = lax.axis_index("pair"), lax.axis_index("side")
+    z, core = lax.axis_index("z"), lax.axis_index("core")
+    section = 2 * pair + side
+    where = jnp.stack([2 * pair + core, z * OWN, core, side, section]).astype(jnp.int32)
 
     raw = weights.reshape(27, 2, 32, C)
     raw = jnp.concatenate([raw[:, 0], raw[:, 1]], axis=-1).reshape(864, 128)
     near = lax.ppermute(
         raw,
-        ("section", "band"),
+        SECTION + ("core",),
         [
-            (s * bands + b, (s + 1 - 2 * (b % 2)) % DEPTH * bands + b)
+            (s * 2 + c, (s + 1 - 2 * c) % DEPTH * 2 + c)
             for s in range(DEPTH)
-            for b in range(bands)
+            for c in range(2)
         ],
     )
     half = lax.ppermute(
         jnp.where(core == 0, raw[:448], raw[416:]),
-        "section",
+        SECTION,
         [(s, (s + 2) % DEPTH) for s in range(DEPTH)],
     )
-    other_weights = lax.ppermute(jnp.concatenate([near, half]), "band", swapped)
+    field = jnp.where(side == 0, jnp.stack([images[0], cotangent[0]]), jnp.stack([images[1], cotangent[1]]))
+    center = field.transpose(0, 2, 1, 3).reshape(8, C, WID)
+    swapped = [(i, i ^ 1) for i in range(2 * CHIPS)]
+
+    def chips_away(value, chips):
+        pairs = [(i, i + chips) for i in range(CHIPS) if 0 <= i + chips < CHIPS]
+        return lax.ppermute(value, "z", pairs)
+
+    other_c = lax.ppermute(center, BAND, swapped)
+    center, other_c, raw = lax.optimization_barrier((center, other_c, raw))
+    left3, right3 = chips_away(center[0:4], 3), chips_away(center[0:4], -3)
+    left2, right2 = chips_away(center, 2), chips_away(center, -2)
+    left1, right1 = chips_away(center, 1), chips_away(center, -1)
+    other_1 = lax.ppermute(jnp.concatenate([left1, right1]), BAND, swapped)
+    other_23 = lax.ppermute(jnp.concatenate([left2, right2, left3, right3]), BAND, swapped)
+
+    other_weights = lax.ppermute(jnp.concatenate([near, half]), BAND, swapped)
     fwd, bwd = pl.pallas_call(
         weight_blocks_kernel,
         out_shape=[jax.ShapeDtypeStruct((12, 128, 768), BF)] * 2,
@@ -306,20 +307,29 @@
         name="weight_blocks",
     )(where, raw, near, half, other_weights)
 
-    keep, send, grads = sections_call(
-        where, (center, left1, right1, left2, right2, left3, right3), fwd, bwd
-    )
-
-    received = lax.ppermute(send, "band", swapped)
-    zero = jnp.where(core == 0, keep, received)
-    one = jnp.where(core == 0, received, keep)
+    even, odd, grads = sections_call(
+        where,
+        (center, left1, right1, left2, right2, left3, right3, other_c, other_1, other_23),
+        fwd,
+        bwd,
+    )
+
+    parts = lax.all_to_all(grads.reshape(64, 16, 128), ("rep", "side", "z"), 0, 0, tiled=True)
+    total = jnp.sum(parts.astype(F32), axis=0).astype(BF)
+    turned = [(2 * q + c, 2 * c + q) for q in range(2) for c in range(2)]
+    total = lax.ppermute(total, ("side", "core"), turned)
+    summed = lax.all_to_all(
+        jnp.broadcast_to(total[None], (64, 16, 128)), ("rep", "core", "z"), 0, 0, tiled=True
+    ).reshape(1024, 128)
+
+    even = lax.ppermute(even, ("side", "core"), turned)
+    odd = lax.ppermute(
+        odd, ("side", "core"), [(2 * q + c, 2 * c + 1 - q) for q in range(2) for c in range(2)]
+    )
+    zero = jnp.where(core == 0, even, odd)
+    one = jnp.where(core == 0, odd, even)
     both = jnp.stack([zero, one]).transpose(1, 0, 3, 2, 4)
 
-    parts = lax.all_to_all(grads.reshape(64, 16, 128), ("rep", "band"), 0, 0, tiled=True)
-    total = jnp.sum(parts.astype(F32), axis=0).astype(BF)
-    summed = lax.all_to_all(
-        jnp.broadcast_to(total[None], (64, 16, 128)), ("rep", "band"), 0, 0, tiled=True
-    ).reshape(1024, 128)
     weight_grads = pl.pallas_call(
         unpack_kernel,
         out_shape=jax.ShapeDtypeStruct((1, 3, 3, 3, C, C), F32),
@@ -331,16 +341,19 @@
 
 
 def solution(mesh):
+    finer = Mesh(
+        mesh.devices.reshape(2, 2, CHIPS, 2, mesh.devices.shape[2]), SECTION + BAND + ("rep",)
+    )
     in_specs = (
-        P("rep", None, "band", None),
-        P("section", None, None, None, None, None),
-        P("rep", None, "band", None),
+        P("rep", None, BAND, None),
+        P(SECTION, None, None, None, None, None),
+        P("rep", None, BAND, None),
     )
     out_specs = (
-        P("section", "rep", None, "band", None),
-        P("section", "rep", None, "band", None),
-        P("section", None, None, None, None, None),
+        P(SECTION, "rep", None, BAND, None),
+        P(SECTION, "rep", None, BAND, None),
+        P(SECTION, None, None, None, None, None),
     )
     return jax.shard_map(
-        on_device, mesh=mesh, in_specs=in_specs, out_specs=out_specs, check_vma=False
-    )
+        on_device, mesh=finer, in_specs=in_specs, out_specs=out_specs, check_vma=False
+    )

time: 110 us -> 116 us (1.055)
  starting transfers between devices: 46.4 us -> 49.6 us
  local copies, waits for them, and re-layouts: 6.05 us -> 7.35 us
  waiting for transfers between devices: 29.1 us -> 30.3 us
    ppermute x11 -> x15, starting transfers between devices: 26.5 us -> 39.7 us  [the longest x6 23.2 us: chips_away(): return lax.ppermute(value, 'z', pairs)]
    all_to_all x2, starting transfers between devices: 19.9 us -> 9.94 us  [the longest x1 5.14 us: on_device(): lax.all_to_all(grads.reshape(64, 16, 128), ('rep', 'side', 'z'), 0, 0, ti...]
    ppermute x11 -> x15, waiting for transfers between devices: 8.16 us -> 10.8 us  [the longest x6 9.45 us: chips_away(): return lax.ppermute(value, 'z', pairs)]
    all_to_all x2, waiting for transfers between devices: 20.9 us -> 19.6 us  [the longest x1 10.4 us: on_device(): lax.all_to_all(jnp.broadcast_to(total[None], (64, 16, 128)), ('rep', 'cor...]
    unnamed x26 -> x32, local copies, waits for them, and re-layouts: 3.06 us -> 3.71 us
  transfers between devices with their start and end apart: 13 -> 17, of which waited for: 4 -> 6; matrix products, arithmetic and copies ran while one was open for 5% -> 5% of each run, Pallas kernels for 5% -> 5%
where the time goes in v3:
time: 116 us; the launch traced here: 115 us
  starting transfers between devices  49.6 us (43%)
  waiting for transfers between devices  30.3 us (26%)
  Pallas kernels  25.2 us (22%)
  local copies, waits for them, and re-layouts  7.35 us (6%)
  other arithmetic  1.39 us (1%)
    ppermute x6, starting transfers between devices, chips_away(): return lax.ppermute(value, 'z', pairs)  23.2 us
    pallas_call x1, Pallas kernels, sections_call(): pl.pallas_call(sections_kernel, out_shape=[jax.ShapeDtypeStruct((2, 4, C,...  17.9 us
    all_to_all x1, waiting for transfers between devices, on_device(): lax.all_to_all(jnp.broadcast_to(total[None], (64, 16, 128)), ('rep', 'cor...  10.4 us
    ppermute x6, waiting for transfers between devices, chips_away(): return lax.ppermute(value, 'z', pairs)  9.45 us
    all_to_all x1, waiting for transfers between devices, on_device(): lax.all_to_all(grads.reshape(64, 16, 128), ('rep', 'side', 'z'), 0, 0, ti...  9.17 us
    pallas_call x1, Pallas kernels, on_device(): pl.pallas_call(weight_blocks_kernel, out_shape=[jax.ShapeDtypeStruct((12,...  5.24 us
    all_to_all x1, starting transfers between devices, on_device(): lax.all_to_all(grads.reshape(64, 16, 128), ('rep', 'side', 'z'), 0, 0, ti...  5.14 us
    all_to_all x1, starting transfers between devices, on_device(): lax.all_to_all(jnp.broadcast_to(total[None], (64, 16, 128)), ('rep', 'cor...  4.8 us
  transfers between devices with their start and end apart: 17, of which 6 were waited for; matrix products, arithmetic and copies ran while one was open for 5% of the time, Pallas kernels for 5%

profile of v3, /device:TPU:1, one launch (start us, length us, event | category | flops | bytes accessed | tf_op | source)
XLA Modules:
  0.0 114.9 jit_solution(13074624328394405709)
XLA Ops:
  0.6 1.0 fusion.4
  1.9 3.3 %collective-permute-start = (bf16[8,64,128]{2,1,0:T(8,128)(2,1)S(1)}, bf16[8,64,128]{2,1,0:T(8,128)(2,1)S(1)}, u32[]{:S(2)}, u32[]{:S(2)}) collective-permute-start(bf16[8,64,128]{2,1,0:T(8,128)(2,1)S(1)} %bitcast.33), channel_id=1, source_target_pairs={{0,4},{4,0},{8,12},{12,8},{16,20},{20,16},{24,28},{28,24},{32,36},... | collective-permute-start | bytes 393224 | tf_op jit(solution)/shard_map/ppermute | solution.py:292
  5.2 1.2 %slice_bitcast_fusion = (bf16[27,32,64]{2,1,0:T(8,128)(2,1)S(1)}, bf16[27,32,64]{2,1,0:T(8,128)(2,1)S(1)}, bf16[27,1,32,64]{3,2,1,0:T(8,128)(2,1)S(1)}, bf16[27,1,32,64]{3,2,1,0:T(8,128)(2,1)S(1)}) fusion(bf16[27,2,32,64]{3,2,1,0:T(8,128)(2,1)} %bitcast.40), kind=kLoop, calls=%fused_computation.14 | loop fusion | bytes 663552 | tf_op jit(solution)/shard_map/squeeze | solution.py:269
  6.5 3.2 %collective-permute-start.3 = (bf16[8,64,128]{2,1,0:T(8,128)(2,1)S(1)}, bf16[8,64,128]{2,1,0:T(8,128)(2,1)S(1)}, u32[]{:S(2)}, u32[]{:S(2)}) collective-permute-start(bf16[8,64,128]{2,1,0:T(8,128)(2,1)S(1)} %bitcast.34), channel_id=1, source_target_pairs={{0,16},{8,24},{16,32},{24,40},{32,48},{40,56},{1,17},{9,25},{17,33... | collective-permute-start | bytes 393224 | tf_op jit(solution)/shard_map/ppermute | solution.py:290
  9.7 1.3 %collective-permute-start.4 = (bf16[8,64,128]{2,1,0:T(8,128)(2,1)S(1)}, bf16[8,64,128]{2,1,0:T(8,128)(2,1)S(1)}, u32[]{:S(2)}, u32[]{:S(2)}) collective-permute-start(bf16[8,64,128]{2,1,0:T(8,128)(2,1)S(1)} %bitcast.35), channel_id=1, source_target_pairs={{16,0},{24,8},{32,16},{40,24},{48,32},{56,40},{17,1},{25,9},{33,17... | collective-permute-start | bytes 393224 | tf_op jit(solution)/shard_map/ppermute | solution.py:290
  11.0 2.8 %collective-permute-start.9 = (bf16[864,128]{1,0:T(8,128)(2,1)S(1)}, bf16[864,128]{1,0:T(8,128)(2,1)S(1)}, u32[]{:S(2)}, u32[]{:S(2)}) collective-permute-start(bf16[864,128]{1,0:T(8,128)(2,1)S(1)} %pad_maximum_fusion.3.own), channel_id=1, source_target_pairs={{0,64},{4,196},{64,128},{68,4},{128,192},{132,68},{192,0},{196,132... | collective-permute-start | bytes 663560 | tf_op jit(solution)/shard_map/ppermute | solution.py:270
  13.8 7.2 %collective-permute-start.5 = (bf16[4,64,128]{2,1,0:T(8,128)(2,1)S(1)}, bf16[4,64,128]{2,1,0:T(8,128)(2,1)S(1)}, u32[]{:S(2)}, u32[]{:S(2)}) collective-permute-start(bf16[4,64,128]{2,1,0:T(8,128)(2,1)S(1)} %slice.42), channel_id=1, source_target_pairs={{0,24},{8,32},{16,40},{24,48},{32,56},{1,25},{9,33},{17,41},{25,49... | collective-permute-start | bytes 196616 | tf_op jit(solution)/shard_map/ppermute | solution.py:290
  21.0 1.3 %collective-permute-start.6 = (bf16[4,64,128]{2,1,0:T(8,128)(2,1)S(1)}, bf16[4,64,128]{2,1,0:T(8,128)(2,1)S(1)}, u32[]{:S(2)}, u32[]{:S(2)}) collective-permute-start(bf16[4,64,128]{2,1,0:T(8,128)(2,1)S(1)} %slice.42), channel_id=1, source_target_pairs={{24,0},{32,8},{40,16},{48,24},{56,32},{25,1},{33,9},{41,17},{49,25... | collective-permute-start | bytes 196616 | tf_op jit(solution)/shard_map/ppermute | solution.py:290
  22.9 5.8 %collective-permute-done.6.mine_r3 = bf16[4,64,128]{2,1,0:T(8,128)(2,1)S(1)} collective-permute-done((bf16[4,64,128]{2,1,0:T(8,128)(2,1)S(1)}, bf16[4,64,128]{2,1,0:T(8,128)(2,1)S(1)}, u32[]{:S(2)}, u32[]{:S(2)}) %collective-permute-start.6) | collective-permute-done | bytes 65568 | tf_op jit(solution)/shard_map/ppermute | solution.py:290
  28.7 9.0 %collective-permute-start.1 = (bf16[8,64,128]{2,1,0:T(8,128)(2,1)S(1)}, bf16[8,64,128]{2,1,0:T(8,128)(2,1)S(1)}, u32[]{:S(2)}, u32[]{:S(2)}) collective-permute-start(bf16[8,64,128]{2,1,0:T(8,128)(2,1)S(1)} %bitcast.37), channel_id=1, source_target_pairs={{0,8},{8,16},{16,24},{24,32},{32,40},{40,48},{48,56},{1,9},{9,17},... | collective-permute-start | bytes 393224 | tf_op jit(solution)/shard_map/ppermute | solution.py:290
  37.7 1.3 %collective-permute-start.2 = (bf16[8,64,128]{2,1,0:T(8,128)(2,1)S(1)}, bf16[8,64,128]{2,1,0:T(8,128)(2,1)S(1)}, u32[]{:S(2)}, u32[]{:S(2)}) collective-permute-start(bf16[8,64,128]{2,1,0:T(8,128)(2,1)S(1)} %bitcast.38), channel_id=1, source_target_pairs={{8,0},{16,8},{24,16},{32,24},{40,32},{48,40},{56,48},{9,1},{17,9},... | collective-permute-start | bytes 393224 | tf_op jit(solution)/shard_map/ppermute | solution.py:290
  39.1 0.9 collective-permute-start.8
  40.2 3.6 %collective-permute-done.2.mine_r1 = bf16[8,64,128]{2,1,0:T(8,128)(2,1)S(1)} collective-permute-done((bf16[8,64,128]{2,1,0:T(8,128)(2,1)S(1)}, bf16[8,64,128]{2,1,0:T(8,128)(2,1)S(1)}, u32[]{:S(2)}, u32[]{:S(2)}) %collective-permute-start.2) | collective-permute-done | bytes 131104 | tf_op jit(solution)/shard_map/ppermute | solution.py:290
  43.8 0.7 pad_maximum_fusion.2
  44.5 1.7 %collective-permute-start.7 = (bf16[16,64,128]{2,1,0:T(8,128)(2,1)}, bf16[16,64,128]{2,1,0:T(8,128)(2,1)S(1)}, u32[]{:S(2)}, u32[]{:S(2)}) collective-permute-start(bf16[16,64,128]{2,1,0:T(8,128)(2,1)} %pad_maximum_fusion.2), channel_id=1, source_target_pairs={{0,4},{4,0},{8,12},{12,8},{16,20},{20,16},{24,28},{28,24},{32,36},... | collective-permute-start | bytes 786440 | tf_op jit(solution)/shard_map/ppermute | solution.py:297
  46.3 0.7 stack.38.where_ref
  47.0 0.7 copy-done.10
  47.7 5.2 %weight_blocks.1 = (bf16[12,128,768]{2,1,0:T(8,128)(2,1)}, bf16[12,128,768]{2,1,0:T(8,128)(2,1)}) custom-call(s32[5]{0:T(128)} %stack.38.where_ref, bf16[864,128]{1,0:T(8,128)(2,1)} %copy-done.1, bf16[864,128]{1,0:T(8,128)(2,1)} %copy-done.2, bf16[448,128]{1,0:T(8,128)(2,1)} %copy-done.8, bf16[1312,128]{1,0:T(8,128)(2,1)} %copy-done.10), custom_call_target="tpu_custom_call" | custom-call | tf_op jit(solution)/shard_map/weight_blocks/pallas_call | solution.py:301
  53.0 0.6 copy-done.13
  53.8 17.9 %sections.1 = (bf16[2,4,64,128]{3,2,1,0:T(8,128)(2,1)}, bf16[2,4,64,128]{3,2,1,0:T(8,128)(2,1)}, bf16[1024,128]{1,0:T(8,128)(2,1)}) custom-call(s32[5]{0:T(128)} %stack.38.where_ref, bf16[8,64,128]{2,1,0:T(8,128)(2,1)} %bitcast.39, bf16[8,64,128]{2,1,0:T(8,128)(2,1)} %copy-done.6, bf16[8,64,128]{2,1,0:T(8,128)(2,1)} %copy-done.7, ...), custom_call_target="tpu_custom_call" | custom-call | tf_op jit(solution)/shard_map/sections/pallas_call | solution.py:233
  71.7 5.1 %all-to-all-start = ((bf16[64,16,128]{2,1,0:T(8,128)(2,1)}), bf16[64,16,128]{2,1,0:T(8,128)(2,1)S(1)}, u32[]{:S(2)}, u32[]{:S(2)}) async-start(bf16[64,16,128]{2,1,0:T(8,128)(2,1)} %bitcast.41), calls=%async_computation | async-start | bytes 524288 | tf_op jit(solution)/shard_map/all_to_all | solution.py:317
  76.8 3.4 %collective-permute-start.12 = (bf16[2,4,64,128]{3,2,1,0:T(8,128)(2,1)}, bf16[2,4,64,128]{3,2,1,0:T(8,128)(2,1)S(1)}, u32[]{:S(2)}, u32[]{:S(2)}) collective-permute-start(bf16[2,4,64,128]{3,2,1,0:T(8,128)(2,1)} %get-tuple-element.16), channel_id=1, source_target_pairs={{0,0},{4,64},{64,4},{68,68},{1,1},{5,65},{65,5},{69,69},{2,2},{6,6... | collective-permute-start | bytes 393224 | tf_op jit(solution)/shard_map/ppermute | solution.py:325
  80.3 9.2 %all-to-all-done = bf16[64,16,128]{2,1,0:T(8,128)(2,1)S(1)} async-done(((bf16[64,16,128]{2,1,0:T(8,128)(2,1)}), bf16[64,16,128]{2,1,0:T(8,128)(2,1)S(1)}, u32[]{:S(2)}, u32[]{:S(2)}) %all-to-all-start) | async-done | bytes 262176 | tf_op jit(solution)/shard_map/all_to_all | solution.py:317
  89.6 3.8 %collective-permute-start.14 = (bf16[16,128]{1,0:T(8,128)(2,1)S(1)}, bf16[16,128]{1,0:T(8,128)(2,1)S(1)}, u32[]{:S(2)}, u32[]{:S(2)}) collective-permute-start(bf16[16,128]{1,0:T(8,128)(2,1)S(1)} %reduce_sum.12), channel_id=1, source_target_pairs={{0,0},{4,64},{64,4},{68,68},{1,1},{5,65},{65,5},{69,69},{2,2},{6,6... | collective-permute-start | bytes 12296 | tf_op jit(solution)/shard_map/ppermute | solution.py:320
  93.3 1.3 %collective-permute-done.14 = bf16[16,128]{1,0:T(8,128)(2,1)S(1)} collective-permute-done((bf16[16,128]{1,0:T(8,128)(2,1)S(1)}, bf16[16,128]{1,0:T(8,128)(2,1)S(1)}, u32[]{:S(2)}, u32[]{:S(2)}) %collective-permute-start.14) | collective-permute-done | bytes 4128 | tf_op jit(solution)/shard_map/ppermute | solution.py:320
  94.6 0.7 broadcast_in_dim.2
  95.3 4.8 %all-to-all-start.1 = ((bf16[64,16,128]{2,1,0:T(8,128)(2,1)}), bf16[64,16,128]{2,1,0:T(8,128)(2,1)S(1)}, u32[]{:S(2)}, u32[]{:S(2)}) async-start(bf16[64,16,128]{2,1,0:T(8,128)(2,1)} %broadcast_in_dim.2), calls=%async_computation.1 | async-start | bytes 524288 | tf_op jit(solution)/shard_map/all_to_all | solution.py:321
  100.3 0.8 copy.10
  101.0 0.8 copy.9
  101.8 10.4 %all-to-all-done.1 = bf16[64,16,128]{2,1,0:T(8,128)(2,1)S(1)} async-done(((bf16[64,16,128]{2,1,0:T(8,128)(2,1)}), bf16[64,16,128]{2,1,0:T(8,128)(2,1)S(1)}, u32[]{:S(2)}, u32[]{:S(2)}) %all-to-all-start.1) | async-done | bytes 262176 | tf_op jit(solution)/shard_map/all_to_all | solution.py:321
  112.2 0.7 copy-done
  112.9 2.0 %unpack.1 = f32[1,3,3,3,64,64]{5,4,3,2,1,0:T(8,128)} custom-call(bf16[1024,128]{1,0:T(8,128)(2,1)} %bitcast.30), custom_call_target="tpu_custom_call" | custom-call | tf_op jit(solution)/shard_map/unpack/pallas_call | solution.py:333
  (53 shorter events, 1.6 us)
Async XLA Ops:
  1.9 45.1 %copy-start.3 = (bf16[2,4,64,128]{3,2,1,0:T(8,128)(2,1)}, bf16[2,4,64,128]{3,2,1,0:T(8,128)(2,1)S(1)}, u32[]{:S(2)}) copy-start(bf16[2,4,64,128]{3,2,1,0:T(8,128)(2,1)S(1)} %copy.6) | copy-start | bytes 393220
  1.9 4.6 %collective-permute-start = (bf16[8,64,128]{2,1,0:T(8,128)(2,1)S(1)}, bf16[8,64,128]{2,1,0:T(8,128)(2,1)S(1)}, u32[]{:S(2)}, u32[]{:S(2)}) collective-permute-start(bf16[8,64,128]{2,1,0:T(8,128)(2,1)S(1)} %bitcast.33), channel_id=1, source_target_pairs={{0,4},{4,0},{8,12},{12,8},{16,20},{20,16},{24,28},{28,24},{32,36},... | collective-permute-start | bytes 393224 | tf_op jit(solution)/shard_map/ppermute | solution.py:292
  6.5 40.4 %copy-start.1 = (bf16[864,128]{1,0:T(8,128)(2,1)}, bf16[864,128]{1,0:T(8,128)(2,1)S(1)}, u32[]{:S(2)}) copy-start(bf16[864,128]{1,0:T(8,128)(2,1)S(1)} %pad_maximum_fusion.3.own) | copy-start | bytes 663556
  6.5 46.4 %copy-start.14 = (bf16[8,64,128]{2,1,0:T(8,128)(2,1)}, bf16[8,64,128]{2,1,0:T(8,128)(2,1)S(1)}, u32[]{:S(2)}) copy-start(bf16[8,64,128]{2,1,0:T(8,128)(2,1)S(1)} %collective-permute-done.other_c) | copy-start | bytes 393220
  6.5 31.1 %collective-permute-start.3 = (bf16[8,64,128]{2,1,0:T(8,128)(2,1)S(1)}, bf16[8,64,128]{2,1,0:T(8,128)(2,1)S(1)}, u32[]{:S(2)}, u32[]{:S(2)}) collective-permute-start(bf16[8,64,128]{2,1,0:T(8,128)(2,1)S(1)} %bitcast.34), channel_id=1, source_target_pairs={{0,16},{8,24},{16,32},{24,40},{32,48},{40,56},{1,17},{9,25},{17,33... | collective-permute-start | bytes 393224 | tf_op jit(solution)/shard_map/ppermute | solution.py:290
  9.7 29.3 %collective-permute-start.4 = (bf16[8,64,128]{2,1,0:T(8,128)(2,1)S(1)}, bf16[8,64,128]{2,1,0:T(8,128)(2,1)S(1)}, u32[]{:S(2)}, u32[]{:S(2)}) collective-permute-start(bf16[8,64,128]{2,1,0:T(8,128)(2,1)S(1)} %bitcast.35), channel_id=1, source_target_pairs={{16,0},{24,8},{32,16},{40,24},{48,32},{56,40},{17,1},{25,9},{33,17... | collective-permute-start | bytes 393224 | tf_op jit(solution)/shard_map/ppermute | solution.py:290
  11.0 29.0 %collective-permute-start.9 = (bf16[864,128]{1,0:T(8,128)(2,1)S(1)}, bf16[864,128]{1,0:T(8,128)(2,1)S(1)}, u32[]{:S(2)}, u32[]{:S(2)}) collective-permute-start(bf16[864,128]{1,0:T(8,128)(2,1)S(1)} %pad_maximum_fusion.3.own), channel_id=1, source_target_pairs={{0,64},{4,196},{64,128},{68,4},{128,192},{132,68},{192,0},{196,132... | collective-permute-start | bytes 663560 | tf_op jit(solution)/shard_map/ppermute | solution.py:270
  13.8 8.7 %collective-permute-start.5 = (bf16[4,64,128]{2,1,0:T(8,128)(2,1)S(1)}, bf16[4,64,128]{2,1,0:T(8,128)(2,1)S(1)}, u32[]{:S(2)}, u32[]{:S(2)}) collective-permute-start(bf16[4,64,128]{2,1,0:T(8,128)(2,1)S(1)} %slice.42), channel_id=1, source_target_pairs={{0,24},{8,32},{16,40},{24,48},{32,56},{1,25},{9,33},{17,41},{25,49... | collective-permute-start | bytes 196616 | tf_op jit(solution)/shard_map/ppermute | solution.py:290
  21.0 7.7 %collective-permute-start.6 = (bf16[4,64,128]{2,1,0:T(8,128)(2,1)S(1)}, bf16[4,64,128]{2,1,0:T(8,128)(2,1)S(1)}, u32[]{:S(2)}, u32[]{:S(2)}) collective-permute-start(bf16[4,64,128]{2,1,0:T(8,128)(2,1)S(1)} %slice.42), channel_id=1, source_target_pairs={{24,0},{32,8},{40,16},{48,24},{56,32},{25,1},{33,9},{41,17},{49,25... | collective-permute-start | bytes 196616 | tf_op jit(solution)/shard_map/ppermute | solution.py:290
  22.5 30.4 %copy-start.11 = (bf16[4,64,128]{2,1,0:T(8,128)(2,1)}, bf16[4,64,128]{2,1,0:T(8,128)(2,1)S(1)}, u32[]{:S(2)}) copy-start(bf16[4,64,128]{2,1,0:T(8,128)(2,1)S(1)} %collective-permute-done.5.mine_l3) | copy-start | bytes 196612
  22.5 17.5 %collective-permute-start.10 = (bf16[448,128]{1,0:T(8,128)(2,1)S(1)}, bf16[448,128]{1,0:T(8,128)(2,1)S(1)}, u32[]{:S(2)}, u32[]{:S(2)}) collective-permute-start(bf16[448,128]{1,0:T(8,128)(2,1)S(1)} %bitcast.42), channel_id=1, source_target_pairs={{0,128},{64,192},{128,0},{192,64},{1,129},{65,193},{129,1},{193,65... | collective-permute-start | bytes 344072 | tf_op jit(solution)/shard_map/ppermute | solution.py:279
  28.7 24.3 %copy-start.12 = (bf16[4,64,128]{2,1,0:T(8,128)(2,1)}, bf16[4,64,128]{2,1,0:T(8,128)(2,1)S(1)}, u32[]{:S(2)}) copy-start(bf16[4,64,128]{2,1,0:T(8,128)(2,1)S(1)} %collective-permute-done.6.mine_r3) | copy-start | bytes 196612
  28.7 11.5 %collective-permute-start.1 = (bf16[8,64,128]{2,1,0:T(8,128)(2,1)S(1)}, bf16[8,64,128]{2,1,0:T(8,128)(2,1)S(1)}, u32[]{:S(2)}, u32[]{:S(2)}) collective-permute-start(bf16[8,64,128]{2,1,0:T(8,128)(2,1)S(1)} %bitcast.37), channel_id=1, source_target_pairs={{0,8},{8,16},{16,24},{24,32},{32,40},{40,48},{48,56},{1,9},{9,17},... | collective-permute-start | bytes 393224 | tf_op jit(solution)/shard_map/ppermute | solution.py:290
  37.7 15.3 %copy-start.4 = (bf16[8,64,128]{2,1,0:T(8,128)(2,1)}, bf16[8,64,128]{2,1,0:T(8,128)(2,1)S(1)}, u32[]{:S(2)}) copy-start(bf16[8,64,128]{2,1,0:T(8,128)(2,1)S(1)} %collective-permute-done.3.mine_l2) | copy-start | bytes 393220
  37.7 6.1 %collective-permute-start.2 = (bf16[8,64,128]{2,1,0:T(8,128)(2,1)S(1)}, bf16[8,64,128]{2,1,0:T(8,128)(2,1)S(1)}, u32[]{:S(2)}, u32[]{:S(2)}) collective-permute-start(bf16[8,64,128]{2,1,0:T(8,128)(2,1)S(1)} %bitcast.38), channel_id=1, source_target_pairs={{8,0},{16,8},{24,16},{32,24},{40,32},{48,40},{56,48},{9,1},{17,9},... | collective-permute-start | bytes 393224 | tf_op jit(solution)/shard_map/ppermute | solution.py:290
  39.0 14.0 %copy-start.5 = (bf16[8,64,128]{2,1,0:T(8,128)(2,1)}, bf16[8,64,128]{2,1,0:T(8,128)(2,1)S(1)}, u32[]{:S(2)}) copy-start(bf16[8,64,128]{2,1,0:T(8,128)(2,1)S(1)} %collective-permute-done.4.mine_r2) | copy-start | bytes 393220
  39.1 13.8 %collective-permute-start.8 = (bf16[24,64,128]{2,1,0:T(8,128)(2,1)S(1)}, bf16[24,64,128]{2,1,0:T(8,128)(2,1)S(1)}, u32[]{:S(2)}, u32[]{:S(2)}) collective-permute-start(bf16[24,64,128]{2,1,0:T(8,128)(2,1)S(1)} %pad_maximum_fusion), channel_id=1, source_target_pairs={{0,4},{4,0},{8,12},{12,8},{16,20},{20,16},{24,28},{28,24},{32,36},... | collective-permute-start | bytes 1179656 | tf_op jit(solution)/shard_map/ppermute | solution.py:298
  40.0 6.9 %copy-start.8 = (bf16[448,128]{1,0:T(8,128)(2,1)}, bf16[448,128]{1,0:T(8,128)(2,1)S(1)}, u32[]{:S(2)}) copy-start(bf16[448,128]{1,0:T(8,128)(2,1)S(1)} %collective-permute-done.10.half) | copy-start | bytes 344068
  40.0 6.9 %copy-start.2 = (bf16[864,128]{1,0:T(8,128)(2,1)}, bf16[864,128]{1,0:T(8,128)(2,1)S(1)}, u32[]{:S(2)}) copy-start(bf16[864,128]{1,0:T(8,128)(2,1)S(1)} %collective-permute-done.9.near) | copy-start | bytes 663556
  40.1 6.9 %collective-permute-start.11 = (bf16[1312,128]{1,0:T(8,128)(2,1)S(1)}, bf16[1312,128]{1,0:T(8,128)(2,1)S(1)}, u32[]{:S(2)}, u32[]{:S(2)}) collective-permute-start(bf16[1312,128]{1,0:T(8,128)(2,1)S(1)} %pad_maximum_fusion.1), channel_id=1, source_target_pairs={{0,4},{4,0},{8,12},{12,8},{16,20},{20,16},{24,28},{28,24},{32,36},... | collective-permute-start | bytes 1007624 | tf_op jit(solution)/shard_map/ppermute | solution.py:300
  40.2 12.8 %copy-start.6 = (bf16[8,64,128]{2,1,0:T(8,128)(2,1)}, bf16[8,64,128]{2,1,0:T(8,128)(2,1)S(1)}, u32[]{:S(2)}) copy-start(bf16[8,64,128]{2,1,0:T(8,128)(2,1)S(1)} %collective-permute-done.1.mine_l1) | copy-start | bytes 393220
  43.8 9.2 %copy-start.7 = (bf16[8,64,128]{2,1,0:T(8,128)(2,1)}, bf16[8,64,128]{2,1,0:T(8,128)(2,1)S(1)}, u32[]{:S(2)}) copy-start(bf16[8,64,128]{2,1,0:T(8,128)(2,1)S(1)} %collective-permute-done.2.mine_r1) | copy-start | bytes 393220
  44.5 8.4 %collective-permute-start.7 = (bf16[16,64,128]{2,1,0:T(8,128)(2,1)}, bf16[16,64,128]{2,1,0:T(8,128)(2,1)S(1)}, u32[]{:S(2)}, u32[]{:S(2)}) collective-permute-start(bf16[16,64,128]{2,1,0:T(8,128)(2,1)} %pad_maximum_fusion.2), channel_id=1, source_target_pairs={{0,4},{4,0},{8,12},{12,8},{16,20},{20,16},{24,28},{28,24},{32,36},... | collective-permute-start | bytes 786440 | tf_op jit(solution)/shard_map/ppermute | solution.py:297
  46.9 0.7 copy-start.10
  52.9 0.7 copy-start.13
  52.9 0.8 copy-start.9
  71.7 17.8 %all-to-all-start = ((bf16[64,16,128]{2,1,0:T(8,128)(2,1)}), bf16[64,16,128]{2,1,0:T(8,128)(2,1)S(1)}, u32[]{:S(2)}, u32[]{:S(2)}) async-start(bf16[64,16,128]{2,1,0:T(8,128)(2,1)} %bitcast.41), calls=%async_computation | async-start | bytes 524288 | tf_op jit(solution)/shard_map/all_to_all | solution.py:317
  76.8 23.3 %collective-permute-start.12 = (bf16[2,4,64,128]{3,2,1,0:T(8,128)(2,1)}, bf16[2,4,64,128]{3,2,1,0:T(8,128)(2,1)S(1)}, u32[]{:S(2)}, u32[]{:S(2)}) collective-permute-start(bf16[2,4,64,128]{3,2,1,0:T(8,128)(2,1)} %get-tuple-element.16), channel_id=1, source_target_pairs={{0,0},{4,64},{64,4},{68,68},{1,1},{5,65},{65,5},{69,69},{2,2},{6,6... | collective-permute-start | bytes 393224 | tf_op jit(solution)/shard_map/ppermute | solution.py:325
  80.2 19.9 %collective-permute-start.13 = (bf16[2,4,64,128]{3,2,1,0:T(8,128)(2,1)}, bf16[2,4,64,128]{3,2,1,0:T(8,128)(2,1)S(1)}, u32[]{:S(2)}, u32[]{:S(2)}) collective-permute-start(bf16[2,4,64,128]{3,2,1,0:T(8,128)(2,1)} %get-tuple-element.17), channel_id=1, source_target_pairs={{0,4},{4,68},{64,0},{68,64},{1,5},{5,69},{65,1},{69,65},{2,6},{6,7... | collective-permute-start | bytes 393224 | tf_op jit(solution)/shard_map/ppermute | solution.py:326
  89.6 5.0 %collective-permute-start.14 = (bf16[16,128]{1,0:T(8,128)(2,1)S(1)}, bf16[16,128]{1,0:T(8,128)(2,1)S(1)}, u32[]{:S(2)}, u32[]{:S(2)}) collective-permute-start(bf16[16,128]{1,0:T(8,128)(2,1)S(1)} %reduce_sum.12), channel_id=1, source_target_pairs={{0,0},{4,64},{64,4},{68,68},{1,1},{5,65},{65,5},{69,69},{2,2},{6,6... | collective-permute-start | bytes 12296 | tf_op jit(solution)/shard_map/ppermute | solution.py:320
  95.3 16.8 %all-to-all-start.1 = ((bf16[64,16,128]{2,1,0:T(8,128)(2,1)}), bf16[64,16,128]{2,1,0:T(8,128)(2,1)S(1)}, u32[]{:S(2)}, u32[]{:S(2)}) async-start(bf16[64,16,128]{2,1,0:T(8,128)(2,1)} %broadcast_in_dim.2), calls=%async_computation.1 | async-start | bytes 524288 | tf_op jit(solution)/shard_map/all_to_all | solution.py:321
  112.2 0.7 copy-start

commit v4 on v3

--- a/solution.py
+++ b/solution.py
@@ -56,7 +56,7 @@
 
 def sections_kernel(
     where_ref,
-    mine_c, mine_l1, mine_r1, mine_l2, mine_r2, mine_l3, mine_r3, other_c, other_1, other_23,
+    chip_rows, got1, got2, got3, other1, other2, other3,
     wf_ref, wb_ref,
     even_ref, odd_ref, wg_ref,
     h_ref, a1_ref, a2_ref, p1_ref, p2_ref, g_ref, gp1_ref, gp2_ref,
@@ -64,19 +64,15 @@
     mine = where_ref[0]
     first_row = where_ref[1]
     core = where_ref[2]
-    here, there = 4 * core, 4 * (1 - core)
-    mine_pieces = (mine_c, mine_l1, mine_r1, mine_l2, mine_r2, mine_l3, mine_r3)
-    for piece, base in zip(mine_pieces, (24, 16, 32, 8, 40, 0, 48)):
-        h_ref[0, pl.ds(base + here, 4)] = piece[0:4]
-        if 8 <= base <= 40:
-            g_ref[DEPTH, pl.ds(base + here, 4)] = piece[4:8]
-    for piece, at, base in (
-        (other_c, 0, 24), (other_1, 0, 16), (other_1, 8, 32),
-        (other_23, 0, 8), (other_23, 8, 40), (other_23, 16, 0), (other_23, 20, 48),
-    ):
-        h_ref[0, pl.ds(base + there, 4)] = piece[at:at + 4]
-        if 8 <= base <= 40:
-            g_ref[DEPTH, pl.ds(base + there, 4)] = piece[at + 4:at + 8]
+    h_ref[0, 24:32] = chip_rows[0:8]
+    g_ref[DEPTH, 24:32] = chip_rows[8:16]
+    for pieces, lower in (((got1, got2, got3), core), ((other1, other2, other3), 1 - core)):
+        one, two, three = pieces
+        h_ref[0, pl.ds(16 + 16 * lower, 8)] = one[0:8]
+        h_ref[0, pl.ds(8 + 32 * lower, 8)] = two[0:8]
+        h_ref[0, pl.ds(2 + 46 * lower, 6)] = three[...]
+        g_ref[DEPTH, pl.ds(16 + 16 * lower, 8)] = one[8:16]
+        g_ref[DEPTH, pl.ds(12 + 28 * lower, 4)] = two[8:12]
 
     lane = lax.broadcasted_iota(jnp.int32, (128, WID), 1)
     not_first = lane > 0
@@ -237,7 +233,7 @@
             jax.ShapeDtypeStruct((2, 4, C, WID), BF),
             jax.ShapeDtypeStruct((1024, 128), BF),
         ],
-        in_specs=[pl.BlockSpec(memory_space=pltpu.SMEM)] + vmem(12),
+        in_specs=[pl.BlockSpec(memory_space=pltpu.SMEM)] + vmem(9),
         out_specs=vmem(3),
         scratch_shapes=[
             pltpu.VMEM((DEPTH + 1,) + window, BF),
@@ -286,17 +282,22 @@
     swapped = [(i, i ^ 1) for i in range(2 * CHIPS)]
 
     def chips_away(value, chips):
-        pairs = [(i, i + chips) for i in range(CHIPS) if 0 <= i + chips < CHIPS]
-        return lax.ppermute(value, "z", pairs)
-
-    other_c = lax.ppermute(center, BAND, swapped)
-    center, other_c, raw = lax.optimization_barrier((center, other_c, raw))
-    left3, right3 = chips_away(center[0:4], 3), chips_away(center[0:4], -3)
-    left2, right2 = chips_away(center, 2), chips_away(center, -2)
-    left1, right1 = chips_away(center, 1), chips_away(center, -1)
-    other_1 = lax.ppermute(jnp.concatenate([left1, right1]), BAND, swapped)
-    other_23 = lax.ppermute(jnp.concatenate([left2, right2, left3, right3]), BAND, swapped)
-
+        pairs = [
+            (2 * z + c, 2 * (z + step) + c)
+            for c, step in ((0, chips), (1, -chips))
+            for z in range(CHIPS)
+            if 0 <= z + step < CHIPS
+        ]
+        return lax.ppermute(value, BAND, pairs)
+
+    upper = core == 0
+    swap = lax.ppermute(center, BAND, swapped)
+    first, last = jnp.where(upper, center, swap), jnp.where(upper, swap, center)
+    chip = jnp.concatenate([first[0:4], last[0:4], first[4:8], last[4:8]])
+    got3 = chips_away(jnp.where(upper, chip[2:8], chip[0:6]), 3)
+    got2 = chips_away(jnp.concatenate([chip[0:8], jnp.where(upper, chip[12:16], chip[8:12])]), 2)
+    got1 = chips_away(chip, 1)
+    other1, other2, other3 = (lax.ppermute(got, BAND, swapped) for got in (got1, got2, got3))
     other_weights = lax.ppermute(jnp.concatenate([near, half]), BAND, swapped)
     fwd, bwd = pl.pallas_call(
         weight_blocks_kernel,
@@ -309,7 +310,7 @@
 
     even, odd, grads = sections_call(
         where,
-        (center, left1, right1, left2, right2, left3, right3, other_c, other_1, other_23),
+        (chip, got1, got2, got3, other1, other2, other3),
         fwd,
         bwd,
     )

time: 116 us -> 110 us (0.948)
  waiting for transfers between devices: 30.3 us -> 26.5 us
  starting transfers between devices: 49.6 us -> 47.8 us
    ppermute x9 -> x7, starting transfers between devices: 29.1 us -> 17.4 us  [the longest x3 10.2 us: on_device(): lax.ppermute(got, BAND, swapped)]
    all_to_all x1, starting transfers between devices: 5.14 us -> 12.1 us  [on_device(): lax.all_to_all(grads.reshape(64, 16, 128), ('rep', 'side', 'z'), 0, 0, ti...]
    ppermute x9 -> x7, waiting for transfers between devices: 9.46 us -> 2.9 us  [the longest x3 2.89 us: chips_away(): return lax.ppermute(value, BAND, pairs)]
    ppermute x1, starting transfers between devices: 0.12 us -> 4.07 us  [on_device(): other_weights = lax.ppermute(jnp.concatenate([near, half]), BAND, swapped)]
    ppermute x1, starting transfers between devices: 2.81 us -> 0.85 us  [on_device(): lax.ppermute(raw, SECTION + ('core',), [(s * 2 + c, (s + 1 - 2 * c) % DEP...]
    ppermute x1, waiting for transfers between devices: 0.01 us -> 1.4 us  [on_device(): lax.ppermute(raw, SECTION + ('core',), [(s * 2 + c, (s + 1 - 2 * c) % DEP...]
    ppermute x1, waiting for transfers between devices: 0.01 us -> 1.31 us  [on_device(): lax.ppermute(jnp.where(core == 0, raw[:448], raw[416:]), SECTION, [(s, (s...]
    unnamed x32 -> x26, local copies, waits for them, and re-layouts: 3.71 us -> 3.68 us
  transfers between devices with their start and end apart: 17 -> 15, of which waited for: 6 -> 7; matrix products, arithmetic and copies ran while one was open for 5% -> 4% of each run, Pallas kernels for 5% -> 5%
where the time goes in v4:
time: 110 us; the launch traced here: 108 us
  starting transfers between devices  47.8 us (43%)
  waiting for transfers between devices  26.5 us (24%)
  Pallas kernels  25 us (23%)
  local copies, waits for them, and re-layouts  7.32 us (7%)
    pallas_call x1, Pallas kernels, sections_call(): pl.pallas_call(sections_kernel, out_shape=[jax.ShapeDtypeStruct((2, 4, C,...  17.8 us
    all_to_all x1, starting transfers between devices, on_device(): lax.all_to_all(grads.reshape(64, 16, 128), ('rep', 'side', 'z'), 0, 0, ti...  12.1 us
    all_to_all x1, waiting for transfers between devices, on_device(): lax.all_to_all(jnp.broadcast_to(total[None], (64, 16, 128)), ('rep', 'cor...  10.4 us
    ppermute x3, starting transfers between devices, on_device(): lax.ppermute(got, BAND, swapped)  10.2 us
    all_to_all x1, waiting for transfers between devices, on_device(): lax.all_to_all(grads.reshape(64, 16, 128), ('rep', 'side', 'z'), 0, 0, ti...  9.18 us
    pallas_call x1, Pallas kernels, on_device(): pl.pallas_call(weight_blocks_kernel, out_shape=[jax.ShapeDtypeStruct((12,...  5.23 us
    all_to_all x1, starting transfers between devices, on_device(): lax.all_to_all(jnp.broadcast_to(total[None], (64, 16, 128)), ('rep', 'cor...  4.82 us
    ppermute x1, starting transfers between devices, on_device(): other_weights = lax.ppermute(jnp.concatenate([near, half]), BAND, swapped)  4.07 us
  transfers between devices with their start and end apart: 15, of which 7 were waited for; matrix products, arithmetic and copies ran while one was open for 4% of the time, Pallas kernels for 5%

profile of v4, /device:TPU:1, one launch (start us, length us, event | category | flops | bytes accessed | tf_op | source)
XLA Modules:
  0.0 108.3 jit_solution(15127373506556556655)
XLA Ops:
  0.6 1.0 fusion.6
  1.9 3.3 %collective-permute-start = (bf16[8,64,128]{2,1,0:T(8,128)(2,1)S(1)}, bf16[8,64,128]{2,1,0:T(8,128)(2,1)S(1)}, u32[]{:S(2)}, u32[]{:S(2)}) collective-permute-start(bf16[8,64,128]{2,1,0:T(8,128)(2,1)S(1)} %bitcast.35), channel_id=1, source_target_pairs={{0,4},{4,0},{8,12},{12,8},{16,20},{20,16},{24,28},{28,24},{32,36},... | collective-permute-start | bytes 393224 | tf_op jit(solution)/shard_map/ppermute | solution.py:294
  5.2 1.2 %slice_bitcast_fusion = (bf16[27,32,64]{2,1,0:T(8,128)(2,1)S(1)}, bf16[27,32,64]{2,1,0:T(8,128)(2,1)S(1)}, bf16[27,1,32,64]{3,2,1,0:T(8,128)(2,1)S(1)}, bf16[27,1,32,64]{3,2,1,0:T(8,128)(2,1)S(1)}) fusion(bf16[27,2,32,64]{3,2,1,0:T(8,128)(2,1)} %bitcast.36), kind=kLoop, calls=%fused_computation.22 | loop fusion | bytes 663552 | tf_op jit(solution)/shard_map/squeeze | solution.py:265
  6.5 1.3 %collective-permute-start.8 = (bf16[448,128]{1,0:T(8,128)(2,1)S(1)}, bf16[448,128]{1,0:T(8,128)(2,1)S(1)}, u32[]{:S(2)}, u32[]{:S(2)}) collective-permute-start(bf16[448,128]{1,0:T(8,128)(2,1)S(1)} %bitcast.38), channel_id=1, source_target_pairs={{0,128},{64,192},{128,0},{192,64},{1,129},{65,193},{129,1},{193,65... | collective-permute-start | bytes 344072 | tf_op jit(solution)/shard_map/ppermute | solution.py:275
  7.9 0.9 collective-permute-start.7
  8.9 1.3 %collective-permute-start.2 = (bf16[12,64,128]{2,1,0:T(8,128)(2,1)S(1)}, bf16[12,64,128]{2,1,0:T(8,128)(2,1)S(1)}, u32[]{:S(2)}, u32[]{:S(2)}) collective-permute-start(bf16[12,64,128]{2,1,0:T(8,128)(2,1)S(1)} %pad_maximum_fusion.3), channel_id=1, source_target_pairs={{0,16},{8,24},{16,32},{24,40},{32,48},{40,56},{20,4},{28,12},{36,2... | collective-permute-start | bytes 589832 | tf_op jit(solution)/shard_map/ppermute | solution.py:291
  10.2 1.3 %collective-permute-start.1 = (bf16[16,64,128]{2,1,0:T(8,128)(2,1)S(1)}, bf16[16,64,128]{2,1,0:T(8,128)(2,1)S(1)}, u32[]{:S(2)}, u32[]{:S(2)}) collective-permute-start(bf16[16,64,128]{2,1,0:T(8,128)(2,1)S(1)} %pad_maximum_fusion.1.chip_rows), channel_id=1, source_target_pairs={{0,8},{8,16},{16,24},{24,32},{32,40},{40,48},{48,56},{12,4},{20,12... | collective-permute-start | bytes 786440 | tf_op jit(solution)/shard_map/ppermute | solution.py:291
  11.5 1.3 %collective-permute-done.8.half = bf16[448,128]{1,0:T(8,128)(2,1)S(1)} collective-permute-done((bf16[448,128]{1,0:T(8,128)(2,1)S(1)}, bf16[448,128]{1,0:T(8,128)(2,1)S(1)}, u32[]{:S(2)}, u32[]{:S(2)}) %collective-permute-start.8) | collective-permute-done | bytes 114720 | tf_op jit(solution)/shard_map/ppermute | solution.py:275
  12.8 1.4 %collective-permute-done.7.near = bf16[864,128]{1,0:T(8,128)(2,1)S(1)} collective-permute-done((bf16[864,128]{1,0:T(8,128)(2,1)S(1)}, bf16[864,128]{1,0:T(8,128)(2,1)S(1)}, u32[]{:S(2)}, u32[]{:S(2)}) %collective-permute-start.7) | collective-permute-done | bytes 221216 | tf_op jit(solution)/shard_map/ppermute | solution.py:266
  14.3 4.1 %collective-permute-start.9 = (bf16[1312,128]{1,0:T(8,128)(2,1)S(1)}, bf16[1312,128]{1,0:T(8,128)(2,1)S(1)}, u32[]{:S(2)}, u32[]{:S(2)}) collective-permute-start(bf16[1312,128]{1,0:T(8,128)(2,1)S(1)} %pad_maximum_fusion), channel_id=1, source_target_pairs={{0,4},{4,0},{8,12},{12,8},{16,20},{20,16},{24,28},{28,24},{32,36},... | collective-permute-start | bytes 1007624 | tf_op jit(solution)/shard_map/ppermute | solution.py:301
  18.3 1.3 %collective-permute-done.1.got1 = bf16[16,64,128]{2,1,0:T(8,128)(2,1)S(1)} collective-permute-done((bf16[16,64,128]{2,1,0:T(8,128)(2,1)S(1)}, bf16[16,64,128]{2,1,0:T(8,128)(2,1)S(1)}, u32[]{:S(2)}, u32[]{:S(2)}) %collective-permute-start.1) | collective-permute-done | bytes 262176 | tf_op jit(solution)/shard_map/ppermute | solution.py:291
  19.6 2.4 %collective-permute-start.4 = (bf16[16,64,128]{2,1,0:T(8,128)(2,1)S(1)}, bf16[16,64,128]{2,1,0:T(8,128)(2,1)S(1)}, u32[]{:S(2)}, u32[]{:S(2)}) collective-permute-start(bf16[16,64,128]{2,1,0:T(8,128)(2,1)S(1)} %collective-permute-done.1.got1), channel_id=1, source_target_pairs={{0,4},{4,0},{8,12},{12,8},{16,20},{20,16},{24,28},{28,24},{32,36},... | collective-permute-start | bytes 786440 | tf_op jit(solution)/shard_map/ppermute | solution.py:300
  22.1 1.3 %collective-permute-start.3 = (bf16[6,64,128]{2,1,0:T(8,128)(2,1)S(1)}, bf16[6,64,128]{2,1,0:T(8,128)(2,1)S(1)}, u32[]{:S(2)}, u32[]{:S(2)}) collective-permute-start(bf16[6,64,128]{2,1,0:T(8,128)(2,1)S(1)} %fusion.4), channel_id=1, source_target_pairs={{0,24},{8,32},{16,40},{24,48},{32,56},{28,4},{36,12},{44,20},{52,2... | collective-permute-start | bytes 294920 | tf_op jit(solution)/shard_map/ppermute | solution.py:291
  23.4 7.3 %collective-permute-start.5 = (bf16[12,64,128]{2,1,0:T(8,128)(2,1)S(1)}, bf16[12,64,128]{2,1,0:T(8,128)(2,1)S(1)}, u32[]{:S(2)}, u32[]{:S(2)}) collective-permute-start(bf16[12,64,128]{2,1,0:T(8,128)(2,1)S(1)} %collective-permute-done.2.got2), channel_id=1, source_target_pairs={{0,4},{4,0},{8,12},{12,8},{16,20},{20,16},{24,28},{28,24},{32,36},... | collective-permute-start | bytes 589832 | tf_op jit(solution)/shard_map/ppermute | solution.py:300
  30.7 1.6 %collective-permute-done.3.got3 = bf16[6,64,128]{2,1,0:T(8,128)(2,1)S(1)} collective-permute-done((bf16[6,64,128]{2,1,0:T(8,128)(2,1)S(1)}, bf16[6,64,128]{2,1,0:T(8,128)(2,1)S(1)}, u32[]{:S(2)}, u32[]{:S(2)}) %collective-permute-start.3) | collective-permute-done | bytes 98336 | tf_op jit(solution)/shard_map/ppermute | solution.py:291
  32.8 0.7 stack.38.where_ref
  33.5 0.7 copy-done.5
  34.2 5.2 %weight_blocks.1 = (bf16[12,128,768]{2,1,0:T(8,128)(2,1)}, bf16[12,128,768]{2,1,0:T(8,128)(2,1)}) custom-call(s32[5]{0:T(128)} %stack.38.where_ref, bf16[864,128]{1,0:T(8,128)(2,1)} %copy-done.2, bf16[864,128]{1,0:T(8,128)(2,1)} %copy-done.3, bf16[448,128]{1,0:T(8,128)(2,1)} %copy-done.4, bf16[1312,128]{1,0:T(8,128)(2,1)} %copy-done.5), custom_call_target="tpu_custom_call" | custom-call | tf_op jit(solution)/shard_map/weight_blocks/pallas_call | solution.py:302
  39.5 0.5 copy-done.11
  40.3 17.8 %sections.1 = (bf16[2,4,64,128]{3,2,1,0:T(8,128)(2,1)}, bf16[2,4,64,128]{3,2,1,0:T(8,128)(2,1)}, bf16[1024,128]{1,0:T(8,128)(2,1)}) custom-call(s32[5]{0:T(128)} %stack.38.where_ref, bf16[16,64,128]{2,1,0:T(8,128)(2,1)} %copy-done, bf16[16,64,128]{2,1,0:T(8,128)(2,1)} %copy-done.6, bf16[12,64,128]{2,1,0:T(8,128)(2,1)} %copy-done.8, ...), custom_call_target="tpu_custom_call" | custom-call | tf_op jit(solution)/shard_map/sections/pallas_call | solution.py:229
  58.1 12.1 %all-to-all-start = ((bf16[64,16,128]{2,1,0:T(8,128)(2,1)}), bf16[64,16,128]{2,1,0:T(8,128)(2,1)S(1)}, u32[]{:S(2)}, u32[]{:S(2)}) async-start(bf16[64,16,128]{2,1,0:T(8,128)(2,1)} %bitcast.37), calls=%async_computation | async-start | bytes 524288 | tf_op jit(solution)/shard_map/all_to_all | solution.py:318
  70.2 3.4 %collective-permute-start.10 = (bf16[2,4,64,128]{3,2,1,0:T(8,128)(2,1)}, bf16[2,4,64,128]{3,2,1,0:T(8,128)(2,1)S(1)}, u32[]{:S(2)}, u32[]{:S(2)}) collective-permute-start(bf16[2,4,64,128]{3,2,1,0:T(8,128)(2,1)} %get-tuple-element.10), channel_id=1, source_target_pairs={{0,0},{4,64},{64,4},{68,68},{1,1},{5,65},{65,5},{69,69},{2,2},{6,6... | collective-permute-start | bytes 393224 | tf_op jit(solution)/shard_map/ppermute | solution.py:326
  73.7 9.2 %all-to-all-done = bf16[64,16,128]{2,1,0:T(8,128)(2,1)S(1)} async-done(((bf16[64,16,128]{2,1,0:T(8,128)(2,1)}), bf16[64,16,128]{2,1,0:T(8,128)(2,1)S(1)}, u32[]{:S(2)}, u32[]{:S(2)}) %all-to-all-start) | async-done | bytes 262176 | tf_op jit(solution)/shard_map/all_to_all | solution.py:318
  82.9 3.8 %collective-permute-start.12 = (bf16[16,128]{1,0:T(8,128)(2,1)S(1)}, bf16[16,128]{1,0:T(8,128)(2,1)S(1)}, u32[]{:S(2)}, u32[]{:S(2)}) collective-permute-start(bf16[16,128]{1,0:T(8,128)(2,1)S(1)} %reduce_sum.12), channel_id=1, source_target_pairs={{0,0},{4,64},{64,4},{68,68},{1,1},{5,65},{65,5},{69,69},{2,2},{6,6... | collective-permute-start | bytes 12296 | tf_op jit(solution)/shard_map/ppermute | solution.py:321
  86.7 1.3 %collective-permute-done.12 = bf16[16,128]{1,0:T(8,128)(2,1)S(1)} collective-permute-done((bf16[16,128]{1,0:T(8,128)(2,1)S(1)}, bf16[16,128]{1,0:T(8,128)(2,1)S(1)}, u32[]{:S(2)}, u32[]{:S(2)}) %collective-permute-start.12) | collective-permute-done | bytes 4128 | tf_op jit(solution)/shard_map/ppermute | solution.py:321
  88.0 0.7 broadcast_in_dim.2
  88.7 4.8 %all-to-all-start.1 = ((bf16[64,16,128]{2,1,0:T(8,128)(2,1)}), bf16[64,16,128]{2,1,0:T(8,128)(2,1)S(1)}, u32[]{:S(2)}, u32[]{:S(2)}) async-start(bf16[64,16,128]{2,1,0:T(8,128)(2,1)} %broadcast_in_dim.2), calls=%async_computation.1 | async-start | bytes 524288 | tf_op jit(solution)/shard_map/all_to_all | solution.py:322
  93.7 0.8 copy.10
  94.4 0.8 copy.9
  95.2 10.4 %all-to-all-done.1 = bf16[64,16,128]{2,1,0:T(8,128)(2,1)S(1)} async-done(((bf16[64,16,128]{2,1,0:T(8,128)(2,1)}), bf16[64,16,128]{2,1,0:T(8,128)(2,1)S(1)}, u32[]{:S(2)}, u32[]{:S(2)}) %all-to-all-start.1) | async-done | bytes 262176 | tf_op jit(solution)/shard_map/all_to_all | solution.py:322
  105.6 0.7 copy-done.1
  106.3 2.0 %unpack.1 = f32[1,3,3,3,64,64]{5,4,3,2,1,0:T(8,128)} custom-call(bf16[1024,128]{1,0:T(8,128)(2,1)} %bitcast.32), custom_call_target="tpu_custom_call" | custom-call | tf_op jit(solution)/shard_map/unpack/pallas_call | solution.py:334
  (45 shorter events, 1.6 us)
Async XLA Ops:
  1.9 6.9 %collective-permute-start = (bf16[8,64,128]{2,1,0:T(8,128)(2,1)S(1)}, bf16[8,64,128]{2,1,0:T(8,128)(2,1)S(1)}, u32[]{:S(2)}, u32[]{:S(2)}) collective-permute-start(bf16[8,64,128]{2,1,0:T(8,128)(2,1)S(1)} %bitcast.35), channel_id=1, source_target_pairs={{0,4},{4,0},{8,12},{12,8},{16,20},{20,16},{24,28},{28,24},{32,36},... | collective-permute-start | bytes 393224 | tf_op jit(solution)/shard_map/ppermute | solution.py:294
  6.5 6.3 %collective-permute-start.8 = (bf16[448,128]{1,0:T(8,128)(2,1)S(1)}, bf16[448,128]{1,0:T(8,128)(2,1)S(1)}, u32[]{:S(2)}, u32[]{:S(2)}) collective-permute-start(bf16[448,128]{1,0:T(8,128)(2,1)S(1)} %bitcast.38), channel_id=1, source_target_pairs={{0,128},{64,192},{128,0},{192,64},{1,129},{65,193},{129,1},{193,65... | collective-permute-start | bytes 344072 | tf_op jit(solution)/shard_map/ppermute | solution.py:275
  7.9 25.6 %copy-start.2 = (bf16[864,128]{1,0:T(8,128)(2,1)}, bf16[864,128]{1,0:T(8,128)(2,1)S(1)}, u32[]{:S(2)}) copy-start(bf16[864,128]{1,0:T(8,128)(2,1)S(1)} %pad_maximum_fusion.2.own) | copy-start | bytes 663556
  7.9 6.3 %collective-permute-start.7 = (bf16[864,128]{1,0:T(8,128)(2,1)S(1)}, bf16[864,128]{1,0:T(8,128)(2,1)S(1)}, u32[]{:S(2)}, u32[]{:S(2)}) collective-permute-start(bf16[864,128]{1,0:T(8,128)(2,1)S(1)} %pad_maximum_fusion.2.own), channel_id=1, source_target_pairs={{0,64},{4,196},{64,128},{68,4},{128,192},{132,68},{192,0},{196,132... | collective-permute-start | bytes 663560 | tf_op jit(solution)/shard_map/ppermute | solution.py:266
  8.9 14.5 %collective-permute-start.2 = (bf16[12,64,128]{2,1,0:T(8,128)(2,1)S(1)}, bf16[12,64,128]{2,1,0:T(8,128)(2,1)S(1)}, u32[]{:S(2)}, u32[]{:S(2)}) collective-permute-start(bf16[12,64,128]{2,1,0:T(8,128)(2,1)S(1)} %pad_maximum_fusion.3), channel_id=1, source_target_pairs={{0,16},{8,24},{16,32},{24,40},{32,48},{40,56},{20,4},{28,12},{36,2... | collective-permute-start | bytes 589832 | tf_op jit(solution)/shard_map/ppermute | solution.py:291
  10.2 29.3 %copy-start = (bf16[16,64,128]{2,1,0:T(8,128)(2,1)}, bf16[16,64,128]{2,1,0:T(8,128)(2,1)S(1)}, u32[]{:S(2)}) copy-start(bf16[16,64,128]{2,1,0:T(8,128)(2,1)S(1)} %pad_maximum_fusion.1.chip_rows) | copy-start | bytes 786436
  10.2 9.4 %collective-permute-start.1 = (bf16[16,64,128]{2,1,0:T(8,128)(2,1)S(1)}, bf16[16,64,128]{2,1,0:T(8,128)(2,1)S(1)}, u32[]{:S(2)}, u32[]{:S(2)}) collective-permute-start(bf16[16,64,128]{2,1,0:T(8,128)(2,1)S(1)} %pad_maximum_fusion.1.chip_rows), channel_id=1, source_target_pairs={{0,8},{8,16},{16,24},{24,32},{32,40},{40,48},{48,56},{12,4},{20,12... | collective-permute-start | bytes 786440 | tf_op jit(solution)/shard_map/ppermute | solution.py:291
  12.8 20.6 %copy-start.4 = (bf16[448,128]{1,0:T(8,128)(2,1)}, bf16[448,128]{1,0:T(8,128)(2,1)S(1)}, u32[]{:S(2)}) copy-start(bf16[448,128]{1,0:T(8,128)(2,1)S(1)} %collective-permute-done.8.half) | copy-start | bytes 344068
  14.2 19.2 %copy-start.3 = (bf16[864,128]{1,0:T(8,128)(2,1)}, bf16[864,128]{1,0:T(8,128)(2,1)S(1)}, u32[]{:S(2)}) copy-start(bf16[864,128]{1,0:T(8,128)(2,1)S(1)} %collective-permute-done.7.near) | copy-start | bytes 663556
  14.3 19.2 %collective-permute-start.9 = (bf16[1312,128]{1,0:T(8,128)(2,1)S(1)}, bf16[1312,128]{1,0:T(8,128)(2,1)S(1)}, u32[]{:S(2)}, u32[]{:S(2)}) collective-permute-start(bf16[1312,128]{1,0:T(8,128)(2,1)S(1)} %pad_maximum_fusion), channel_id=1, source_target_pairs={{0,4},{4,0},{8,12},{12,8},{16,20},{20,16},{24,28},{28,24},{32,36},... | collective-permute-start | bytes 1007624 | tf_op jit(solution)/shard_map/ppermute | solution.py:301
  19.6 19.9 %copy-start.6 = (bf16[16,64,128]{2,1,0:T(8,128)(2,1)}, bf16[16,64,128]{2,1,0:T(8,128)(2,1)S(1)}, u32[]{:S(2)}) copy-start(bf16[16,64,128]{2,1,0:T(8,128)(2,1)S(1)} %collective-permute-done.1.got1) | copy-start | bytes 786436
  19.6 19.9 %collective-permute-start.4 = (bf16[16,64,128]{2,1,0:T(8,128)(2,1)S(1)}, bf16[16,64,128]{2,1,0:T(8,128)(2,1)S(1)}, u32[]{:S(2)}, u32[]{:S(2)}) collective-permute-start(bf16[16,64,128]{2,1,0:T(8,128)(2,1)S(1)} %collective-permute-done.1.got1), channel_id=1, source_target_pairs={{0,4},{4,0},{8,12},{12,8},{16,20},{20,16},{24,28},{28,24},{32,36},... | collective-permute-start | bytes 786440 | tf_op jit(solution)/shard_map/ppermute | solution.py:300
  22.1 10.3 %collective-permute-start.3 = (bf16[6,64,128]{2,1,0:T(8,128)(2,1)S(1)}, bf16[6,64,128]{2,1,0:T(8,128)(2,1)S(1)}, u32[]{:S(2)}, u32[]{:S(2)}) collective-permute-start(bf16[6,64,128]{2,1,0:T(8,128)(2,1)S(1)} %fusion.4), channel_id=1, source_target_pairs={{0,24},{8,32},{16,40},{24,48},{32,56},{28,4},{36,12},{44,20},{52,2... | collective-permute-start | bytes 294920 | tf_op jit(solution)/shard_map/ppermute | solution.py:291
  23.4 16.2 %copy-start.8 = (bf16[12,64,128]{2,1,0:T(8,128)(2,1)}, bf16[12,64,128]{2,1,0:T(8,128)(2,1)S(1)}, u32[]{:S(2)}) copy-start(bf16[12,64,128]{2,1,0:T(8,128)(2,1)S(1)} %collective-permute-done.2.got2) | copy-start | bytes 589828
  23.4 16.1 %collective-permute-start.5 = (bf16[12,64,128]{2,1,0:T(8,128)(2,1)S(1)}, bf16[12,64,128]{2,1,0:T(8,128)(2,1)S(1)}, u32[]{:S(2)}, u32[]{:S(2)}) collective-permute-start(bf16[12,64,128]{2,1,0:T(8,128)(2,1)S(1)} %collective-permute-done.2.got2), channel_id=1, source_target_pairs={{0,4},{4,0},{8,12},{12,8},{16,20},{20,16},{24,28},{28,24},{32,36},... | collective-permute-start | bytes 589832 | tf_op jit(solution)/shard_map/ppermute | solution.py:300
  32.3 7.2 %copy-start.10 = (bf16[6,64,128]{2,1,0:T(8,128)(2,1)}, bf16[6,64,128]{2,1,0:T(8,128)(2,1)S(1)}, u32[]{:S(2)}) copy-start(bf16[6,64,128]{2,1,0:T(8,128)(2,1)S(1)} %collective-permute-done.3.got3) | copy-start | bytes 294916
  32.3 7.1 %collective-permute-start.6 = (bf16[6,64,128]{2,1,0:T(8,128)(2,1)S(1)}, bf16[6,64,128]{2,1,0:T(8,128)(2,1)S(1)}, u32[]{:S(2)}, u32[]{:S(2)}) collective-permute-start(bf16[6,64,128]{2,1,0:T(8,128)(2,1)S(1)} %collective-permute-done.3.got3), channel_id=1, source_target_pairs={{0,4},{4,0},{8,12},{12,8},{16,20},{20,16},{24,28},{28,24},{32,36},... | collective-permute-start | bytes 294920 | tf_op jit(solution)/shard_map/ppermute | solution.py:300
  33.5 0.7 copy-start.5
  39.5 0.6 copy-start.11
  39.5 0.7 copy-start.9
  39.5 0.8 copy-start.7
  58.1 24.8 %all-to-all-start = ((bf16[64,16,128]{2,1,0:T(8,128)(2,1)}), bf16[64,16,128]{2,1,0:T(8,128)(2,1)S(1)}, u32[]{:S(2)}, u32[]{:S(2)}) async-start(bf16[64,16,128]{2,1,0:T(8,128)(2,1)} %bitcast.37), calls=%async_computation | async-start | bytes 524288 | tf_op jit(solution)/shard_map/all_to_all | solution.py:318
  70.2 23.3 %collective-permute-start.10 = (bf16[2,4,64,128]{3,2,1,0:T(8,128)(2,1)}, bf16[2,4,64,128]{3,2,1,0:T(8,128)(2,1)S(1)}, u32[]{:S(2)}, u32[]{:S(2)}) collective-permute-start(bf16[2,4,64,128]{3,2,1,0:T(8,128)(2,1)} %get-tuple-element.10), channel_id=1, source_target_pairs={{0,0},{4,64},{64,4},{68,68},{1,1},{5,65},{65,5},{69,69},{2,2},{6,6... | collective-permute-start | bytes 393224 | tf_op jit(solution)/shard_map/ppermute | solution.py:326
  73.6 20.0 %collective-permute-start.11 = (bf16[2,4,64,128]{3,2,1,0:T(8,128)(2,1)}, bf16[2,4,64,128]{3,2,1,0:T(8,128)(2,1)S(1)}, u32[]{:S(2)}, u32[]{:S(2)}) collective-permute-start(bf16[2,4,64,128]{3,2,1,0:T(8,128)(2,1)} %get-tuple-element.11), channel_id=1, source_target_pairs={{0,4},{4,68},{64,0},{68,64},{1,5},{5,69},{65,1},{69,65},{2,6},{6,7... | collective-permute-start | bytes 393224 | tf_op jit(solution)/shard_map/ppermute | solution.py:327
  82.9 5.0 %collective-permute-start.12 = (bf16[16,128]{1,0:T(8,128)(2,1)S(1)}, bf16[16,128]{1,0:T(8,128)(2,1)S(1)}, u32[]{:S(2)}, u32[]{:S(2)}) collective-permute-start(bf16[16,128]{1,0:T(8,128)(2,1)S(1)} %reduce_sum.12), channel_id=1, source_target_pairs={{0,0},{4,64},{64,4},{68,68},{1,1},{5,65},{65,5},{69,69},{2,2},{6,6... | collective-permute-start | bytes 12296 | tf_op jit(solution)/shard_map/ppermute | solution.py:321
  88.7 16.9 %all-to-all-start.1 = ((bf16[64,16,128]{2,1,0:T(8,128)(2,1)}), bf16[64,16,128]{2,1,0:T(8,128)(2,1)S(1)}, u32[]{:S(2)}, u32[]{:S(2)}) async-start(bf16[64,16,128]{2,1,0:T(8,128)(2,1)} %broadcast_in_dim.2), calls=%async_computation.1 | async-start | bytes 524288 | tf_op jit(solution)/shard_map/all_to_all | solution.py:322
  105.6 0.7 copy-start.1

commit v5 on v4

--- a/solution.py
+++ b/solution.py
@@ -56,7 +56,7 @@
 
 def sections_kernel(
     where_ref,
-    chip_rows, got1, got2, got3, other1, other2, other3,
+    chip_rows, near_rows, far_rows, other_near, other_far,
     wf_ref, wb_ref,
     even_ref, odd_ref, wg_ref,
     h_ref, a1_ref, a2_ref, p1_ref, p2_ref, g_ref, gp1_ref, gp2_ref,
@@ -66,13 +66,11 @@
     core = where_ref[2]
     h_ref[0, 24:32] = chip_rows[0:8]
     g_ref[DEPTH, 24:32] = chip_rows[8:16]
-    for pieces, lower in (((got1, got2, got3), core), ((other1, other2, other3), 1 - core)):
-        one, two, three = pieces
+    for one, two, lower in ((near_rows, far_rows, core), (other_near, other_far, 1 - core)):
         h_ref[0, pl.ds(16 + 16 * lower, 8)] = one[0:8]
-        h_ref[0, pl.ds(8 + 32 * lower, 8)] = two[0:8]
-        h_ref[0, pl.ds(2 + 46 * lower, 6)] = three[...]
+        h_ref[0, pl.ds(2 + 38 * lower, 14)] = two[0:14]
         g_ref[DEPTH, pl.ds(16 + 16 * lower, 8)] = one[8:16]
-        g_ref[DEPTH, pl.ds(12 + 28 * lower, 4)] = two[8:12]
+        g_ref[DEPTH, pl.ds(12 + 28 * lower, 4)] = two[14:18]
 
     lane = lax.broadcasted_iota(jnp.int32, (128, WID), 1)
     not_first = lane > 0
@@ -233,7 +231,7 @@
             jax.ShapeDtypeStruct((2, 4, C, WID), BF),
             jax.ShapeDtypeStruct((1024, 128), BF),
         ],
-        in_specs=[pl.BlockSpec(memory_space=pltpu.SMEM)] + vmem(9),
+        in_specs=[pl.BlockSpec(memory_space=pltpu.SMEM)] + vmem(7),
         out_specs=vmem(3),
         scratch_shapes=[
             pltpu.VMEM((DEPTH + 1,) + window, BF),
@@ -294,10 +292,16 @@
     swap = lax.ppermute(center, BAND, swapped)
     first, last = jnp.where(upper, center, swap), jnp.where(upper, swap, center)
     chip = jnp.concatenate([first[0:4], last[0:4], first[4:8], last[4:8]])
-    got3 = chips_away(jnp.where(upper, chip[2:8], chip[0:6]), 3)
-    got2 = chips_away(jnp.concatenate([chip[0:8], jnp.where(upper, chip[12:16], chip[8:12])]), 2)
-    got1 = chips_away(chip, 1)
-    other1, other2, other3 = (lax.ppermute(got, BAND, swapped) for got in (got1, got2, got3))
+    near_rows = chips_away(chip, 1)
+    other_near = lax.ppermute(near_rows, BAND, swapped)
+    far_rows = chips_away(
+        jnp.where(
+            upper,
+            jnp.concatenate([near_rows[2:8], chip[0:8], chip[12:16]]),
+            jnp.concatenate([chip[0:8], near_rows[0:6], chip[8:12]]),
+        ),
+        2,
+    )
     other_weights = lax.ppermute(jnp.concatenate([near, half]), BAND, swapped)
     fwd, bwd = pl.pallas_call(
         weight_blocks_kernel,
@@ -307,10 +311,12 @@
         scratch_shapes=[pltpu.VMEM((864, 128), BF)],
         name="weight_blocks",
     )(where, raw, near, half, other_weights)
+    far_rows, other_near, fwd, bwd = lax.optimization_barrier((far_rows, other_near, fwd, bwd))
+    other_far = lax.ppermute(far_rows, BAND, swapped)
 
     even, odd, grads = sections_call(
         where,
-        (chip, got1, got2, got3, other1, other2, other3),
+        (chip, near_rows, far_rows, other_near, other_far),
         fwd,
         bwd,
     )

time: 110 us -> 103 us (0.936)
  starting transfers between devices: 47.8 us -> 42.4 us
  waiting for transfers between devices: 26.5 us -> 25.4 us
    ppermute x3 -> x2, starting transfers between devices: 10.2 us -> 5.28 us  [the longest x1 5.17 us: on_device(): other_near = lax.ppermute(near_rows, BAND, swapped)]
    ppermute x3 -> x2, waiting for transfers between devices: 2.89 us -> 0.06 us  [chips_away(): return lax.ppermute(value, BAND, pairs)]
    ppermute x1, starting transfers between devices: 4.07 us -> 1.88 us  [on_device(): other_weights = lax.ppermute(jnp.concatenate([near, half]), BAND, swapped)]
    all_to_all x1, starting transfers between devices: 12.1 us -> 14.2 us  [on_device(): lax.all_to_all(grads.reshape(64, 16, 128), ('rep', 'side', 'z'), 0, 0, ti...]
    ppermute x3 -> x2, waiting for transfers between devices: 0.01 us -> 1.56 us  [the longest x1 1.56 us: on_device(): other_far = lax.ppermute(far_rows, BAND, swapped)]
    ppermute x1, waiting for transfers between devices: 1.31 us -> 2.64 us  [on_device(): lax.ppermute(jnp.where(core == 0, raw[:448], raw[416:]), SECTION, [(s, (s...]
    ppermute x3 -> x2, starting transfers between devices: 3.88 us -> 2.58 us  [chips_away(): return lax.ppermute(value, BAND, pairs)]
    all_to_all x1, waiting for transfers between devices: 9.18 us -> 8.03 us  [on_device(): lax.all_to_all(grads.reshape(64, 16, 128), ('rep', 'side', 'z'), 0, 0, ti...]
  transfers between devices with their start and end apart: 15 -> 13, of which waited for: 7 -> 7; matrix products, arithmetic and copies ran while one was open for 4% -> 5% of each run, Pallas kernels for 5% -> 5%
where the time goes in v5:
time: 103 us; the launch traced here: 102 us
  starting transfers between devices  42.4 us (41%)
  waiting for transfers between devices  25.4 us (25%)
  Pallas kernels  25 us (24%)
  local copies, waits for them, and re-layouts  7.31 us (7%)
    pallas_call x1, Pallas kernels, sections_call(): pl.pallas_call(sections_kernel, out_shape=[jax.ShapeDtypeStruct((2, 4, C,...  17.7 us
    all_to_all x1, starting transfers between devices, on_device(): lax.all_to_all(grads.reshape(64, 16, 128), ('rep', 'side', 'z'), 0, 0, ti...  14.2 us
    all_to_all x1, waiting for transfers between devices, on_device(): lax.all_to_all(jnp.broadcast_to(total[None], (64, 16, 128)), ('rep', 'cor...  10.4 us
    all_to_all x1, waiting for transfers between devices, on_device(): lax.all_to_all(grads.reshape(64, 16, 128), ('rep', 'side', 'z'), 0, 0, ti...  8.03 us
    pallas_call x1, Pallas kernels, on_device(): pl.pallas_call(weight_blocks_kernel, out_shape=[jax.ShapeDtypeStruct((12,...  5.23 us
    ppermute x1, starting transfers between devices, on_device(): other_near = lax.ppermute(near_rows, BAND, swapped)  5.17 us
    ppermute x1, starting transfers between devices, on_device(): total = lax.ppermute(total, ('side', 'core'), turned)  4.62 us
    all_to_all x1, starting transfers between devices, on_device(): lax.all_to_all(jnp.broadcast_to(total[None], (64, 16, 128)), ('rep', 'cor...  4.57 us
  transfers between devices with their start and end apart: 13, of which 7 were waited for; matrix products, arithmetic and copies ran while one was open for 5% of the time, Pallas kernels for 5%

profile of v5, /device:TPU:1, one launch (start us, length us, event | category | flops | bytes accessed | tf_op | source)
XLA Modules:
  0.0 101.6 jit_solution(214959264877070083)
XLA Ops:
  0.6 1.0 %fusion.7 = (bf16[1,64,4,128]{3,2,1,0:T(4,128)(2,1)S(1)}, bf16[1,64,4,128]{3,2,1,0:T(4,128)(2,1)S(1)}, bf16[1,64,4,128]{3,2,1,0:T(4,128)(2,1)S(1)}, bf16[1,64,4,128]{3,2,1,0:T(4,128)(2,1)S(1)}) fusion(bf16[2,64,4,128]{3,2,1,0:T(4,128)(2,1)} %param.3, bf16[2,64,4,128]{3,2,1,0:T(4,128)(2,1)} %param.5), kind=kLoop, calls=%fused_computation.22 | loop fusion | bytes 524288 | tf_op jit(solution)/shard_map/slice | solution.py:278
  1.7 0.2 fusion
  1.9 3.3 %collective-permute-start = (bf16[8,64,128]{2,1,0:T(8,128)(2,1)S(1)}, bf16[8,64,128]{2,1,0:T(8,128)(2,1)S(1)}, u32[]{:S(2)}, u32[]{:S(2)}) collective-permute-start(bf16[8,64,128]{2,1,0:T(8,128)(2,1)S(1)} %bitcast.35), channel_id=1, source_target_pairs={{0,4},{4,0},{8,12},{12,8},{16,20},{20,16},{24,28},{28,24},{32,36},... | collective-permute-start | bytes 393224 | tf_op jit(solution)/shard_map/ppermute | solution.py:292
  5.2 1.2 %slice_bitcast_fusion = (bf16[27,32,64]{2,1,0:T(8,128)(2,1)S(1)}, bf16[27,32,64]{2,1,0:T(8,128)(2,1)S(1)}, bf16[27,1,32,64]{3,2,1,0:T(8,128)(2,1)S(1)}, bf16[27,1,32,64]{3,2,1,0:T(8,128)(2,1)S(1)}) fusion(bf16[27,2,32,64]{3,2,1,0:T(8,128)(2,1)} %bitcast.36), kind=kLoop, calls=%fused_computation.16 | loop fusion | bytes 663552 | tf_op jit(solution)/shard_map/squeeze | solution.py:263
  6.4 0.1 fusion.2
  6.5 1.3 %collective-permute-start.5 = (bf16[448,128]{1,0:T(8,128)(2,1)S(1)}, bf16[448,128]{1,0:T(8,128)(2,1)S(1)}, u32[]{:S(2)}, u32[]{:S(2)}) collective-permute-start(bf16[448,128]{1,0:T(8,128)(2,1)S(1)} %bitcast.38), channel_id=1, source_target_pairs={{0,128},{64,192},{128,0},{192,64},{1,129},{65,193},{129,1},{193,65... | collective-permute-start | bytes 344072 | tf_op jit(solution)/shard_map/ppermute | solution.py:273
  7.8 0.1 pad_maximum_fusion.2.own
  7.9 0.9 collective-permute-start.4
  8.9 1.3 %collective-permute-start.1 = (bf16[16,64,128]{2,1,0:T(8,128)(2,1)S(1)}, bf16[16,64,128]{2,1,0:T(8,128)(2,1)S(1)}, u32[]{:S(2)}, u32[]{:S(2)}) collective-permute-start(bf16[16,64,128]{2,1,0:T(8,128)(2,1)S(1)} %pad_maximum_fusion.1.chip_rows), channel_id=1, source_target_pairs={{0,8},{8,16},{16,24},{24,32},{32,40},{40,48},{48,56},{12,4},{20,12... | collective-permute-start | bytes 786440 | tf_op jit(solution)/shard_map/ppermute | solution.py:289
  10.2 2.6 %collective-permute-done.5.half = bf16[448,128]{1,0:T(8,128)(2,1)S(1)} collective-permute-done((bf16[448,128]{1,0:T(8,128)(2,1)S(1)}, bf16[448,128]{1,0:T(8,128)(2,1)S(1)}, u32[]{:S(2)}, u32[]{:S(2)}) %collective-permute-start.5) | collective-permute-done | bytes 114720 | tf_op jit(solution)/shard_map/ppermute | solution.py:273
  12.8 1.4 %collective-permute-done.4.near = bf16[864,128]{1,0:T(8,128)(2,1)S(1)} collective-permute-done((bf16[864,128]{1,0:T(8,128)(2,1)S(1)}, bf16[864,128]{1,0:T(8,128)(2,1)S(1)}, u32[]{:S(2)}, u32[]{:S(2)}) %collective-permute-start.4) | collective-permute-done | bytes 221216 | tf_op jit(solution)/shard_map/ppermute | solution.py:264
  14.3 1.9 %collective-permute-start.6 = (bf16[1312,128]{1,0:T(8,128)(2,1)S(1)}, bf16[1312,128]{1,0:T(8,128)(2,1)S(1)}, u32[]{:S(2)}, u32[]{:S(2)}) collective-permute-start(bf16[1312,128]{1,0:T(8,128)(2,1)S(1)} %pad_maximum_fusion), channel_id=1, source_target_pairs={{0,4},{4,0},{8,12},{12,8},{16,20},{20,16},{24,28},{28,24},{32,36},... | collective-permute-start | bytes 1007624 | tf_op jit(solution)/shard_map/ppermute | solution.py:305
  16.3 1.3 %collective-permute-start.2 = (bf16[18,64,128]{2,1,0:T(8,128)(2,1)S(1)}, bf16[18,64,128]{2,1,0:T(8,128)(2,1)S(1)}, u32[]{:S(2)}, u32[]{:S(2)}) collective-permute-start(bf16[18,64,128]{2,1,0:T(8,128)(2,1)S(1)} %maximum_select_fusion), channel_id=1, source_target_pairs={{0,16},{8,24},{16,32},{24,40},{32,48},{40,56},{20,4},{28,12},{36,2... | collective-permute-start | bytes 884744 | tf_op jit(solution)/shard_map/ppermute | solution.py:289
  17.6 5.2 %collective-permute-start.3 = (bf16[16,64,128]{2,1,0:T(8,128)(2,1)S(1)}, bf16[16,64,128]{2,1,0:T(8,128)(2,1)S(1)}, u32[]{:S(2)}, u32[]{:S(2)}) collective-permute-start(bf16[16,64,128]{2,1,0:T(8,128)(2,1)S(1)} %collective-permute-done.1.near_rows), channel_id=1, source_target_pairs={{0,4},{4,0},{8,12},{12,8},{16,20},{20,16},{24,28},{28,24},{32,36},... | collective-permute-start | bytes 786440 | tf_op jit(solution)/shard_map/ppermute | solution.py:296
  22.8 0.6 stack.38.where_ref
  23.4 0.7 copy-done.6
  24.1 5.2 %weight_blocks.1 = (bf16[12,128,768]{2,1,0:T(8,128)(2,1)}, bf16[12,128,768]{2,1,0:T(8,128)(2,1)}) custom-call(s32[5]{0:T(128)} %stack.38.where_ref, bf16[864,128]{1,0:T(8,128)(2,1)} %copy-done.2, bf16[864,128]{1,0:T(8,128)(2,1)} %copy-done.3, bf16[448,128]{1,0:T(8,128)(2,1)} %copy-done.5, bf16[1312,128]{1,0:T(8,128)(2,1)} %copy-done.6), custom_call_target="tpu_custom_call" | custom-call | tf_op jit(solution)/shard_map/weight_blocks/pallas_call | solution.py:306
  29.5 1.6 %collective-permute-done.7.other_far = bf16[18,64,128]{2,1,0:T(8,128)(2,1)S(1)} collective-permute-done((bf16[18,64,128]{2,1,0:T(8,128)(2,1)S(1)}, bf16[18,64,128]{2,1,0:T(8,128)(2,1)S(1)}, u32[]{:S(2)}, u32[]{:S(2)}) %collective-permute-start.7) | collective-permute-done | bytes 294944 | tf_op jit(solution)/shard_map/ppermute | solution.py:315
  31.1 0.7 copy-done.8
  31.8 17.7 %sections.1 = (bf16[2,4,64,128]{3,2,1,0:T(8,128)(2,1)}, bf16[2,4,64,128]{3,2,1,0:T(8,128)(2,1)}, bf16[1024,128]{1,0:T(8,128)(2,1)}) custom-call(s32[5]{0:T(128)} %stack.38.where_ref, bf16[16,64,128]{2,1,0:T(8,128)(2,1)} %copy-done, bf16[16,64,128]{2,1,0:T(8,128)(2,1)} %copy-done.4, bf16[18,64,128]{2,1,0:T(8,128)(2,1)} %copy-done.7, ...), custom_call_target="tpu_custom_call" | custom-call | tf_op jit(solution)/shard_map/sections/pallas_call | solution.py:227
  49.6 14.2 %all-to-all-start = ((bf16[64,16,128]{2,1,0:T(8,128)(2,1)}), bf16[64,16,128]{2,1,0:T(8,128)(2,1)S(1)}, u32[]{:S(2)}, u32[]{:S(2)}) async-start(bf16[64,16,128]{2,1,0:T(8,128)(2,1)} %bitcast.37), calls=%async_computation | async-start | bytes 524288 | tf_op jit(solution)/shard_map/all_to_all | solution.py:324
  63.8 3.8 %collective-permute-start.8 = (bf16[2,4,64,128]{3,2,1,0:T(8,128)(2,1)}, bf16[2,4,64,128]{3,2,1,0:T(8,128)(2,1)S(1)}, u32[]{:S(2)}, u32[]{:S(2)}) collective-permute-start(bf16[2,4,64,128]{3,2,1,0:T(8,128)(2,1)} %get-tuple-element.18), channel_id=1, source_target_pairs={{0,0},{4,64},{64,4},{68,68},{1,1},{5,65},{65,5},{69,69},{2,2},{6,6... | collective-permute-start | bytes 393224 | tf_op jit(solution)/shard_map/ppermute | solution.py:332
  67.6 8.0 %all-to-all-done = bf16[64,16,128]{2,1,0:T(8,128)(2,1)S(1)} async-done(((bf16[64,16,128]{2,1,0:T(8,128)(2,1)}), bf16[64,16,128]{2,1,0:T(8,128)(2,1)S(1)}, u32[]{:S(2)}, u32[]{:S(2)}) %all-to-all-start) | async-done | bytes 262176 | tf_op jit(solution)/shard_map/all_to_all | solution.py:324
  75.7 4.6 %collective-permute-start.10 = (bf16[16,128]{1,0:T(8,128)(2,1)S(1)}, bf16[16,128]{1,0:T(8,128)(2,1)S(1)}, u32[]{:S(2)}, u32[]{:S(2)}) collective-permute-start(bf16[16,128]{1,0:T(8,128)(2,1)S(1)} %reduce_sum.12), channel_id=1, source_target_pairs={{0,0},{4,64},{64,4},{68,68},{1,1},{5,65},{65,5},{69,69},{2,2},{6,6... | collective-permute-start | bytes 12296 | tf_op jit(solution)/shard_map/ppermute | solution.py:327
  80.3 1.3 %collective-permute-done.10 = bf16[16,128]{1,0:T(8,128)(2,1)S(1)} collective-permute-done((bf16[16,128]{1,0:T(8,128)(2,1)S(1)}, bf16[16,128]{1,0:T(8,128)(2,1)S(1)}, u32[]{:S(2)}, u32[]{:S(2)}) %collective-permute-start.10) | collective-permute-done | bytes 4128 | tf_op jit(solution)/shard_map/ppermute | solution.py:327
  81.6 0.7 broadcast_in_dim.2
  82.4 4.6 %all-to-all-start.1 = ((bf16[64,16,128]{2,1,0:T(8,128)(2,1)}), bf16[64,16,128]{2,1,0:T(8,128)(2,1)S(1)}, u32[]{:S(2)}, u32[]{:S(2)}) async-start(bf16[64,16,128]{2,1,0:T(8,128)(2,1)} %broadcast_in_dim.2), calls=%async_computation.1 | async-start | bytes 524288 | tf_op jit(solution)/shard_map/all_to_all | solution.py:328
  87.1 0.8 copy.10
  87.8 0.8 copy.9
  88.6 10.4 %all-to-all-done.1 = bf16[64,16,128]{2,1,0:T(8,128)(2,1)S(1)} async-done(((bf16[64,16,128]{2,1,0:T(8,128)(2,1)}), bf16[64,16,128]{2,1,0:T(8,128)(2,1)S(1)}, u32[]{:S(2)}, u32[]{:S(2)}) %all-to-all-start.1) | async-done | bytes 262176 | tf_op jit(solution)/shard_map/all_to_all | solution.py:328
  99.0 0.7 copy-done.1
  99.7 2.0 %unpack.1 = f32[1,3,3,3,64,64]{5,4,3,2,1,0:T(8,128)} custom-call(bf16[1024,128]{1,0:T(8,128)(2,1)} %bitcast.32), custom_call_target="tpu_custom_call" | custom-call | tf_op jit(solution)/shard_map/unpack/pallas_call | solution.py:340
  (38 shorter events, 0.7 us)
Async XLA Ops:
  1.9 6.9 %collective-permute-start = (bf16[8,64,128]{2,1,0:T(8,128)(2,1)S(1)}, bf16[8,64,128]{2,1,0:T(8,128)(2,1)S(1)}, u32[]{:S(2)}, u32[]{:S(2)}) collective-permute-start(bf16[8,64,128]{2,1,0:T(8,128)(2,1)S(1)} %bitcast.35), channel_id=1, source_target_pairs={{0,4},{4,0},{8,12},{12,8},{16,20},{20,16},{24,28},{28,24},{32,36},... | collective-permute-start | bytes 393224 | tf_op jit(solution)/shard_map/ppermute | solution.py:292
  6.5 6.3 %collective-permute-start.5 = (bf16[448,128]{1,0:T(8,128)(2,1)S(1)}, bf16[448,128]{1,0:T(8,128)(2,1)S(1)}, u32[]{:S(2)}, u32[]{:S(2)}) collective-permute-start(bf16[448,128]{1,0:T(8,128)(2,1)S(1)} %bitcast.38), channel_id=1, source_target_pairs={{0,128},{64,192},{128,0},{192,64},{1,129},{65,193},{129,1},{193,65... | collective-permute-start | bytes 344072 | tf_op jit(solution)/shard_map/ppermute | solution.py:273
  7.9 15.5 %copy-start.2 = (bf16[864,128]{1,0:T(8,128)(2,1)}, bf16[864,128]{1,0:T(8,128)(2,1)S(1)}, u32[]{:S(2)}) copy-start(bf16[864,128]{1,0:T(8,128)(2,1)S(1)} %pad_maximum_fusion.2.own) | copy-start | bytes 663556
  7.9 6.3 %collective-permute-start.4 = (bf16[864,128]{1,0:T(8,128)(2,1)S(1)}, bf16[864,128]{1,0:T(8,128)(2,1)S(1)}, u32[]{:S(2)}, u32[]{:S(2)}) collective-permute-start(bf16[864,128]{1,0:T(8,128)(2,1)S(1)} %pad_maximum_fusion.2.own), channel_id=1, source_target_pairs={{0,64},{4,196},{64,128},{68,4},{128,192},{132,68},{192,0},{196,132... | collective-permute-start | bytes 663560 | tf_op jit(solution)/shard_map/ppermute | solution.py:264
  8.9 22.2 %copy-start = (bf16[16,64,128]{2,1,0:T(8,128)(2,1)}, bf16[16,64,128]{2,1,0:T(8,128)(2,1)S(1)}, u32[]{:S(2)}) copy-start(bf16[16,64,128]{2,1,0:T(8,128)(2,1)S(1)} %pad_maximum_fusion.1.chip_rows) | copy-start | bytes 786436
  8.9 7.3 %collective-permute-start.1 = (bf16[16,64,128]{2,1,0:T(8,128)(2,1)S(1)}, bf16[16,64,128]{2,1,0:T(8,128)(2,1)S(1)}, u32[]{:S(2)}, u32[]{:S(2)}) collective-permute-start(bf16[16,64,128]{2,1,0:T(8,128)(2,1)S(1)} %pad_maximum_fusion.1.chip_rows), channel_id=1, source_target_pairs={{0,8},{8,16},{16,24},{24,32},{32,40},{40,48},{48,56},{12,4},{20,12... | collective-permute-start | bytes 786440 | tf_op jit(solution)/shard_map/ppermute | solution.py:289
  12.8 10.6 %copy-start.5 = (bf16[448,128]{1,0:T(8,128)(2,1)}, bf16[448,128]{1,0:T(8,128)(2,1)S(1)}, u32[]{:S(2)}) copy-start(bf16[448,128]{1,0:T(8,128)(2,1)S(1)} %collective-permute-done.5.half) | copy-start | bytes 344068
  14.2 9.2 %copy-start.3 = (bf16[864,128]{1,0:T(8,128)(2,1)}, bf16[864,128]{1,0:T(8,128)(2,1)S(1)}, u32[]{:S(2)}) copy-start(bf16[864,128]{1,0:T(8,128)(2,1)S(1)} %collective-permute-done.4.near) | copy-start | bytes 663556
  14.3 9.1 %collective-permute-start.6 = (bf16[1312,128]{1,0:T(8,128)(2,1)S(1)}, bf16[1312,128]{1,0:T(8,128)(2,1)S(1)}, u32[]{:S(2)}, u32[]{:S(2)}) collective-permute-start(bf16[1312,128]{1,0:T(8,128)(2,1)S(1)} %pad_maximum_fusion), channel_id=1, source_target_pairs={{0,4},{4,0},{8,12},{12,8},{16,20},{20,16},{24,28},{28,24},{32,36},... | collective-permute-start | bytes 1007624 | tf_op jit(solution)/shard_map/ppermute | solution.py:305
  16.2 14.9 %copy-start.4 = (bf16[16,64,128]{2,1,0:T(8,128)(2,1)}, bf16[16,64,128]{2,1,0:T(8,128)(2,1)S(1)}, u32[]{:S(2)}) copy-start(bf16[16,64,128]{2,1,0:T(8,128)(2,1)S(1)} %collective-permute-done.1.near_rows) | copy-start | bytes 786436
  16.3 13.1 %collective-permute-start.2 = (bf16[18,64,128]{2,1,0:T(8,128)(2,1)S(1)}, bf16[18,64,128]{2,1,0:T(8,128)(2,1)S(1)}, u32[]{:S(2)}, u32[]{:S(2)}) collective-permute-start(bf16[18,64,128]{2,1,0:T(8,128)(2,1)S(1)} %maximum_select_fusion), channel_id=1, source_target_pairs={{0,16},{8,24},{16,32},{24,40},{32,48},{40,56},{20,4},{28,12},{36,2... | collective-permute-start | bytes 884744 | tf_op jit(solution)/shard_map/ppermute | solution.py:289
  17.6 11.8 %collective-permute-start.3 = (bf16[16,64,128]{2,1,0:T(8,128)(2,1)S(1)}, bf16[16,64,128]{2,1,0:T(8,128)(2,1)S(1)}, u32[]{:S(2)}, u32[]{:S(2)}) collective-permute-start(bf16[16,64,128]{2,1,0:T(8,128)(2,1)S(1)} %collective-permute-done.1.near_rows), channel_id=1, source_target_pairs={{0,4},{4,0},{8,12},{12,8},{16,20},{20,16},{24,28},{28,24},{32,36},... | collective-permute-start | bytes 786440 | tf_op jit(solution)/shard_map/ppermute | solution.py:296
  23.4 0.7 copy-start.6
  29.4 1.7 %copy-start.9 = (bf16[16,64,128]{2,1,0:T(8,128)(2,1)}, bf16[16,64,128]{2,1,0:T(8,128)(2,1)S(1)}, u32[]{:S(2)}) copy-start(bf16[16,64,128]{2,1,0:T(8,128)(2,1)S(1)} %collective-permute-done.3.other_near) | copy-start | bytes 786436
  29.4 1.7 %copy-start.7 = (bf16[18,64,128]{2,1,0:T(8,128)(2,1)}, bf16[18,64,128]{2,1,0:T(8,128)(2,1)S(1)}, u32[]{:S(2)}) copy-start(bf16[18,64,128]{2,1,0:T(8,128)(2,1)S(1)} %collective-permute-done.2.far_rows) | copy-start | bytes 884740
  29.4 1.7 %collective-permute-start.7 = (bf16[18,64,128]{2,1,0:T(8,128)(2,1)S(1)}, bf16[18,64,128]{2,1,0:T(8,128)(2,1)S(1)}, u32[]{:S(2)}, u32[]{:S(2)}) collective-permute-start(bf16[18,64,128]{2,1,0:T(8,128)(2,1)S(1)} %collective-permute-done.2.far_rows), channel_id=1, source_target_pairs={{0,4},{4,0},{8,12},{12,8},{16,20},{20,16},{24,28},{28,24},{32,36},... | collective-permute-start | bytes 884744 | tf_op jit(solution)/shard_map/ppermute | solution.py:315
  31.1 0.7 copy-start.8
  49.6 26.1 %all-to-all-start = ((bf16[64,16,128]{2,1,0:T(8,128)(2,1)}), bf16[64,16,128]{2,1,0:T(8,128)(2,1)S(1)}, u32[]{:S(2)}, u32[]{:S(2)}) async-start(bf16[64,16,128]{2,1,0:T(8,128)(2,1)} %bitcast.37), calls=%async_computation | async-start | bytes 524288 | tf_op jit(solution)/shard_map/all_to_all | solution.py:324
  63.8 23.2 %collective-permute-start.8 = (bf16[2,4,64,128]{3,2,1,0:T(8,128)(2,1)}, bf16[2,4,64,128]{3,2,1,0:T(8,128)(2,1)S(1)}, u32[]{:S(2)}, u32[]{:S(2)}) collective-permute-start(bf16[2,4,64,128]{3,2,1,0:T(8,128)(2,1)} %get-tuple-element.18), channel_id=1, source_target_pairs={{0,0},{4,64},{64,4},{68,68},{1,1},{5,65},{65,5},{69,69},{2,2},{6,6... | collective-permute-start | bytes 393224 | tf_op jit(solution)/shard_map/ppermute | solution.py:332
  67.5 19.4 %collective-permute-start.9 = (bf16[2,4,64,128]{3,2,1,0:T(8,128)(2,1)}, bf16[2,4,64,128]{3,2,1,0:T(8,128)(2,1)S(1)}, u32[]{:S(2)}, u32[]{:S(2)}) collective-permute-start(bf16[2,4,64,128]{3,2,1,0:T(8,128)(2,1)} %get-tuple-element.19), channel_id=1, source_target_pairs={{0,4},{4,68},{64,0},{68,64},{1,5},{5,69},{65,1},{69,65},{2,6},{6,7... | collective-permute-start | bytes 393224 | tf_op jit(solution)/shard_map/ppermute | solution.py:333
  75.7 5.9 %collective-permute-start.10 = (bf16[16,128]{1,0:T(8,128)(2,1)S(1)}, bf16[16,128]{1,0:T(8,128)(2,1)S(1)}, u32[]{:S(2)}, u32[]{:S(2)}) collective-permute-start(bf16[16,128]{1,0:T(8,128)(2,1)S(1)} %reduce_sum.12), channel_id=1, source_target_pairs={{0,0},{4,64},{64,4},{68,68},{1,1},{5,65},{65,5},{69,69},{2,2},{6,6... | collective-permute-start | bytes 12296 | tf_op jit(solution)/shard_map/ppermute | solution.py:327
  82.4 16.6 %all-to-all-start.1 = ((bf16[64,16,128]{2,1,0:T(8,128)(2,1)}), bf16[64,16,128]{2,1,0:T(8,128)(2,1)S(1)}, u32[]{:S(2)}, u32[]{:S(2)}) async-start(bf16[64,16,128]{2,1,0:T(8,128)(2,1)} %broadcast_in_dim.2), calls=%async_computation.1 | async-start | bytes 524288 | tf_op jit(solution)/shard_map/all_to_all | solution.py:328
  99.0 0.7 copy-start.1

commit v6 on v5

--- a/solution.py
+++ b/solution.py
@@ -57,13 +57,21 @@
 def sections_kernel(
     where_ref,
     chip_rows, near_rows, far_rows, other_near, other_far,
-    wf_ref, wb_ref,
+    wf_hbm, wb_hbm,
     even_ref, odd_ref, wg_ref,
-    h_ref, a1_ref, a2_ref, p1_ref, p2_ref, g_ref, gp1_ref, gp2_ref,
+    h_ref, a1_ref, a2_ref, p1_ref, p2_ref, g_ref, gp1_ref, gp2_ref, wf_ref, wb_ref, sems,
 ):
     mine = where_ref[0]
     first_row = where_ref[1]
     core = where_ref[2]
+    slabs = [
+        pltpu.make_async_copy(
+            wf_hbm.at[3 * n:3 * n + 3], wf_ref.at[3 * n:3 * n + 3], sems.at[n]
+        )
+        for n in range(DEPTH)
+    ] + [pltpu.make_async_copy(wb_hbm, wb_ref, sems.at[DEPTH])]
+    for slab_copy in slabs:
+        slab_copy.start()
     h_ref[0, 24:32] = chip_rows[0:8]
     g_ref[DEPTH, 24:32] = chip_rows[8:16]
     for one, two, lower in ((near_rows, far_rows, core), (other_near, other_far, 1 - core)):
@@ -104,13 +112,13 @@
                 for one in range(2):
                     finish(row + at + 2 * half + one, product[one * C:(one + 1) * C, half * WID:(half + 1) * WID])
 
-    def conv_loop(reach, source, slab, finish):
+    def conv_loop(reach, source, slab, finish, needed=None):
         start = OFF - reach
         count = -(-(8 + 2 * reach) // 4) * 4
         parts = -(-count // 28)
         size = -(-count // (4 * parts)) * 4
         for part in range(parts):
-            @pl.when(mine >= 0)
+            @pl.when(mine >= 0 if needed is None else needed)
             def _(part=part):
                 conv_rows(start + size * part, min(size, count - size * part), source, slab, finish)
 
@@ -148,7 +156,9 @@
         return carry
 
     for section in range(DEPTH):
+        slabs[section].wait()
         forward(section, 0)
+    slabs[DEPTH].wait()
 
     def kernel_grad(layer, source, grads):
         wide_in, wide_out = [], []
@@ -186,10 +196,10 @@
             result = g_ref[section + 1, row].astype(F32) + values
             g_ref[section, row] = jnp.where(inside(row), result, 0.0).astype(BF)
 
-        conv_loop(2 + 3 * section, g_ref.at[section + 1], wb_ref.at[slot + 2], through(p2_ref, gp2_ref))
-        conv_loop(1 + 3 * section, gp2_ref.at[section], wb_ref.at[slot + 1], through(p1_ref, gp1_ref))
-
-        conv_loop(3 * section, gp1_ref.at[section], wb_ref.at[slot], residual)
+        conv_loop(2 + 3 * section, g_ref.at[section + 1], wb_ref.at[slot + 2], through(p2_ref, gp2_ref), section >= mine)
+        conv_loop(1 + 3 * section, gp2_ref.at[section], wb_ref.at[slot + 1], through(p1_ref, gp1_ref), section >= mine)
+
+        conv_loop(3 * section, gp1_ref.at[section], wb_ref.at[slot], residual, section >= mine)
         return carry
 
     for turn in range(DEPTH):
@@ -231,7 +241,9 @@
             jax.ShapeDtypeStruct((2, 4, C, WID), BF),
             jax.ShapeDtypeStruct((1024, 128), BF),
         ],
-        in_specs=[pl.BlockSpec(memory_space=pltpu.SMEM)] + vmem(7),
+        in_specs=[pl.BlockSpec(memory_space=pltpu.SMEM)]
+        + vmem(5)
+        + [pl.BlockSpec(memory_space=pl.ANY)] * 2,
         out_specs=vmem(3),
         scratch_shapes=[
             pltpu.VMEM((DEPTH + 1,) + window, BF),
@@ -242,6 +254,9 @@
             pltpu.VMEM((DEPTH + 1,) + window, BF),
             pltpu.VMEM((DEPTH,) + window, BF),
             pltpu.VMEM((DEPTH,) + window, BF),
+            pltpu.VMEM((12, 128, 768), BF),
+            pltpu.VMEM((12, 128, 768), BF),
+            pltpu.SemaphoreType.DMA((DEPTH + 1,)),
         ],
         compiler_params=pltpu.CompilerParams(vmem_limit_bytes=62 * 1024 * 1024),
         name="sections",
@@ -302,6 +317,7 @@
         ),
         2,
     )
+    near, where = lax.optimization_barrier((near, where))
     other_weights = lax.ppermute(jnp.concatenate([near, half]), BAND, swapped)
     fwd, bwd = pl.pallas_call(
         weight_blocks_kernel,

time: 103 us -> 102 us (level)
  starting transfers between devices: 42.4 us -> 44.6 us
  waiting for transfers between devices: 25.4 us -> 23.6 us
    all_to_all x1, waiting for transfers between devices: 8.03 us -> 6 us  [on_device(): lax.all_to_all(grads.reshape(64, 16, 128), ('rep', 'side', 'z'), 0, 0, ti...]
    ppermute x1, starting transfers between devices: 3.75 us -> 4.92 us  [on_device(): even = lax.ppermute(even, ('side', 'core'), turned)]
  transfers between devices with their start and end apart: 13 -> 13, of which waited for: 7 -> 6; matrix products, arithmetic and copies ran while one was open for 5% -> 5% of each run, Pallas kernels for 5% -> 5%
where the time goes in v6:
time: 102 us; the launch traced here: 101 us
  starting transfers between devices  44.6 us (44%)
  Pallas kernels  24 us (24%)
  waiting for transfers between devices  23.6 us (23%)
  local copies, waits for them, and re-layouts  7.32 us (7%)
    pallas_call x1, Pallas kernels, sections_call(): pl.pallas_call(sections_kernel, out_shape=[jax.ShapeDtypeStruct((2, 4, C,...  16.8 us
    all_to_all x1, starting transfers between devices, on_device(): lax.all_to_all(grads.reshape(64, 16, 128), ('rep', 'side', 'z'), 0, 0, ti...  14.8 us
    all_to_all x1, waiting for transfers between devices, on_device(): lax.all_to_all(jnp.broadcast_to(total[None], (64, 16, 128)), ('rep', 'cor...  10.4 us
    all_to_all x1, waiting for transfers between devices, on_device(): lax.all_to_all(grads.reshape(64, 16, 128), ('rep', 'side', 'z'), 0, 0, ti...  6 us
    ppermute x1, starting transfers between devices, on_device(): other_near = lax.ppermute(near_rows, BAND, swapped)  5.62 us
    ppermute x1, starting transfers between devices, on_device(): total = lax.ppermute(total, ('side', 'core'), turned)  5.6 us
    pallas_call x1, Pallas kernels, on_device(): pl.pallas_call(weight_blocks_kernel, out_shape=[jax.ShapeDtypeStruct((12,...  5.23 us
    ppermute x1, starting transfers between devices, on_device(): even = lax.ppermute(even, ('side', 'core'), turned)  4.92 us
  transfers between devices with their start and end apart: 13, of which 6 were waited for; matrix products, arithmetic and copies ran while one was open for 5% of the time, Pallas kernels for 5%

profile of v6, /device:TPU:1, one launch (start us, length us, event | category | flops | bytes accessed | tf_op | source)
XLA Modules:
  0.0 101.1 jit_solution(9654559726877812788)
XLA Ops:
  0.6 1.0 %fusion.7 = (bf16[1,64,4,128]{3,2,1,0:T(4,128)(2,1)S(1)}, bf16[1,64,4,128]{3,2,1,0:T(4,128)(2,1)S(1)}, bf16[1,64,4,128]{3,2,1,0:T(4,128)(2,1)S(1)}, bf16[1,64,4,128]{3,2,1,0:T(4,128)(2,1)S(1)}) fusion(bf16[2,64,4,128]{3,2,1,0:T(4,128)(2,1)} %param.3, bf16[2,64,4,128]{3,2,1,0:T(4,128)(2,1)} %param.5), kind=kLoop, calls=%fused_computation.22 | loop fusion | bytes 524288 | tf_op jit(solution)/shard_map/slice | solution.py:293
  1.7 0.2 fusion
  1.9 3.3 %collective-permute-start.1 = (bf16[8,64,128]{2,1,0:T(8,128)(2,1)S(1)}, bf16[8,64,128]{2,1,0:T(8,128)(2,1)S(1)}, u32[]{:S(2)}, u32[]{:S(2)}) collective-permute-start(bf16[8,64,128]{2,1,0:T(8,128)(2,1)S(1)} %bitcast.35), channel_id=1, source_target_pairs={{0,4},{4,0},{8,12},{12,8},{16,20},{20,16},{24,28},{28,24},{32,36},... | collective-permute-start | bytes 393224 | tf_op jit(solution)/shard_map/ppermute | solution.py:307
  5.2 1.2 %slice_bitcast_fusion = (bf16[27,32,64]{2,1,0:T(8,128)(2,1)S(1)}, bf16[27,32,64]{2,1,0:T(8,128)(2,1)S(1)}, bf16[27,1,32,64]{3,2,1,0:T(8,128)(2,1)S(1)}, bf16[27,1,32,64]{3,2,1,0:T(8,128)(2,1)S(1)}) fusion(bf16[27,2,32,64]{3,2,1,0:T(8,128)(2,1)} %bitcast.36), kind=kLoop, calls=%fused_computation.16 | loop fusion | bytes 663552 | tf_op jit(solution)/shard_map/squeeze | solution.py:278
  6.4 0.1 pad_maximum_fusion.2.own
  6.5 1.1 %collective-permute-start = (bf16[864,128]{1,0:T(8,128)(2,1)S(1)}, bf16[864,128]{1,0:T(8,128)(2,1)S(1)}, u32[]{:S(2)}, u32[]{:S(2)}) collective-permute-start(bf16[864,128]{1,0:T(8,128)(2,1)S(1)} %pad_maximum_fusion.2.own), channel_id=1, source_target_pairs={{0,64},{4,196},{64,128},{68,4},{128,192},{132,68},{192,0},{196,132... | collective-permute-start | bytes 663560 | tf_op jit(solution)/shard_map/ppermute | solution.py:279
  7.6 0.1 fusion.2
  7.7 0.4 collective-permute-start.5
  8.3 1.3 %collective-permute-start.2 = (bf16[16,64,128]{2,1,0:T(8,128)(2,1)S(1)}, bf16[16,64,128]{2,1,0:T(8,128)(2,1)S(1)}, u32[]{:S(2)}, u32[]{:S(2)}) collective-permute-start(bf16[16,64,128]{2,1,0:T(8,128)(2,1)S(1)} %pad_maximum_fusion.1.chip_rows), channel_id=1, source_target_pairs={{0,8},{8,16},{16,24},{24,32},{32,40},{40,48},{48,56},{12,4},{20,12... | collective-permute-start | bytes 786440 | tf_op jit(solution)/shard_map/ppermute | solution.py:304
  9.6 0.6 stack.38.where_ref
  10.2 1.4 %collective-permute-done.near = bf16[864,128]{1,0:T(8,128)(2,1)S(1)} collective-permute-done((bf16[864,128]{1,0:T(8,128)(2,1)S(1)}, bf16[864,128]{1,0:T(8,128)(2,1)S(1)}, u32[]{:S(2)}, u32[]{:S(2)}) %collective-permute-start) | collective-permute-done | bytes 221216 | tf_op jit(solution)/shard_map/ppermute | solution.py:279
  11.7 2.9 %collective-permute-done.5.half = bf16[448,128]{1,0:T(8,128)(2,1)S(1)} collective-permute-done((bf16[448,128]{1,0:T(8,128)(2,1)S(1)}, bf16[448,128]{1,0:T(8,128)(2,1)S(1)}, u32[]{:S(2)}, u32[]{:S(2)}) %collective-permute-start.5) | collective-permute-done | bytes 114720 | tf_op jit(solution)/shard_map/ppermute | solution.py:288
  14.6 1.8 %collective-permute-start.6 = (bf16[1312,128]{1,0:T(8,128)(2,1)S(1)}, bf16[1312,128]{1,0:T(8,128)(2,1)S(1)}, u32[]{:S(2)}, u32[]{:S(2)}) collective-permute-start(bf16[1312,128]{1,0:T(8,128)(2,1)S(1)} %pad_maximum_fusion), channel_id=1, source_target_pairs={{0,4},{4,0},{8,12},{12,8},{16,20},{20,16},{24,28},{28,24},{32,36},... | collective-permute-start | bytes 1007624 | tf_op jit(solution)/shard_map/ppermute | solution.py:321
  16.4 1.3 %collective-permute-start.3 = (bf16[18,64,128]{2,1,0:T(8,128)(2,1)S(1)}, bf16[18,64,128]{2,1,0:T(8,128)(2,1)S(1)}, u32[]{:S(2)}, u32[]{:S(2)}) collective-permute-start(bf16[18,64,128]{2,1,0:T(8,128)(2,1)S(1)} %maximum_select_fusion), channel_id=1, source_target_pairs={{0,16},{8,24},{16,32},{24,40},{32,48},{40,56},{20,4},{28,12},{36,2... | collective-permute-start | bytes 884744 | tf_op jit(solution)/shard_map/ppermute | solution.py:304
  17.7 5.6 %collective-permute-start.4 = (bf16[16,64,128]{2,1,0:T(8,128)(2,1)S(1)}, bf16[16,64,128]{2,1,0:T(8,128)(2,1)S(1)}, u32[]{:S(2)}, u32[]{:S(2)}) collective-permute-start(bf16[16,64,128]{2,1,0:T(8,128)(2,1)S(1)} %collective-permute-done.2.near_rows), channel_id=1, source_target_pairs={{0,4},{4,0},{8,12},{12,8},{16,20},{20,16},{24,28},{28,24},{32,36},... | collective-permute-start | bytes 786440 | tf_op jit(solution)/shard_map/ppermute | solution.py:311
  23.4 0.7 copy-done.6
  24.1 5.2 %weight_blocks.1 = (bf16[12,128,768]{2,1,0:T(8,128)(2,1)}, bf16[12,128,768]{2,1,0:T(8,128)(2,1)}) custom-call(s32[5]{0:T(128)} %stack.38.where_ref, bf16[864,128]{1,0:T(8,128)(2,1)} %copy-done.2, bf16[864,128]{1,0:T(8,128)(2,1)} %copy-done.3, bf16[448,128]{1,0:T(8,128)(2,1)} %copy-done.5, bf16[1312,128]{1,0:T(8,128)(2,1)} %copy-done.6), custom_call_target="tpu_custom_call" | custom-call | tf_op jit(solution)/shard_map/weight_blocks/pallas_call | solution.py:322
  29.5 1.5 %collective-permute-done.7.other_far = bf16[18,64,128]{2,1,0:T(8,128)(2,1)S(1)} collective-permute-done((bf16[18,64,128]{2,1,0:T(8,128)(2,1)S(1)}, bf16[18,64,128]{2,1,0:T(8,128)(2,1)S(1)}, u32[]{:S(2)}, u32[]{:S(2)}) %collective-permute-start.7) | collective-permute-done | bytes 294944 | tf_op jit(solution)/shard_map/ppermute | solution.py:331
  31.1 0.7 copy-done.8
  31.8 16.8 %sections.1 = (bf16[2,4,64,128]{3,2,1,0:T(8,128)(2,1)}, bf16[2,4,64,128]{3,2,1,0:T(8,128)(2,1)}, bf16[1024,128]{1,0:T(8,128)(2,1)}) custom-call(s32[5]{0:T(128)} %stack.38.where_ref, bf16[16,64,128]{2,1,0:T(8,128)(2,1)} %copy-done, bf16[16,64,128]{2,1,0:T(8,128)(2,1)} %copy-done.4, bf16[18,64,128]{2,1,0:T(8,128)(2,1)} %copy-done.7, ...), custom_call_target="tpu_custom_call" | custom-call | tf_op jit(solution)/shard_map/sections/pallas_call | solution.py:237
  48.6 14.8 %all-to-all-start = ((bf16[64,16,128]{2,1,0:T(8,128)(2,1)}), bf16[64,16,128]{2,1,0:T(8,128)(2,1)S(1)}, u32[]{:S(2)}, u32[]{:S(2)}) async-start(bf16[64,16,128]{2,1,0:T(8,128)(2,1)} %bitcast.37), calls=%async_computation | async-start | bytes 524288 | tf_op jit(solution)/shard_map/all_to_all | solution.py:340
  63.4 4.9 %collective-permute-start.8 = (bf16[2,4,64,128]{3,2,1,0:T(8,128)(2,1)}, bf16[2,4,64,128]{3,2,1,0:T(8,128)(2,1)S(1)}, u32[]{:S(2)}, u32[]{:S(2)}) collective-permute-start(bf16[2,4,64,128]{3,2,1,0:T(8,128)(2,1)} %get-tuple-element.22), channel_id=1, source_target_pairs={{0,0},{4,64},{64,4},{68,68},{1,1},{5,65},{65,5},{69,69},{2,2},{6,6... | collective-permute-start | bytes 393224 | tf_op jit(solution)/shard_map/ppermute | solution.py:348
  68.5 6.0 %all-to-all-done = bf16[64,16,128]{2,1,0:T(8,128)(2,1)S(1)} async-done(((bf16[64,16,128]{2,1,0:T(8,128)(2,1)}), bf16[64,16,128]{2,1,0:T(8,128)(2,1)S(1)}, u32[]{:S(2)}, u32[]{:S(2)}) %all-to-all-start) | async-done | bytes 262176 | tf_op jit(solution)/shard_map/all_to_all | solution.py:340
  74.5 5.6 %collective-permute-start.10 = (bf16[16,128]{1,0:T(8,128)(2,1)S(1)}, bf16[16,128]{1,0:T(8,128)(2,1)S(1)}, u32[]{:S(2)}, u32[]{:S(2)}) collective-permute-start(bf16[16,128]{1,0:T(8,128)(2,1)S(1)} %reduce_sum.12), channel_id=1, source_target_pairs={{0,0},{4,64},{64,4},{68,68},{1,1},{5,65},{65,5},{69,69},{2,2},{6,6... | collective-permute-start | bytes 12296 | tf_op jit(solution)/shard_map/ppermute | solution.py:343
  80.1 1.3 %collective-permute-done.10 = bf16[16,128]{1,0:T(8,128)(2,1)S(1)} collective-permute-done((bf16[16,128]{1,0:T(8,128)(2,1)S(1)}, bf16[16,128]{1,0:T(8,128)(2,1)S(1)}, u32[]{:S(2)}, u32[]{:S(2)}) %collective-permute-start.10) | collective-permute-done | bytes 4128 | tf_op jit(solution)/shard_map/ppermute | solution.py:343
  81.4 0.7 broadcast_in_dim.2
  82.2 4.2 %all-to-all-start.1 = ((bf16[64,16,128]{2,1,0:T(8,128)(2,1)}), bf16[64,16,128]{2,1,0:T(8,128)(2,1)S(1)}, u32[]{:S(2)}, u32[]{:S(2)}) async-start(bf16[64,16,128]{2,1,0:T(8,128)(2,1)} %broadcast_in_dim.2), calls=%async_computation.1 | async-start | bytes 524288 | tf_op jit(solution)/shard_map/all_to_all | solution.py:344
  86.5 0.8 copy.10
  87.3 0.8 copy.9
  88.0 10.4 %all-to-all-done.1 = bf16[64,16,128]{2,1,0:T(8,128)(2,1)S(1)} async-done(((bf16[64,16,128]{2,1,0:T(8,128)(2,1)}), bf16[64,16,128]{2,1,0:T(8,128)(2,1)S(1)}, u32[]{:S(2)}, u32[]{:S(2)}) %all-to-all-start.1) | async-done | bytes 262176 | tf_op jit(solution)/shard_map/all_to_all | solution.py:344
  98.4 0.7 copy-done.1
  99.1 2.0 %unpack.1 = f32[1,3,3,3,64,64]{5,4,3,2,1,0:T(8,128)} custom-call(bf16[1024,128]{1,0:T(8,128)(2,1)} %bitcast.32), custom_call_target="tpu_custom_call" | custom-call | tf_op jit(solution)/shard_map/unpack/pallas_call | solution.py:356
  (38 shorter events, 0.6 us)
Async XLA Ops:
  1.9 6.3 %collective-permute-start.1 = (bf16[8,64,128]{2,1,0:T(8,128)(2,1)S(1)}, bf16[8,64,128]{2,1,0:T(8,128)(2,1)S(1)}, u32[]{:S(2)}, u32[]{:S(2)}) collective-permute-start(bf16[8,64,128]{2,1,0:T(8,128)(2,1)S(1)} %bitcast.35), channel_id=1, source_target_pairs={{0,4},{4,0},{8,12},{12,8},{16,20},{20,16},{24,28},{28,24},{32,36},... | collective-permute-start | bytes 393224 | tf_op jit(solution)/shard_map/ppermute | solution.py:307
  6.5 16.9 %copy-start.2 = (bf16[864,128]{1,0:T(8,128)(2,1)}, bf16[864,128]{1,0:T(8,128)(2,1)S(1)}, u32[]{:S(2)}) copy-start(bf16[864,128]{1,0:T(8,128)(2,1)S(1)} %pad_maximum_fusion.2.own) | copy-start | bytes 663556
  6.5 5.2 %collective-permute-start = (bf16[864,128]{1,0:T(8,128)(2,1)S(1)}, bf16[864,128]{1,0:T(8,128)(2,1)S(1)}, u32[]{:S(2)}, u32[]{:S(2)}) collective-permute-start(bf16[864,128]{1,0:T(8,128)(2,1)S(1)} %pad_maximum_fusion.2.own), channel_id=1, source_target_pairs={{0,64},{4,196},{64,128},{68,4},{128,192},{132,68},{192,0},{196,132... | collective-permute-start | bytes 663560 | tf_op jit(solution)/shard_map/ppermute | solution.py:279
  7.7 6.8 %collective-permute-start.5 = (bf16[448,128]{1,0:T(8,128)(2,1)S(1)}, bf16[448,128]{1,0:T(8,128)(2,1)S(1)}, u32[]{:S(2)}, u32[]{:S(2)}) collective-permute-start(bf16[448,128]{1,0:T(8,128)(2,1)S(1)} %bitcast.38), channel_id=1, source_target_pairs={{0,128},{64,192},{128,0},{192,64},{1,129},{65,193},{129,1},{193,65... | collective-permute-start | bytes 344072 | tf_op jit(solution)/shard_map/ppermute | solution.py:288
  8.3 22.8 %copy-start = (bf16[16,64,128]{2,1,0:T(8,128)(2,1)}, bf16[16,64,128]{2,1,0:T(8,128)(2,1)S(1)}, u32[]{:S(2)}) copy-start(bf16[16,64,128]{2,1,0:T(8,128)(2,1)S(1)} %pad_maximum_fusion.1.chip_rows) | copy-start | bytes 786436
  8.3 8.0 %collective-permute-start.2 = (bf16[16,64,128]{2,1,0:T(8,128)(2,1)S(1)}, bf16[16,64,128]{2,1,0:T(8,128)(2,1)S(1)}, u32[]{:S(2)}, u32[]{:S(2)}) collective-permute-start(bf16[16,64,128]{2,1,0:T(8,128)(2,1)S(1)} %pad_maximum_fusion.1.chip_rows), channel_id=1, source_target_pairs={{0,8},{8,16},{16,24},{24,32},{32,40},{40,48},{48,56},{12,4},{20,12... | collective-permute-start | bytes 786440 | tf_op jit(solution)/shard_map/ppermute | solution.py:304
  11.7 11.7 %copy-start.3 = (bf16[864,128]{1,0:T(8,128)(2,1)}, bf16[864,128]{1,0:T(8,128)(2,1)S(1)}, u32[]{:S(2)}) copy-start(bf16[864,128]{1,0:T(8,128)(2,1)S(1)} %collective-permute-done.near) | copy-start | bytes 663556
  14.5 8.8 %copy-start.5 = (bf16[448,128]{1,0:T(8,128)(2,1)}, bf16[448,128]{1,0:T(8,128)(2,1)S(1)}, u32[]{:S(2)}) copy-start(bf16[448,128]{1,0:T(8,128)(2,1)S(1)} %collective-permute-done.5.half) | copy-start | bytes 344068
  14.6 8.8 %collective-permute-start.6 = (bf16[1312,128]{1,0:T(8,128)(2,1)S(1)}, bf16[1312,128]{1,0:T(8,128)(2,1)S(1)}, u32[]{:S(2)}, u32[]{:S(2)}) collective-permute-start(bf16[1312,128]{1,0:T(8,128)(2,1)S(1)} %pad_maximum_fusion), channel_id=1, source_target_pairs={{0,4},{4,0},{8,12},{12,8},{16,20},{20,16},{24,28},{28,24},{32,36},... | collective-permute-start | bytes 1007624 | tf_op jit(solution)/shard_map/ppermute | solution.py:321
  16.3 14.7 %copy-start.4 = (bf16[16,64,128]{2,1,0:T(8,128)(2,1)}, bf16[16,64,128]{2,1,0:T(8,128)(2,1)S(1)}, u32[]{:S(2)}) copy-start(bf16[16,64,128]{2,1,0:T(8,128)(2,1)S(1)} %collective-permute-done.2.near_rows) | copy-start | bytes 786436
  16.4 12.9 %collective-permute-start.3 = (bf16[18,64,128]{2,1,0:T(8,128)(2,1)S(1)}, bf16[18,64,128]{2,1,0:T(8,128)(2,1)S(1)}, u32[]{:S(2)}, u32[]{:S(2)}) collective-permute-start(bf16[18,64,128]{2,1,0:T(8,128)(2,1)S(1)} %maximum_select_fusion), channel_id=1, source_target_pairs={{0,16},{8,24},{16,32},{24,40},{32,48},{40,56},{20,4},{28,12},{36,2... | collective-permute-start | bytes 884744 | tf_op jit(solution)/shard_map/ppermute | solution.py:304
  17.7 11.6 %collective-permute-start.4 = (bf16[16,64,128]{2,1,0:T(8,128)(2,1)S(1)}, bf16[16,64,128]{2,1,0:T(8,128)(2,1)S(1)}, u32[]{:S(2)}, u32[]{:S(2)}) collective-permute-start(bf16[16,64,128]{2,1,0:T(8,128)(2,1)S(1)} %collective-permute-done.2.near_rows), channel_id=1, source_target_pairs={{0,4},{4,0},{8,12},{12,8},{16,20},{20,16},{24,28},{28,24},{32,36},... | collective-permute-start | bytes 786440 | tf_op jit(solution)/shard_map/ppermute | solution.py:311
  23.4 0.7 copy-start.6
  29.3 1.7 %copy-start.9 = (bf16[16,64,128]{2,1,0:T(8,128)(2,1)}, bf16[16,64,128]{2,1,0:T(8,128)(2,1)S(1)}, u32[]{:S(2)}) copy-start(bf16[16,64,128]{2,1,0:T(8,128)(2,1)S(1)} %collective-permute-done.4.other_near) | copy-start | bytes 786436
  29.4 1.7 %copy-start.7 = (bf16[18,64,128]{2,1,0:T(8,128)(2,1)}, bf16[18,64,128]{2,1,0:T(8,128)(2,1)S(1)}, u32[]{:S(2)}) copy-start(bf16[18,64,128]{2,1,0:T(8,128)(2,1)S(1)} %collective-permute-done.3.far_rows) | copy-start | bytes 884740
  29.4 1.7 %collective-permute-start.7 = (bf16[18,64,128]{2,1,0:T(8,128)(2,1)S(1)}, bf16[18,64,128]{2,1,0:T(8,128)(2,1)S(1)}, u32[]{:S(2)}, u32[]{:S(2)}) collective-permute-start(bf16[18,64,128]{2,1,0:T(8,128)(2,1)S(1)} %collective-permute-done.3.far_rows), channel_id=1, source_target_pairs={{0,4},{4,0},{8,12},{12,8},{16,20},{20,16},{24,28},{28,24},{32,36},... | collective-permute-start | bytes 884744 | tf_op jit(solution)/shard_map/ppermute | solution.py:331
  31.1 0.7 copy-start.8
  48.6 25.9 %all-to-all-start = ((bf16[64,16,128]{2,1,0:T(8,128)(2,1)}), bf16[64,16,128]{2,1,0:T(8,128)(2,1)S(1)}, u32[]{:S(2)}, u32[]{:S(2)}) async-start(bf16[64,16,128]{2,1,0:T(8,128)(2,1)} %bitcast.37), calls=%async_computation | async-start | bytes 524288 | tf_op jit(solution)/shard_map/all_to_all | solution.py:340
  63.4 23.0 %collective-permute-start.8 = (bf16[2,4,64,128]{3,2,1,0:T(8,128)(2,1)}, bf16[2,4,64,128]{3,2,1,0:T(8,128)(2,1)S(1)}, u32[]{:S(2)}, u32[]{:S(2)}) collective-permute-start(bf16[2,4,64,128]{3,2,1,0:T(8,128)(2,1)} %get-tuple-element.22), channel_id=1, source_target_pairs={{0,0},{4,64},{64,4},{68,68},{1,1},{5,65},{65,5},{69,69},{2,2},{6,6... | collective-permute-start | bytes 393224 | tf_op jit(solution)/shard_map/ppermute | solution.py:348
  68.4 18.0 %collective-permute-start.9 = (bf16[2,4,64,128]{3,2,1,0:T(8,128)(2,1)}, bf16[2,4,64,128]{3,2,1,0:T(8,128)(2,1)S(1)}, u32[]{:S(2)}, u32[]{:S(2)}) collective-permute-start(bf16[2,4,64,128]{3,2,1,0:T(8,128)(2,1)} %get-tuple-element.23), channel_id=1, source_target_pairs={{0,4},{4,68},{64,0},{68,64},{1,5},{5,69},{65,1},{69,65},{2,6},{6,7... | collective-permute-start | bytes 393224 | tf_op jit(solution)/shard_map/ppermute | solution.py:349
  74.5 6.9 %collective-permute-start.10 = (bf16[16,128]{1,0:T(8,128)(2,1)S(1)}, bf16[16,128]{1,0:T(8,128)(2,1)S(1)}, u32[]{:S(2)}, u32[]{:S(2)}) collective-permute-start(bf16[16,128]{1,0:T(8,128)(2,1)S(1)} %reduce_sum.12), channel_id=1, source_target_pairs={{0,0},{4,64},{64,4},{68,68},{1,1},{5,65},{65,5},{69,69},{2,2},{6,6... | collective-permute-start | bytes 12296 | tf_op jit(solution)/shard_map/ppermute | solution.py:343
  82.2 16.3 %all-to-all-start.1 = ((bf16[64,16,128]{2,1,0:T(8,128)(2,1)}), bf16[64,16,128]{2,1,0:T(8,128)(2,1)S(1)}, u32[]{:S(2)}, u32[]{:S(2)}) async-start(bf16[64,16,128]{2,1,0:T(8,128)(2,1)} %broadcast_in_dim.2), calls=%async_computation.1 | async-start | bytes 524288 | tf_op jit(solution)/shard_map/all_to_all | solution.py:344
  98.4 0.7 copy-start.1

commit v7 on v6

--- a/solution.py
+++ b/solution.py
@@ -337,12 +337,12 @@
         bwd,
     )
 
-    parts = lax.all_to_all(grads.reshape(64, 16, 128), ("rep", "side", "z"), 0, 0, tiled=True)
+    parts = lax.all_to_all(grads.reshape(64, 16, 128), ("rep", "z", "side"), 0, 0, tiled=True)
     total = jnp.sum(parts.astype(F32), axis=0).astype(BF)
     turned = [(2 * q + c, 2 * c + q) for q in range(2) for c in range(2)]
     total = lax.ppermute(total, ("side", "core"), turned)
     summed = lax.all_to_all(
-        jnp.broadcast_to(total[None], (64, 16, 128)), ("rep", "core", "z"), 0, 0, tiled=True
+        jnp.broadcast_to(total[None], (64, 16, 128)), ("rep", "z", "core"), 0, 0, tiled=True
     ).reshape(1024, 128)
 
     even = lax.ppermute(even, ("side", "core"), turned)

time: 102 us -> 102 us (level)
  waiting for transfers between devices: 23.6 us -> 22.4 us
    all_to_all x2, waiting for transfers between devices: 16.4 us -> 15.3 us  [the longest x1 10.4 us: on_device(): lax.all_to_all(jnp.broadcast_to(total[None], (64, 16, 128)), ('rep', 'z',...]
where the time goes in v7:
time: 102 us; the launch traced here: 101 us
  starting transfers between devices  45.6 us (45%)
  Pallas kernels  24 us (24%)
  waiting for transfers between devices  22.4 us (22%)
  local copies, waits for them, and re-layouts  7.32 us (7%)
    pallas_call x1, Pallas kernels, sections_call(): pl.pallas_call(sections_kernel, out_shape=[jax.ShapeDtypeStruct((2, 4, C,...  16.8 us
    all_to_all x1, starting transfers between devices, on_device(): lax.all_to_all(grads.reshape(64, 16, 128), ('rep', 'z', 'side'), 0, 0, ti...  14.8 us
    all_to_all x1, waiting for transfers between devices, on_device(): lax.all_to_all(jnp.broadcast_to(total[None], (64, 16, 128)), ('rep', 'z',...  10.4 us
    ppermute x1, starting transfers between devices, on_device(): total = lax.ppermute(total, ('side', 'core'), turned)  5.97 us
    ppermute x1, starting transfers between devices, on_device(): other_near = lax.ppermute(near_rows, BAND, swapped)  5.62 us
    pallas_call x1, Pallas kernels, on_device(): pl.pallas_call(weight_blocks_kernel, out_shape=[jax.ShapeDtypeStruct((12,...  5.23 us
    all_to_all x1, waiting for transfers between devices, on_device(): lax.all_to_all(grads.reshape(64, 16, 128), ('rep', 'z', 'side'), 0, 0, ti...  4.92 us
    ppermute x1, starting transfers between devices, on_device(): even = lax.ppermute(even, ('side', 'core'), turned)  4.91 us
  transfers between devices with their start and end apart: 13, of which 6 were waited for; matrix products, arithmetic and copies ran while one was open for 5% of the time, Pallas kernels for 5%

profile of v7, /device:TPU:1, one launch (start us, length us, event | category | flops | bytes accessed | tf_op | source)
XLA Modules:
  0.0 101.0 jit_solution(11416108705075400728)
XLA Ops:
  0.6 1.0 %fusion.7 = (bf16[1,64,4,128]{3,2,1,0:T(4,128)(2,1)S(1)}, bf16[1,64,4,128]{3,2,1,0:T(4,128)(2,1)S(1)}, bf16[1,64,4,128]{3,2,1,0:T(4,128)(2,1)S(1)}, bf16[1,64,4,128]{3,2,1,0:T(4,128)(2,1)S(1)}) fusion(bf16[2,64,4,128]{3,2,1,0:T(4,128)(2,1)} %param.3, bf16[2,64,4,128]{3,2,1,0:T(4,128)(2,1)} %param.5), kind=kLoop, calls=%fused_computation.22 | loop fusion | bytes 524288 | tf_op jit(solution)/shard_map/slice | solution.py:293
  1.7 0.2 fusion
  1.9 3.3 %collective-permute-start.1 = (bf16[8,64,128]{2,1,0:T(8,128)(2,1)S(1)}, bf16[8,64,128]{2,1,0:T(8,128)(2,1)S(1)}, u32[]{:S(2)}, u32[]{:S(2)}) collective-permute-start(bf16[8,64,128]{2,1,0:T(8,128)(2,1)S(1)} %bitcast.35), channel_id=1, source_target_pairs={{0,4},{4,0},{8,12},{12,8},{16,20},{20,16},{24,28},{28,24},{32,36},... | collective-permute-start | bytes 393224 | tf_op jit(solution)/shard_map/ppermute | solution.py:307
  5.2 1.2 %slice_bitcast_fusion = (bf16[27,32,64]{2,1,0:T(8,128)(2,1)S(1)}, bf16[27,32,64]{2,1,0:T(8,128)(2,1)S(1)}, bf16[27,1,32,64]{3,2,1,0:T(8,128)(2,1)S(1)}, bf16[27,1,32,64]{3,2,1,0:T(8,128)(2,1)S(1)}) fusion(bf16[27,2,32,64]{3,2,1,0:T(8,128)(2,1)} %bitcast.36), kind=kLoop, calls=%fused_computation.16 | loop fusion | bytes 663552 | tf_op jit(solution)/shard_map/squeeze | solution.py:278
  6.4 0.1 pad_maximum_fusion.2.own
  6.5 1.1 %collective-permute-start = (bf16[864,128]{1,0:T(8,128)(2,1)S(1)}, bf16[864,128]{1,0:T(8,128)(2,1)S(1)}, u32[]{:S(2)}, u32[]{:S(2)}) collective-permute-start(bf16[864,128]{1,0:T(8,128)(2,1)S(1)} %pad_maximum_fusion.2.own), channel_id=1, source_target_pairs={{0,64},{4,196},{64,128},{68,4},{128,192},{132,68},{192,0},{196,132... | collective-permute-start | bytes 663560 | tf_op jit(solution)/shard_map/ppermute | solution.py:279
  7.6 0.1 fusion.2
  7.7 0.4 collective-permute-start.5
  8.3 1.3 %collective-permute-start.2 = (bf16[16,64,128]{2,1,0:T(8,128)(2,1)S(1)}, bf16[16,64,128]{2,1,0:T(8,128)(2,1)S(1)}, u32[]{:S(2)}, u32[]{:S(2)}) collective-permute-start(bf16[16,64,128]{2,1,0:T(8,128)(2,1)S(1)} %pad_maximum_fusion.1.chip_rows), channel_id=1, source_target_pairs={{0,8},{8,16},{16,24},{24,32},{32,40},{40,48},{48,56},{12,4},{20,12... | collective-permute-start | bytes 786440 | tf_op jit(solution)/shard_map/ppermute | solution.py:304
  9.6 0.6 stack.38.where_ref
  10.2 1.4 %collective-permute-done.near = bf16[864,128]{1,0:T(8,128)(2,1)S(1)} collective-permute-done((bf16[864,128]{1,0:T(8,128)(2,1)S(1)}, bf16[864,128]{1,0:T(8,128)(2,1)S(1)}, u32[]{:S(2)}, u32[]{:S(2)}) %collective-permute-start) | collective-permute-done | bytes 221216 | tf_op jit(solution)/shard_map/ppermute | solution.py:279
  11.7 2.9 %collective-permute-done.5.half = bf16[448,128]{1,0:T(8,128)(2,1)S(1)} collective-permute-done((bf16[448,128]{1,0:T(8,128)(2,1)S(1)}, bf16[448,128]{1,0:T(8,128)(2,1)S(1)}, u32[]{:S(2)}, u32[]{:S(2)}) %collective-permute-start.5) | collective-permute-done | bytes 114720 | tf_op jit(solution)/shard_map/ppermute | solution.py:288
  14.6 1.8 %collective-permute-start.6 = (bf16[1312,128]{1,0:T(8,128)(2,1)S(1)}, bf16[1312,128]{1,0:T(8,128)(2,1)S(1)}, u32[]{:S(2)}, u32[]{:S(2)}) collective-permute-start(bf16[1312,128]{1,0:T(8,128)(2,1)S(1)} %pad_maximum_fusion), channel_id=1, source_target_pairs={{0,4},{4,0},{8,12},{12,8},{16,20},{20,16},{24,28},{28,24},{32,36},... | collective-permute-start | bytes 1007624 | tf_op jit(solution)/shard_map/ppermute | solution.py:321
  16.4 1.3 %collective-permute-start.3 = (bf16[18,64,128]{2,1,0:T(8,128)(2,1)S(1)}, bf16[18,64,128]{2,1,0:T(8,128)(2,1)S(1)}, u32[]{:S(2)}, u32[]{:S(2)}) collective-permute-start(bf16[18,64,128]{2,1,0:T(8,128)(2,1)S(1)} %maximum_select_fusion), channel_id=1, source_target_pairs={{0,16},{8,24},{16,32},{24,40},{32,48},{40,56},{20,4},{28,12},{36,2... | collective-permute-start | bytes 884744 | tf_op jit(solution)/shard_map/ppermute | solution.py:304
  17.7 5.6 %collective-permute-start.4 = (bf16[16,64,128]{2,1,0:T(8,128)(2,1)S(1)}, bf16[16,64,128]{2,1,0:T(8,128)(2,1)S(1)}, u32[]{:S(2)}, u32[]{:S(2)}) collective-permute-start(bf16[16,64,128]{2,1,0:T(8,128)(2,1)S(1)} %collective-permute-done.2.near_rows), channel_id=1, source_target_pairs={{0,4},{4,0},{8,12},{12,8},{16,20},{20,16},{24,28},{28,24},{32,36},... | collective-permute-start | bytes 786440 | tf_op jit(solution)/shard_map/ppermute | solution.py:311
  23.4 0.7 copy-done.6
  24.1 5.2 %weight_blocks.1 = (bf16[12,128,768]{2,1,0:T(8,128)(2,1)}, bf16[12,128,768]{2,1,0:T(8,128)(2,1)}) custom-call(s32[5]{0:T(128)} %stack.38.where_ref, bf16[864,128]{1,0:T(8,128)(2,1)} %copy-done.2, bf16[864,128]{1,0:T(8,128)(2,1)} %copy-done.3, bf16[448,128]{1,0:T(8,128)(2,1)} %copy-done.5, bf16[1312,128]{1,0:T(8,128)(2,1)} %copy-done.6), custom_call_target="tpu_custom_call" | custom-call | tf_op jit(solution)/shard_map/weight_blocks/pallas_call | solution.py:322
  29.5 1.5 %collective-permute-done.7.other_far = bf16[18,64,128]{2,1,0:T(8,128)(2,1)S(1)} collective-permute-done((bf16[18,64,128]{2,1,0:T(8,128)(2,1)S(1)}, bf16[18,64,128]{2,1,0:T(8,128)(2,1)S(1)}, u32[]{:S(2)}, u32[]{:S(2)}) %collective-permute-start.7) | collective-permute-done | bytes 294944 | tf_op jit(solution)/shard_map/ppermute | solution.py:331
  31.1 0.7 copy-done.8
  31.8 16.8 %sections.1 = (bf16[2,4,64,128]{3,2,1,0:T(8,128)(2,1)}, bf16[2,4,64,128]{3,2,1,0:T(8,128)(2,1)}, bf16[1024,128]{1,0:T(8,128)(2,1)}) custom-call(s32[5]{0:T(128)} %stack.38.where_ref, bf16[16,64,128]{2,1,0:T(8,128)(2,1)} %copy-done, bf16[16,64,128]{2,1,0:T(8,128)(2,1)} %copy-done.4, bf16[18,64,128]{2,1,0:T(8,128)(2,1)} %copy-done.7, ...), custom_call_target="tpu_custom_call" | custom-call | tf_op jit(solution)/shard_map/sections/pallas_call | solution.py:237
  48.6 14.8 %all-to-all-start = ((bf16[64,16,128]{2,1,0:T(8,128)(2,1)}), bf16[64,16,128]{2,1,0:T(8,128)(2,1)S(1)}, u32[]{:S(2)}, u32[]{:S(2)}) async-start(bf16[64,16,128]{2,1,0:T(8,128)(2,1)} %bitcast.37), calls=%async_computation | async-start | bytes 524288 | tf_op jit(solution)/shard_map/all_to_all | solution.py:340
  63.4 4.9 %collective-permute-start.8 = (bf16[2,4,64,128]{3,2,1,0:T(8,128)(2,1)}, bf16[2,4,64,128]{3,2,1,0:T(8,128)(2,1)S(1)}, u32[]{:S(2)}, u32[]{:S(2)}) collective-permute-start(bf16[2,4,64,128]{3,2,1,0:T(8,128)(2,1)} %get-tuple-element.22), channel_id=1, source_target_pairs={{0,0},{4,64},{64,4},{68,68},{1,1},{5,65},{65,5},{69,69},{2,2},{6,6... | collective-permute-start | bytes 393224 | tf_op jit(solution)/shard_map/ppermute | solution.py:348
  68.5 4.9 %all-to-all-done = bf16[64,16,128]{2,1,0:T(8,128)(2,1)S(1)} async-done(((bf16[64,16,128]{2,1,0:T(8,128)(2,1)}), bf16[64,16,128]{2,1,0:T(8,128)(2,1)S(1)}, u32[]{:S(2)}, u32[]{:S(2)}) %all-to-all-start) | async-done | bytes 262176 | tf_op jit(solution)/shard_map/all_to_all | solution.py:340
  73.5 6.0 %collective-permute-start.10 = (bf16[16,128]{1,0:T(8,128)(2,1)S(1)}, bf16[16,128]{1,0:T(8,128)(2,1)S(1)}, u32[]{:S(2)}, u32[]{:S(2)}) collective-permute-start(bf16[16,128]{1,0:T(8,128)(2,1)S(1)} %reduce_sum.12), channel_id=1, source_target_pairs={{0,0},{4,64},{64,4},{68,68},{1,1},{5,65},{65,5},{69,69},{2,2},{6,6... | collective-permute-start | bytes 12296 | tf_op jit(solution)/shard_map/ppermute | solution.py:343
  79.4 1.3 %collective-permute-done.10 = bf16[16,128]{1,0:T(8,128)(2,1)S(1)} collective-permute-done((bf16[16,128]{1,0:T(8,128)(2,1)S(1)}, bf16[16,128]{1,0:T(8,128)(2,1)S(1)}, u32[]{:S(2)}, u32[]{:S(2)}) %collective-permute-start.10) | collective-permute-done | bytes 4128 | tf_op jit(solution)/shard_map/ppermute | solution.py:343
  80.7 0.7 broadcast_in_dim.2
  81.4 4.9 %all-to-all-start.1 = ((bf16[64,16,128]{2,1,0:T(8,128)(2,1)}), bf16[64,16,128]{2,1,0:T(8,128)(2,1)S(1)}, u32[]{:S(2)}, u32[]{:S(2)}) async-start(bf16[64,16,128]{2,1,0:T(8,128)(2,1)} %broadcast_in_dim.2), calls=%async_computation.1 | async-start | bytes 524288 | tf_op jit(solution)/shard_map/all_to_all | solution.py:344
  86.5 0.8 copy.10
  87.2 0.8 copy.9
  88.0 10.4 %all-to-all-done.1 = bf16[64,16,128]{2,1,0:T(8,128)(2,1)S(1)} async-done(((bf16[64,16,128]{2,1,0:T(8,128)(2,1)}), bf16[64,16,128]{2,1,0:T(8,128)(2,1)S(1)}, u32[]{:S(2)}, u32[]{:S(2)}) %all-to-all-start.1) | async-done | bytes 262176 | tf_op jit(solution)/shard_map/all_to_all | solution.py:344
  98.4 0.7 copy-done.1
  99.1 2.0 %unpack.1 = f32[1,3,3,3,64,64]{5,4,3,2,1,0:T(8,128)} custom-call(bf16[1024,128]{1,0:T(8,128)(2,1)} %bitcast.32), custom_call_target="tpu_custom_call" | custom-call | tf_op jit(solution)/shard_map/unpack/pallas_call | solution.py:356
  (38 shorter events, 0.6 us)
Async XLA Ops:
  1.9 6.3 %collective-permute-start.1 = (bf16[8,64,128]{2,1,0:T(8,128)(2,1)S(1)}, bf16[8,64,128]{2,1,0:T(8,128)(2,1)S(1)}, u32[]{:S(2)}, u32[]{:S(2)}) collective-permute-start(bf16[8,64,128]{2,1,0:T(8,128)(2,1)S(1)} %bitcast.35), channel_id=1, source_target_pairs={{0,4},{4,0},{8,12},{12,8},{16,20},{20,16},{24,28},{28,24},{32,36},... | collective-permute-start | bytes 393224 | tf_op jit(solution)/shard_map/ppermute | solution.py:307
  6.5 16.9 %copy-start.2 = (bf16[864,128]{1,0:T(8,128)(2,1)}, bf16[864,128]{1,0:T(8,128)(2,1)S(1)}, u32[]{:S(2)}) copy-start(bf16[864,128]{1,0:T(8,128)(2,1)S(1)} %pad_maximum_fusion.2.own) | copy-start | bytes 663556
  6.5 5.2 %collective-permute-start = (bf16[864,128]{1,0:T(8,128)(2,1)S(1)}, bf16[864,128]{1,0:T(8,128)(2,1)S(1)}, u32[]{:S(2)}, u32[]{:S(2)}) collective-permute-start(bf16[864,128]{1,0:T(8,128)(2,1)S(1)} %pad_maximum_fusion.2.own), channel_id=1, source_target_pairs={{0,64},{4,196},{64,128},{68,4},{128,192},{132,68},{192,0},{196,132... | collective-permute-start | bytes 663560 | tf_op jit(solution)/shard_map/ppermute | solution.py:279
  7.7 6.8 %collective-permute-start.5 = (bf16[448,128]{1,0:T(8,128)(2,1)S(1)}, bf16[448,128]{1,0:T(8,128)(2,1)S(1)}, u32[]{:S(2)}, u32[]{:S(2)}) collective-permute-start(bf16[448,128]{1,0:T(8,128)(2,1)S(1)} %bitcast.38), channel_id=1, source_target_pairs={{0,128},{64,192},{128,0},{192,64},{1,129},{65,193},{129,1},{193,65... | collective-permute-start | bytes 344072 | tf_op jit(solution)/shard_map/ppermute | solution.py:288
  8.3 22.8 %copy-start = (bf16[16,64,128]{2,1,0:T(8,128)(2,1)}, bf16[16,64,128]{2,1,0:T(8,128)(2,1)S(1)}, u32[]{:S(2)}) copy-start(bf16[16,64,128]{2,1,0:T(8,128)(2,1)S(1)} %pad_maximum_fusion.1.chip_rows) | copy-start | bytes 786436
  8.3 8.0 %collective-permute-start.2 = (bf16[16,64,128]{2,1,0:T(8,128)(2,1)S(1)}, bf16[16,64,128]{2,1,0:T(8,128)(2,1)S(1)}, u32[]{:S(2)}, u32[]{:S(2)}) collective-permute-start(bf16[16,64,128]{2,1,0:T(8,128)(2,1)S(1)} %pad_maximum_fusion.1.chip_rows), channel_id=1, source_target_pairs={{0,8},{8,16},{16,24},{24,32},{32,40},{40,48},{48,56},{12,4},{20,12... | collective-permute-start | bytes 786440 | tf_op jit(solution)/shard_map/ppermute | solution.py:304
  11.7 11.7 %copy-start.3 = (bf16[864,128]{1,0:T(8,128)(2,1)}, bf16[864,128]{1,0:T(8,128)(2,1)S(1)}, u32[]{:S(2)}) copy-start(bf16[864,128]{1,0:T(8,128)(2,1)S(1)} %collective-permute-done.near) | copy-start | bytes 663556
  14.5 8.8 %copy-start.5 = (bf16[448,128]{1,0:T(8,128)(2,1)}, bf16[448,128]{1,0:T(8,128)(2,1)S(1)}, u32[]{:S(2)}) copy-start(bf16[448,128]{1,0:T(8,128)(2,1)S(1)} %collective-permute-done.5.half) | copy-start | bytes 344068
  14.6 8.8 %collective-permute-start.6 = (bf16[1312,128]{1,0:T(8,128)(2,1)S(1)}, bf16[1312,128]{1,0:T(8,128)(2,1)S(1)}, u32[]{:S(2)}, u32[]{:S(2)}) collective-permute-start(bf16[1312,128]{1,0:T(8,128)(2,1)S(1)} %pad_maximum_fusion), channel_id=1, source_target_pairs={{0,4},{4,0},{8,12},{12,8},{16,20},{20,16},{24,28},{28,24},{32,36},... | collective-permute-start | bytes 1007624 | tf_op jit(solution)/shard_map/ppermute | solution.py:321
  16.3 14.7 %copy-start.4 = (bf16[16,64,128]{2,1,0:T(8,128)(2,1)}, bf16[16,64,128]{2,1,0:T(8,128)(2,1)S(1)}, u32[]{:S(2)}) copy-start(bf16[16,64,128]{2,1,0:T(8,128)(2,1)S(1)} %collective-permute-done.2.near_rows) | copy-start | bytes 786436
  16.4 12.9 %collective-permute-start.3 = (bf16[18,64,128]{2,1,0:T(8,128)(2,1)S(1)}, bf16[18,64,128]{2,1,0:T(8,128)(2,1)S(1)}, u32[]{:S(2)}, u32[]{:S(2)}) collective-permute-start(bf16[18,64,128]{2,1,0:T(8,128)(2,1)S(1)} %maximum_select_fusion), channel_id=1, source_target_pairs={{0,16},{8,24},{16,32},{24,40},{32,48},{40,56},{20,4},{28,12},{36,2... | collective-permute-start | bytes 884744 | tf_op jit(solution)/shard_map/ppermute | solution.py:304
  17.7 11.6 %collective-permute-start.4 = (bf16[16,64,128]{2,1,0:T(8,128)(2,1)S(1)}, bf16[16,64,128]{2,1,0:T(8,128)(2,1)S(1)}, u32[]{:S(2)}, u32[]{:S(2)}) collective-permute-start(bf16[16,64,128]{2,1,0:T(8,128)(2,1)S(1)} %collective-permute-done.2.near_rows), channel_id=1, source_target_pairs={{0,4},{4,0},{8,12},{12,8},{16,20},{20,16},{24,28},{28,24},{32,36},... | collective-permute-start | bytes 786440 | tf_op jit(solution)/shard_map/ppermute | solution.py:311
  23.4 0.7 copy-start.6
  29.3 1.7 %copy-start.9 = (bf16[16,64,128]{2,1,0:T(8,128)(2,1)}, bf16[16,64,128]{2,1,0:T(8,128)(2,1)S(1)}, u32[]{:S(2)}) copy-start(bf16[16,64,128]{2,1,0:T(8,128)(2,1)S(1)} %collective-permute-done.4.other_near) | copy-start | bytes 786436
  29.4 1.7 %copy-start.7 = (bf16[18,64,128]{2,1,0:T(8,128)(2,1)}, bf16[18,64,128]{2,1,0:T(8,128)(2,1)S(1)}, u32[]{:S(2)}) copy-start(bf16[18,64,128]{2,1,0:T(8,128)(2,1)S(1)} %collective-permute-done.3.far_rows) | copy-start | bytes 884740
  29.4 1.7 %collective-permute-start.7 = (bf16[18,64,128]{2,1,0:T(8,128)(2,1)S(1)}, bf16[18,64,128]{2,1,0:T(8,128)(2,1)S(1)}, u32[]{:S(2)}, u32[]{:S(2)}) collective-permute-start(bf16[18,64,128]{2,1,0:T(8,128)(2,1)S(1)} %collective-permute-done.3.far_rows), channel_id=1, source_target_pairs={{0,4},{4,0},{8,12},{12,8},{16,20},{20,16},{24,28},{28,24},{32,36},... | collective-permute-start | bytes 884744 | tf_op jit(solution)/shard_map/ppermute | solution.py:331
  31.1 0.7 copy-start.8
  48.6 24.8 %all-to-all-start = ((bf16[64,16,128]{2,1,0:T(8,128)(2,1)}), bf16[64,16,128]{2,1,0:T(8,128)(2,1)S(1)}, u32[]{:S(2)}, u32[]{:S(2)}) async-start(bf16[64,16,128]{2,1,0:T(8,128)(2,1)} %bitcast.37), calls=%async_computation | async-start | bytes 524288 | tf_op jit(solution)/shard_map/all_to_all | solution.py:340
  63.4 22.9 %collective-permute-start.8 = (bf16[2,4,64,128]{3,2,1,0:T(8,128)(2,1)}, bf16[2,4,64,128]{3,2,1,0:T(8,128)(2,1)S(1)}, u32[]{:S(2)}, u32[]{:S(2)}) collective-permute-start(bf16[2,4,64,128]{3,2,1,0:T(8,128)(2,1)} %get-tuple-element.22), channel_id=1, source_target_pairs={{0,0},{4,64},{64,4},{68,68},{1,1},{5,65},{65,5},{69,69},{2,2},{6,6... | collective-permute-start | bytes 393224 | tf_op jit(solution)/shard_map/ppermute | solution.py:348
  68.4 18.0 %collective-permute-start.9 = (bf16[2,4,64,128]{3,2,1,0:T(8,128)(2,1)}, bf16[2,4,64,128]{3,2,1,0:T(8,128)(2,1)S(1)}, u32[]{:S(2)}, u32[]{:S(2)}) collective-permute-start(bf16[2,4,64,128]{3,2,1,0:T(8,128)(2,1)} %get-tuple-element.23), channel_id=1, source_target_pairs={{0,4},{4,68},{64,0},{68,64},{1,5},{5,69},{65,1},{69,65},{2,6},{6,7... | collective-permute-start | bytes 393224 | tf_op jit(solution)/shard_map/ppermute | solution.py:349
  73.5 7.3 %collective-permute-start.10 = (bf16[16,128]{1,0:T(8,128)(2,1)S(1)}, bf16[16,128]{1,0:T(8,128)(2,1)S(1)}, u32[]{:S(2)}, u32[]{:S(2)}) collective-permute-start(bf16[16,128]{1,0:T(8,128)(2,1)S(1)} %reduce_sum.12), channel_id=1, source_target_pairs={{0,0},{4,64},{64,4},{68,68},{1,1},{5,65},{65,5},{69,69},{2,2},{6,6... | collective-permute-start | bytes 12296 | tf_op jit(solution)/shard_map/ppermute | solution.py:343
  81.4 16.9 %all-to-all-start.1 = ((bf16[64,16,128]{2,1,0:T(8,128)(2,1)}), bf16[64,16,128]{2,1,0:T(8,128)(2,1)S(1)}, u32[]{:S(2)}, u32[]{:S(2)}) async-start(bf16[64,16,128]{2,1,0:T(8,128)(2,1)} %broadcast_in_dim.2), calls=%async_computation.1 | async-start | bytes 524288 | tf_op jit(solution)/shard_map/all_to_all | solution.py:344
  98.4 0.7 copy-start.1

commit v8 on v7

--- a/solution.py
+++ b/solution.py
@@ -337,12 +337,12 @@
         bwd,
     )
 
-    parts = lax.all_to_all(grads.reshape(64, 16, 128), ("rep", "z", "side"), 0, 0, tiled=True)
+    parts = lax.all_to_all(grads.reshape(64, 16, 128), ("z", "rep", "side"), 0, 0, tiled=True)
     total = jnp.sum(parts.astype(F32), axis=0).astype(BF)
     turned = [(2 * q + c, 2 * c + q) for q in range(2) for c in range(2)]
     total = lax.ppermute(total, ("side", "core"), turned)
     summed = lax.all_to_all(
-        jnp.broadcast_to(total[None], (64, 16, 128)), ("rep", "z", "core"), 0, 0, tiled=True
+        jnp.broadcast_to(total[None], (64, 16, 128)), ("z", "rep", "core"), 0, 0, tiled=True
     ).reshape(1024, 128)
 
     even = lax.ppermute(even, ("side", "core"), turned)

time: 102 us -> 102 us (level)
  waiting for transfers between devices: 22.4 us -> 23.9 us
    all_to_all x2, waiting for transfers between devices: 15.3 us -> 16.8 us  [the longest x1 11.2 us: on_device(): lax.all_to_all(jnp.broadcast_to(total[None], (64, 16, 128)), ('z', 'rep',...]
where the time goes in v8:
time: 102 us
  starting transfers between devices  45.1 us (44%)
  Pallas kernels  24 us (24%)
  waiting for transfers between devices  23.9 us (23%)
  local copies, waits for them, and re-layouts  7.32 us (7%)
    pallas_call x1, Pallas kernels, sections_call(): pl.pallas_call(sections_kernel, out_shape=[jax.ShapeDtypeStruct((2, 4, C,...  16.8 us
    all_to_all x1, starting transfers between devices, on_device(): lax.all_to_all(grads.reshape(64, 16, 128), ('z', 'rep', 'side'), 0, 0, ti...  14.8 us
    all_to_all x1, waiting for transfers between devices, on_device(): lax.all_to_all(jnp.broadcast_to(total[None], (64, 16, 128)), ('z', 'rep',...  11.2 us
    ppermute x1, starting transfers between devices, on_device(): total = lax.ppermute(total, ('side', 'core'), turned)  6.14 us
    ppermute x1, starting transfers between devices, on_device(): other_near = lax.ppermute(near_rows, BAND, swapped)  5.62 us
    all_to_all x1, waiting for transfers between devices, on_device(): lax.all_to_all(grads.reshape(64, 16, 128), ('z', 'rep', 'side'), 0, 0, ti...  5.59 us
    pallas_call x1, Pallas kernels, on_device(): pl.pallas_call(weight_blocks_kernel, out_shape=[jax.ShapeDtypeStruct((12,...  5.23 us
    ppermute x1, starting transfers between devices, on_device(): even = lax.ppermute(even, ('side', 'core'), turned)  4.91 us
  transfers between devices with their start and end apart: 13, of which 6 were waited for; matrix products, arithmetic and copies ran while one was open for 5% of the time, Pallas kernels for 5%

profile of v8, /device:TPU:1, one launch (start us, length us, event | category | flops | bytes accessed | tf_op | source)
XLA Modules:
  0.0 102.0 jit_solution(2194267666029571648)
XLA Ops:
  0.6 1.0 %fusion.7 = (bf16[1,64,4,128]{3,2,1,0:T(4,128)(2,1)S(1)}, bf16[1,64,4,128]{3,2,1,0:T(4,128)(2,1)S(1)}, bf16[1,64,4,128]{3,2,1,0:T(4,128)(2,1)S(1)}, bf16[1,64,4,128]{3,2,1,0:T(4,128)(2,1)S(1)}) fusion(bf16[2,64,4,128]{3,2,1,0:T(4,128)(2,1)} %param.3, bf16[2,64,4,128]{3,2,1,0:T(4,128)(2,1)} %param.5), kind=kLoop, calls=%fused_computation.22 | loop fusion | bytes 524288 | tf_op jit(solution)/shard_map/slice | solution.py:293
  1.7 0.2 fusion
  1.9 3.3 %collective-permute-start.1 = (bf16[8,64,128]{2,1,0:T(8,128)(2,1)S(1)}, bf16[8,64,128]{2,1,0:T(8,128)(2,1)S(1)}, u32[]{:S(2)}, u32[]{:S(2)}) collective-permute-start(bf16[8,64,128]{2,1,0:T(8,128)(2,1)S(1)} %bitcast.35), channel_id=1, source_target_pairs={{0,4},{4,0},{8,12},{12,8},{16,20},{20,16},{24,28},{28,24},{32,36},... | collective-permute-start | bytes 393224 | tf_op jit(solution)/shard_map/ppermute | solution.py:307
  5.2 1.2 %slice_bitcast_fusion = (bf16[27,32,64]{2,1,0:T(8,128)(2,1)S(1)}, bf16[27,32,64]{2,1,0:T(8,128)(2,1)S(1)}, bf16[27,1,32,64]{3,2,1,0:T(8,128)(2,1)S(1)}, bf16[27,1,32,64]{3,2,1,0:T(8,128)(2,1)S(1)}) fusion(bf16[27,2,32,64]{3,2,1,0:T(8,128)(2,1)} %bitcast.36), kind=kLoop, calls=%fused_computation.16 | loop fusion | bytes 663552 | tf_op jit(solution)/shard_map/squeeze | solution.py:278
  6.4 0.1 pad_maximum_fusion.2.own
  6.5 1.1 %collective-permute-start = (bf16[864,128]{1,0:T(8,128)(2,1)S(1)}, bf16[864,128]{1,0:T(8,128)(2,1)S(1)}, u32[]{:S(2)}, u32[]{:S(2)}) collective-permute-start(bf16[864,128]{1,0:T(8,128)(2,1)S(1)} %pad_maximum_fusion.2.own), channel_id=1, source_target_pairs={{0,64},{4,196},{64,128},{68,4},{128,192},{132,68},{192,0},{196,132... | collective-permute-start | bytes 663560 | tf_op jit(solution)/shard_map/ppermute | solution.py:279
  7.6 0.1 fusion.2
  7.7 0.4 collective-permute-start.5
  8.3 1.3 %collective-permute-start.2 = (bf16[16,64,128]{2,1,0:T(8,128)(2,1)S(1)}, bf16[16,64,128]{2,1,0:T(8,128)(2,1)S(1)}, u32[]{:S(2)}, u32[]{:S(2)}) collective-permute-start(bf16[16,64,128]{2,1,0:T(8,128)(2,1)S(1)} %pad_maximum_fusion.1.chip_rows), channel_id=1, source_target_pairs={{0,8},{8,16},{16,24},{24,32},{32,40},{40,48},{48,56},{12,4},{20,12... | collective-permute-start | bytes 786440 | tf_op jit(solution)/shard_map/ppermute | solution.py:304
  9.6 0.6 stack.38.where_ref
  10.2 1.4 %collective-permute-done.near = bf16[864,128]{1,0:T(8,128)(2,1)S(1)} collective-permute-done((bf16[864,128]{1,0:T(8,128)(2,1)S(1)}, bf16[864,128]{1,0:T(8,128)(2,1)S(1)}, u32[]{:S(2)}, u32[]{:S(2)}) %collective-permute-start) | collective-permute-done | bytes 221216 | tf_op jit(solution)/shard_map/ppermute | solution.py:279
  11.7 2.9 %collective-permute-done.5.half = bf16[448,128]{1,0:T(8,128)(2,1)S(1)} collective-permute-done((bf16[448,128]{1,0:T(8,128)(2,1)S(1)}, bf16[448,128]{1,0:T(8,128)(2,1)S(1)}, u32[]{:S(2)}, u32[]{:S(2)}) %collective-permute-start.5) | collective-permute-done | bytes 114720 | tf_op jit(solution)/shard_map/ppermute | solution.py:288
  14.6 1.8 %collective-permute-start.6 = (bf16[1312,128]{1,0:T(8,128)(2,1)S(1)}, bf16[1312,128]{1,0:T(8,128)(2,1)S(1)}, u32[]{:S(2)}, u32[]{:S(2)}) collective-permute-start(bf16[1312,128]{1,0:T(8,128)(2,1)S(1)} %pad_maximum_fusion), channel_id=1, source_target_pairs={{0,4},{4,0},{8,12},{12,8},{16,20},{20,16},{24,28},{28,24},{32,36},... | collective-permute-start | bytes 1007624 | tf_op jit(solution)/shard_map/ppermute | solution.py:321
  16.4 1.3 %collective-permute-start.3 = (bf16[18,64,128]{2,1,0:T(8,128)(2,1)S(1)}, bf16[18,64,128]{2,1,0:T(8,128)(2,1)S(1)}, u32[]{:S(2)}, u32[]{:S(2)}) collective-permute-start(bf16[18,64,128]{2,1,0:T(8,128)(2,1)S(1)} %maximum_select_fusion), channel_id=1, source_target_pairs={{0,16},{8,24},{16,32},{24,40},{32,48},{40,56},{20,4},{28,12},{36,2... | collective-permute-start | bytes 884744 | tf_op jit(solution)/shard_map/ppermute | solution.py:304
  17.7 5.6 %collective-permute-start.4 = (bf16[16,64,128]{2,1,0:T(8,128)(2,1)S(1)}, bf16[16,64,128]{2,1,0:T(8,128)(2,1)S(1)}, u32[]{:S(2)}, u32[]{:S(2)}) collective-permute-start(bf16[16,64,128]{2,1,0:T(8,128)(2,1)S(1)} %collective-permute-done.2.near_rows), channel_id=1, source_target_pairs={{0,4},{4,0},{8,12},{12,8},{16,20},{20,16},{24,28},{28,24},{32,36},... | collective-permute-start | bytes 786440 | tf_op jit(solution)/shard_map/ppermute | solution.py:311
  23.4 0.7 copy-done.6
  24.1 5.2 %weight_blocks.1 = (bf16[12,128,768]{2,1,0:T(8,128)(2,1)}, bf16[12,128,768]{2,1,0:T(8,128)(2,1)}) custom-call(s32[5]{0:T(128)} %stack.38.where_ref, bf16[864,128]{1,0:T(8,128)(2,1)} %copy-done.2, bf16[864,128]{1,0:T(8,128)(2,1)} %copy-done.3, bf16[448,128]{1,0:T(8,128)(2,1)} %copy-done.5, bf16[1312,128]{1,0:T(8,128)(2,1)} %copy-done.6), custom_call_target="tpu_custom_call" | custom-call | tf_op jit(solution)/shard_map/weight_blocks/pallas_call | solution.py:322
  29.5 1.5 %collective-permute-done.7.other_far = bf16[18,64,128]{2,1,0:T(8,128)(2,1)S(1)} collective-permute-done((bf16[18,64,128]{2,1,0:T(8,128)(2,1)S(1)}, bf16[18,64,128]{2,1,0:T(8,128)(2,1)S(1)}, u32[]{:S(2)}, u32[]{:S(2)}) %collective-permute-start.7) | collective-permute-done | bytes 294944 | tf_op jit(solution)/shard_map/ppermute | solution.py:331
  31.1 0.7 copy-done.8
  31.8 16.8 %sections.1 = (bf16[2,4,64,128]{3,2,1,0:T(8,128)(2,1)}, bf16[2,4,64,128]{3,2,1,0:T(8,128)(2,1)}, bf16[1024,128]{1,0:T(8,128)(2,1)}) custom-call(s32[5]{0:T(128)} %stack.38.where_ref, bf16[16,64,128]{2,1,0:T(8,128)(2,1)} %copy-done, bf16[16,64,128]{2,1,0:T(8,128)(2,1)} %copy-done.4, bf16[18,64,128]{2,1,0:T(8,128)(2,1)} %copy-done.7, ...), custom_call_target="tpu_custom_call" | custom-call | tf_op jit(solution)/shard_map/sections/pallas_call | solution.py:237
  48.6 14.8 %all-to-all-start = ((bf16[64,16,128]{2,1,0:T(8,128)(2,1)}), bf16[64,16,128]{2,1,0:T(8,128)(2,1)S(1)}, u32[]{:S(2)}, u32[]{:S(2)}) async-start(bf16[64,16,128]{2,1,0:T(8,128)(2,1)} %bitcast.37), calls=%async_computation | async-start | bytes 524288 | tf_op jit(solution)/shard_map/all_to_all | solution.py:340
  63.4 4.9 %collective-permute-start.8 = (bf16[2,4,64,128]{3,2,1,0:T(8,128)(2,1)}, bf16[2,4,64,128]{3,2,1,0:T(8,128)(2,1)S(1)}, u32[]{:S(2)}, u32[]{:S(2)}) collective-permute-start(bf16[2,4,64,128]{3,2,1,0:T(8,128)(2,1)} %get-tuple-element.22), channel_id=1, source_target_pairs={{0,0},{4,64},{64,4},{68,68},{1,1},{5,65},{65,5},{69,69},{2,2},{6,6... | collective-permute-start | bytes 393224 | tf_op jit(solution)/shard_map/ppermute | solution.py:348
  68.5 5.6 %all-to-all-done = bf16[64,16,128]{2,1,0:T(8,128)(2,1)S(1)} async-done(((bf16[64,16,128]{2,1,0:T(8,128)(2,1)}), bf16[64,16,128]{2,1,0:T(8,128)(2,1)S(1)}, u32[]{:S(2)}, u32[]{:S(2)}) %all-to-all-start) | async-done | bytes 262176 | tf_op jit(solution)/shard_map/all_to_all | solution.py:340
  74.1 6.1 %collective-permute-start.10 = (bf16[16,128]{1,0:T(8,128)(2,1)S(1)}, bf16[16,128]{1,0:T(8,128)(2,1)S(1)}, u32[]{:S(2)}, u32[]{:S(2)}) collective-permute-start(bf16[16,128]{1,0:T(8,128)(2,1)S(1)} %reduce_sum.12), channel_id=1, source_target_pairs={{0,0},{4,64},{64,4},{68,68},{1,1},{5,65},{65,5},{69,69},{2,2},{6,6... | collective-permute-start | bytes 12296 | tf_op jit(solution)/shard_map/ppermute | solution.py:343
  80.3 1.3 %collective-permute-done.10 = bf16[16,128]{1,0:T(8,128)(2,1)S(1)} collective-permute-done((bf16[16,128]{1,0:T(8,128)(2,1)S(1)}, bf16[16,128]{1,0:T(8,128)(2,1)S(1)}, u32[]{:S(2)}, u32[]{:S(2)}) %collective-permute-start.10) | collective-permute-done | bytes 4128 | tf_op jit(solution)/shard_map/ppermute | solution.py:343
  81.5 0.7 broadcast_in_dim.2
  82.3 4.2 %all-to-all-start.1 = ((bf16[64,16,128]{2,1,0:T(8,128)(2,1)}), bf16[64,16,128]{2,1,0:T(8,128)(2,1)S(1)}, u32[]{:S(2)}, u32[]{:S(2)}) async-start(bf16[64,16,128]{2,1,0:T(8,128)(2,1)} %broadcast_in_dim.2), calls=%async_computation.1 | async-start | bytes 524288 | tf_op jit(solution)/shard_map/all_to_all | solution.py:344
  86.6 0.8 copy.10
  87.4 0.8 copy.9
  88.1 11.2 %all-to-all-done.1 = bf16[64,16,128]{2,1,0:T(8,128)(2,1)S(1)} async-done(((bf16[64,16,128]{2,1,0:T(8,128)(2,1)}), bf16[64,16,128]{2,1,0:T(8,128)(2,1)S(1)}, u32[]{:S(2)}, u32[]{:S(2)}) %all-to-all-start.1) | async-done | bytes 262176 | tf_op jit(solution)/shard_map/all_to_all | solution.py:344
  99.3 0.7 copy-done.1
  100.0 2.0 %unpack.1 = f32[1,3,3,3,64,64]{5,4,3,2,1,0:T(8,128)} custom-call(bf16[1024,128]{1,0:T(8,128)(2,1)} %bitcast.32), custom_call_target="tpu_custom_call" | custom-call | tf_op jit(solution)/shard_map/unpack/pallas_call | solution.py:356
  (38 shorter events, 0.6 us)
Async XLA Ops:
  1.9 6.3 %collective-permute-start.1 = (bf16[8,64,128]{2,1,0:T(8,128)(2,1)S(1)}, bf16[8,64,128]{2,1,0:T(8,128)(2,1)S(1)}, u32[]{:S(2)}, u32[]{:S(2)}) collective-permute-start(bf16[8,64,128]{2,1,0:T(8,128)(2,1)S(1)} %bitcast.35), channel_id=1, source_target_pairs={{0,4},{4,0},{8,12},{12,8},{16,20},{20,16},{24,28},{28,24},{32,36},... | collective-permute-start | bytes 393224 | tf_op jit(solution)/shard_map/ppermute | solution.py:307
  6.5 16.9 %copy-start.2 = (bf16[864,128]{1,0:T(8,128)(2,1)}, bf16[864,128]{1,0:T(8,128)(2,1)S(1)}, u32[]{:S(2)}) copy-start(bf16[864,128]{1,0:T(8,128)(2,1)S(1)} %pad_maximum_fusion.2.own) | copy-start | bytes 663556
  6.5 5.2 %collective-permute-start = (bf16[864,128]{1,0:T(8,128)(2,1)S(1)}, bf16[864,128]{1,0:T(8,128)(2,1)S(1)}, u32[]{:S(2)}, u32[]{:S(2)}) collective-permute-start(bf16[864,128]{1,0:T(8,128)(2,1)S(1)} %pad_maximum_fusion.2.own), channel_id=1, source_target_pairs={{0,64},{4,196},{64,128},{68,4},{128,192},{132,68},{192,0},{196,132... | collective-permute-start | bytes 663560 | tf_op jit(solution)/shard_map/ppermute | solution.py:279
  7.7 6.8 %collective-permute-start.5 = (bf16[448,128]{1,0:T(8,128)(2,1)S(1)}, bf16[448,128]{1,0:T(8,128)(2,1)S(1)}, u32[]{:S(2)}, u32[]{:S(2)}) collective-permute-start(bf16[448,128]{1,0:T(8,128)(2,1)S(1)} %bitcast.38), channel_id=1, source_target_pairs={{0,128},{64,192},{128,0},{192,64},{1,129},{65,193},{129,1},{193,65... | collective-permute-start | bytes 344072 | tf_op jit(solution)/shard_map/ppermute | solution.py:288
  8.3 22.8 %copy-start = (bf16[16,64,128]{2,1,0:T(8,128)(2,1)}, bf16[16,64,128]{2,1,0:T(8,128)(2,1)S(1)}, u32[]{:S(2)}) copy-start(bf16[16,64,128]{2,1,0:T(8,128)(2,1)S(1)} %pad_maximum_fusion.1.chip_rows) | copy-start | bytes 786436
  8.3 8.0 %collective-permute-start.2 = (bf16[16,64,128]{2,1,0:T(8,128)(2,1)S(1)}, bf16[16,64,128]{2,1,0:T(8,128)(2,1)S(1)}, u32[]{:S(2)}, u32[]{:S(2)}) collective-permute-start(bf16[16,64,128]{2,1,0:T(8,128)(2,1)S(1)} %pad_maximum_fusion.1.chip_rows), channel_id=1, source_target_pairs={{0,8},{8,16},{16,24},{24,32},{32,40},{40,48},{48,56},{12,4},{20,12... | collective-permute-start | bytes 786440 | tf_op jit(solution)/shard_map/ppermute | solution.py:304
  11.7 11.7 %copy-start.3 = (bf16[864,128]{1,0:T(8,128)(2,1)}, bf16[864,128]{1,0:T(8,128)(2,1)S(1)}, u32[]{:S(2)}) copy-start(bf16[864,128]{1,0:T(8,128)(2,1)S(1)} %collective-permute-done.near) | copy-start | bytes 663556
  14.5 8.8 %copy-start.5 = (bf16[448,128]{1,0:T(8,128)(2,1)}, bf16[448,128]{1,0:T(8,128)(2,1)S(1)}, u32[]{:S(2)}) copy-start(bf16[448,128]{1,0:T(8,128)(2,1)S(1)} %collective-permute-done.5.half) | copy-start | bytes 344068
  14.6 8.8 %collective-permute-start.6 = (bf16[1312,128]{1,0:T(8,128)(2,1)S(1)}, bf16[1312,128]{1,0:T(8,128)(2,1)S(1)}, u32[]{:S(2)}, u32[]{:S(2)}) collective-permute-start(bf16[1312,128]{1,0:T(8,128)(2,1)S(1)} %pad_maximum_fusion), channel_id=1, source_target_pairs={{0,4},{4,0},{8,12},{12,8},{16,20},{20,16},{24,28},{28,24},{32,36},... | collective-permute-start | bytes 1007624 | tf_op jit(solution)/shard_map/ppermute | solution.py:321
  16.3 14.7 %copy-start.4 = (bf16[16,64,128]{2,1,0:T(8,128)(2,1)}, bf16[16,64,128]{2,1,0:T(8,128)(2,1)S(1)}, u32[]{:S(2)}) copy-start(bf16[16,64,128]{2,1,0:T(8,128)(2,1)S(1)} %collective-permute-done.2.near_rows) | copy-start | bytes 786436
  16.4 12.9 %collective-permute-start.3 = (bf16[18,64,128]{2,1,0:T(8,128)(2,1)S(1)}, bf16[18,64,128]{2,1,0:T(8,128)(2,1)S(1)}, u32[]{:S(2)}, u32[]{:S(2)}) collective-permute-start(bf16[18,64,128]{2,1,0:T(8,128)(2,1)S(1)} %maximum_select_fusion), channel_id=1, source_target_pairs={{0,16},{8,24},{16,32},{24,40},{32,48},{40,56},{20,4},{28,12},{36,2... | collective-permute-start | bytes 884744 | tf_op jit(solution)/shard_map/ppermute | solution.py:304
  17.7 11.6 %collective-permute-start.4 = (bf16[16,64,128]{2,1,0:T(8,128)(2,1)S(1)}, bf16[16,64,128]{2,1,0:T(8,128)(2,1)S(1)}, u32[]{:S(2)}, u32[]{:S(2)}) collective-permute-start(bf16[16,64,128]{2,1,0:T(8,128)(2,1)S(1)} %collective-permute-done.2.near_rows), channel_id=1, source_target_pairs={{0,4},{4,0},{8,12},{12,8},{16,20},{20,16},{24,28},{28,24},{32,36},... | collective-permute-start | bytes 786440 | tf_op jit(solution)/shard_map/ppermute | solution.py:311
  23.4 0.7 copy-start.6
  29.3 1.7 %copy-start.9 = (bf16[16,64,128]{2,1,0:T(8,128)(2,1)}, bf16[16,64,128]{2,1,0:T(8,128)(2,1)S(1)}, u32[]{:S(2)}) copy-start(bf16[16,64,128]{2,1,0:T(8,128)(2,1)S(1)} %collective-permute-done.4.other_near) | copy-start | bytes 786436
  29.4 1.7 %copy-start.7 = (bf16[18,64,128]{2,1,0:T(8,128)(2,1)}, bf16[18,64,128]{2,1,0:T(8,128)(2,1)S(1)}, u32[]{:S(2)}) copy-start(bf16[18,64,128]{2,1,0:T(8,128)(2,1)S(1)} %collective-permute-done.3.far_rows) | copy-start | bytes 884740
  29.4 1.7 %collective-permute-start.7 = (bf16[18,64,128]{2,1,0:T(8,128)(2,1)S(1)}, bf16[18,64,128]{2,1,0:T(8,128)(2,1)S(1)}, u32[]{:S(2)}, u32[]{:S(2)}) collective-permute-start(bf16[18,64,128]{2,1,0:T(8,128)(2,1)S(1)} %collective-permute-done.3.far_rows), channel_id=1, source_target_pairs={{0,4},{4,0},{8,12},{12,8},{16,20},{20,16},{24,28},{28,24},{32,36},... | collective-permute-start | bytes 884744 | tf_op jit(solution)/shard_map/ppermute | solution.py:331
  31.1 0.7 copy-start.8
  48.6 25.4 %all-to-all-start = ((bf16[64,16,128]{2,1,0:T(8,128)(2,1)}), bf16[64,16,128]{2,1,0:T(8,128)(2,1)S(1)}, u32[]{:S(2)}, u32[]{:S(2)}) async-start(bf16[64,16,128]{2,1,0:T(8,128)(2,1)} %bitcast.37), calls=%async_computation | async-start | bytes 524288 | tf_op jit(solution)/shard_map/all_to_all | solution.py:340
  63.4 23.0 %collective-permute-start.8 = (bf16[2,4,64,128]{3,2,1,0:T(8,128)(2,1)}, bf16[2,4,64,128]{3,2,1,0:T(8,128)(2,1)S(1)}, u32[]{:S(2)}, u32[]{:S(2)}) collective-permute-start(bf16[2,4,64,128]{3,2,1,0:T(8,128)(2,1)} %get-tuple-element.22), channel_id=1, source_target_pairs={{0,0},{4,64},{64,4},{68,68},{1,1},{5,65},{65,5},{69,69},{2,2},{6,6... | collective-permute-start | bytes 393224 | tf_op jit(solution)/shard_map/ppermute | solution.py:348
  68.4 18.1 %collective-permute-start.9 = (bf16[2,4,64,128]{3,2,1,0:T(8,128)(2,1)}, bf16[2,4,64,128]{3,2,1,0:T(8,128)(2,1)S(1)}, u32[]{:S(2)}, u32[]{:S(2)}) collective-permute-start(bf16[2,4,64,128]{3,2,1,0:T(8,128)(2,1)} %get-tuple-element.23), channel_id=1, source_target_pairs={{0,4},{4,68},{64,0},{68,64},{1,5},{5,69},{65,1},{69,65},{2,6},{6,7... | collective-permute-start | bytes 393224 | tf_op jit(solution)/shard_map/ppermute | solution.py:349
  74.1 7.4 %collective-permute-start.10 = (bf16[16,128]{1,0:T(8,128)(2,1)S(1)}, bf16[16,128]{1,0:T(8,128)(2,1)S(1)}, u32[]{:S(2)}, u32[]{:S(2)}) collective-permute-start(bf16[16,128]{1,0:T(8,128)(2,1)S(1)} %reduce_sum.12), channel_id=1, source_target_pairs={{0,0},{4,64},{64,4},{68,68},{1,1},{5,65},{65,5},{69,69},{2,2},{6,6... | collective-permute-start | bytes 12296 | tf_op jit(solution)/shard_map/ppermute | solution.py:343
  82.3 17.0 %all-to-all-start.1 = ((bf16[64,16,128]{2,1,0:T(8,128)(2,1)}), bf16[64,16,128]{2,1,0:T(8,128)(2,1)S(1)}, u32[]{:S(2)}, u32[]{:S(2)}) async-start(bf16[64,16,128]{2,1,0:T(8,128)(2,1)} %broadcast_in_dim.2), calls=%async_computation.1 | async-start | bytes 524288 | tf_op jit(solution)/shard_map/all_to_all | solution.py:344
  99.3 0.7 copy-start.1
